TPU v7x, 512 devices: a whole 4x8x8 slice. The times are simulated.
512 devices in a mesh: pt: 16 (over z, x_lo), fft: 32 (over y, x_hi, core).
Axes of the slice: x: 4 (x_hi: 2, x_lo: 2; x = x_hi * 2 + x_lo), y: 8, z: 8, core: 2. Of those that a mesh axis runs over, the one named last changes fastest.
Arguments:
- sky_model: float32 [4096, 4096], P('fft'), may hold values from -6 to 6
- intersection: int32 [16, 1024], P('pt'), may hold values from 0 to 4095, as said below
- beam: float32 [2048, 16, 2048], P(None, 'pt', 'fft'), may hold values from 0.1 to 1
- vis_data: float32 [2, 16, 2048, 128], P(None, 'pt', 'fft'), may hold values from -12 to 12
- vis_weight: float32 [16, 2048, 128], P('pt', 'fft'), may hold values from 0.1 to 1
- vis_pos: float32 [2, 16, 2048, 128], P(None, 'pt', 'fft'), may hold values from 4 to 11
- uv_block: int32 [16, 2048], P('pt', 'fft'), may hold values from 0 to 16383, as said below
- counts: int32 [16, 32], P('pt', 'fft'), may hold values from 1 to 64
Outputs:
- gradient: float32 [4096, 4096], P('fft', 'pt')
Inputs may be any that keep to these rules, and one draw needn't show every extreme that they name: Sky tile (a, b), tile row a < 64 and tile column b < 64, is row (a mod 32) * 128 + (a // 32) * 64 + b of sky_model. Pointing p covers the window of 32 x 2048 / 64 tiles at an offset (oy, ox) inside the sky: intersection[p, i * 32 + j] is tile (oy + i, ox + j). `uv_block`: entries m of fft index f (f * 64 <= m < (f + 1) * 64) name blocks n whose kx range lies in the f-th of 32 equal column slabs of the uv grid, that is f * 4 * (128) <= n < (f + 1) * 4 * 128, in ascending order within each fft index.
All inputs are finite; a program needn't handle non-finite values.
Results may differ from a plain program's by a relative error of at most 0.0003.
Values sent between devices are 32-bit elements; how exact they have to be, the bound alone decides.
No kernel may reach another device: no remote copies, remote signals or barrier semaphores. Data moves between devices by JAX's collectives and lax.ppermute only.
A program may use at most 64 MiB of HBM per device.

v0:
```python
import math

import jax
import jax.numpy as jnp
from jax import lax
from jax.sharding import PartitionSpec as P

G = 2048
TS = 64
UB = 16


kernel_spread = 8.0


def split_length(length):
    factor_a = 1
    for candidate in range(1, math.isqrt(length) + 1):
        if length % candidate == 0:
            factor_a = candidate
    return (factor_a, length // factor_a)


def phase_table(count_k, count_n, total, direction):
    k_ids = jnp.arange(count_k, dtype=jnp.int32)[:, None]
    n_ids = jnp.arange(count_n, dtype=jnp.int32)[None, :]
    angle = (k_ids * n_ids % total).astype(jnp.float32) * (2.0 * math.pi / total)
    return (jnp.cos(angle), direction * jnp.sin(angle))


def apply_table(pattern, table_re, table_im, stacked, columns, is_complex, want_imag):
    first = jnp.einsum(pattern, table_re, stacked, precision=lax.Precision.HIGHEST)
    second = jnp.einsum(pattern, table_im, stacked, precision=lax.Precision.HIGHEST)
    if not is_complex:
        return (first, second)
    real_out = first[..., :columns] - second[..., columns:]
    if not want_imag:
        return (real_out, None)
    return (real_out, second[..., :columns] + first[..., columns:])


def transform(data_re, data_im, direction, want_imag=True):
    length, columns = data_re.shape
    factor_a, factor_b = split_length(length)
    outer_re, outer_im = phase_table(factor_a, factor_a, factor_a, direction)
    twist_re, twist_im = phase_table(factor_a, factor_b, length, direction)
    inner_re, inner_im = phase_table(factor_b, factor_b, factor_b, direction)
    if data_im is None:
        stacked = data_re.reshape(factor_a, factor_b, columns)
        step_re, step_im = apply_table(
            "ka,abm->kbm", outer_re, outer_im, stacked, columns, False, True
        )
    else:
        stacked = jnp.concatenate([data_re, data_im], axis=1).reshape(
            factor_a, factor_b, 2 * columns
        )
        step_re, step_im = apply_table(
            "ka,abm->kbm", outer_re, outer_im, stacked, columns, True, True
        )
    turned_re = step_re * twist_re[:, :, None] - step_im * twist_im[:, :, None]
    turned_im = step_re * twist_im[:, :, None] + step_im * twist_re[:, :, None]
    turned = jnp.concatenate([turned_re, turned_im], axis=2)
    out_re, out_im = apply_table(
        "jb,kbm->jkm", inner_re, inner_im, turned, columns, True, want_imag
    )
    if not want_imag:
        return (out_re.reshape(length, columns), None)
    return (out_re.reshape(length, columns), out_im.reshape(length, columns))


def slab_view(tile_lists, groups, tile_span):
    q_count = tile_lists.shape[0]
    per_group = tile_span // groups
    shaped = tile_lists.reshape(q_count, tile_span, groups, per_group)
    return shaped.transpose(0, 2, 1, 3).reshape(q_count, groups, tile_span * per_group)


def rank_slots(owner_of, groups):
    one_hot = (owner_of[..., None] == jnp.arange(groups, dtype=jnp.int32)).astype(jnp.int32)
    earlier = jnp.cumsum(one_hot, axis=-2) - one_hot
    return jnp.sum(earlier * one_hot, axis=-1)


def sender_index(slab_rows, owner_of, slot_rank, my_index, tile_dev, capacity):
    q_count, groups, per_slab = slab_rows.shape
    pick_q = jnp.arange(q_count, dtype=jnp.int32)[:, None, None]
    pick_d = jnp.arange(groups, dtype=jnp.int32)[None, :, None]
    slot_at = jnp.where(owner_of == my_index, slot_rank, capacity)
    local_rows = slab_rows - my_index * tile_dev
    blank = jnp.zeros((groups, q_count, capacity), jnp.int32)
    return blank.at[pick_d, pick_q, slot_at].set(local_rows, mode="drop")


def body(sky_model, intersection, beam, vis_data, vis_weight, vis_pos, uv_block, counts):
    groups = lax.axis_size("fft")
    my_index = lax.axis_index("fft")
    tile_dev, tile_cells = sky_model.shape
    q_count = intersection.shape[0]
    grid_side = G
    slab_cols = grid_side // groups
    tile_span = grid_side // TS
    per_group = slab_cols // TS
    per_slab = tile_span * per_group
    capacity = per_slab // groups
    slab_rows = slab_view(intersection, groups, tile_span)
    owner_of = slab_rows // tile_dev
    slot_rank = rank_slots(owner_of, groups)
    send_rows = sender_index(slab_rows, owner_of, slot_rank, my_index, tile_dev, capacity)
    outgoing = sky_model[send_rows]
    incoming = lax.all_to_all(outgoing, "fft", split_axis=0, concat_axis=0, tiled=True)
    own_owner = lax.dynamic_index_in_dim(owner_of, my_index, 1, keepdims=False)
    own_rank = lax.dynamic_index_in_dim(slot_rank, my_index, 1, keepdims=False)
    pick_q = jnp.arange(q_count, dtype=jnp.int32)[:, None]
    flat_slot = (own_owner * q_count + pick_q) * capacity + own_rank
    placed = incoming.reshape(groups * q_count * capacity, tile_cells)[flat_slot]
    cut_image = (
        placed.reshape(q_count, tile_span, per_group, TS, TS)
        .transpose(1, 3, 0, 2, 4)
        .reshape(grid_side, q_count, slab_cols)
    )
    dirty_image = beam * cut_image
    spec_re, spec_im = transform(dirty_image.reshape(grid_side, q_count * slab_cols), None, -1.0)
    spec_re = spec_re.reshape(grid_side, q_count, slab_cols)
    spec_im = spec_im.reshape(grid_side, q_count, slab_cols)
    part_re = lax.all_to_all(spec_re, "fft", split_axis=0, concat_axis=2, tiled=True)
    part_im = lax.all_to_all(spec_im, "fft", split_axis=0, concat_axis=2, tiled=True)
    cols_n, items, rows_n = part_re.shape
    moved_re = part_re.transpose(2, 1, 0).reshape(rows_n, items * cols_n)
    moved_im = part_im.transpose(2, 1, 0).reshape(rows_n, items * cols_n)
    out_re, out_im = transform(moved_re, moved_im, -1.0)
    uv_re = out_re.reshape(rows_n, items, cols_n)
    uv_im = out_im.reshape(rows_n, items, cols_n)
    block_rows = grid_side // UB
    block_cols = slab_cols // UB
    per_device = block_rows * block_cols

    def to_blocks(grid):
        return (
            grid.reshape(block_rows, UB, q_count, block_cols, UB)
            .transpose(2, 3, 0, 1, 4)
            .reshape(q_count * per_device, UB * UB)
        )

    def from_blocks(blocks):
        return (
            blocks.reshape(q_count, block_cols, block_rows, UB, UB)
            .transpose(2, 3, 0, 1, 4)
            .reshape(grid_side, q_count * slab_cols)
        )

    block_count = uv_block.shape[1]
    block_pick = pick_q * per_device + (uv_block - my_index * per_device)
    chosen_re = to_blocks(uv_re)[block_pick].reshape(q_count, block_count, UB, UB)
    chosen_im = to_blocks(uv_im)[block_pick].reshape(q_count, block_count, UB, UB)
    offsets = jnp.arange(UB, dtype=jnp.float32)[None, None, :, None]
    weight_y = jnp.exp(-((offsets - vis_pos[0][:, :, None, :]) ** 2) / kernel_spread)
    weight_x = jnp.exp(-((offsets - vis_pos[1][:, :, None, :]) ** 2) / kernel_spread)
    pred_re = (
        jnp.sum(
            jnp.einsum("qbyx,qbyv->qbxv", chosen_re, weight_y, precision=lax.Precision.HIGHEST)
            * weight_x,
            axis=2,
        )
        / grid_side
    )
    pred_im = (
        jnp.sum(
            jnp.einsum("qbyx,qbyv->qbxv", chosen_im, weight_y, precision=lax.Precision.HIGHEST)
            * weight_x,
            axis=2,
        )
        / grid_side
    )
    live_mask = (jnp.arange(block_count, dtype=jnp.int32)[None, :] < counts).astype(jnp.float32)
    vis_scale = live_mask[:, :, None] * vis_weight
    resid_re = vis_scale * (vis_data[0] - pred_re)
    resid_im = vis_scale * (vis_data[1] - pred_im)
    cells_re = jnp.einsum(
        "qbyv,qbxv->qbyx",
        weight_y,
        resid_re[:, :, None, :] * weight_x,
        precision=lax.Precision.HIGHEST,
    )
    cells_im = jnp.einsum(
        "qbyv,qbxv->qbyx",
        weight_y,
        resid_im[:, :, None, :] * weight_x,
        precision=lax.Precision.HIGHEST,
    )
    flat_pick = block_pick.reshape(-1)
    empty_grid = jnp.zeros((q_count * per_device, UB * UB), jnp.float32)
    grid_re = empty_grid.at[flat_pick].add(cells_re.reshape(q_count * block_count, UB * UB))
    grid_im = empty_grid.at[flat_pick].add(cells_im.reshape(q_count * block_count, UB * UB))
    back_re, back_im = transform(from_blocks(grid_re), from_blocks(grid_im), 1.0)
    back_re = back_re.reshape(grid_side, q_count, slab_cols)
    back_im = back_im.reshape(grid_side, q_count, slab_cols)
    part_re = lax.all_to_all(back_re, "fft", split_axis=0, concat_axis=2, tiled=True)
    part_im = lax.all_to_all(back_im, "fft", split_axis=0, concat_axis=2, tiled=True)
    rows_n, items, cols_n = part_re.shape
    moved_re = part_re.transpose(2, 1, 0).reshape(cols_n, items * rows_n)
    moved_im = part_im.transpose(2, 1, 0).reshape(cols_n, items * rows_n)
    out_re, unused = transform(moved_re, moved_im, 1.0, False)
    residual_image = out_re.reshape(cols_n, items, rows_n) / grid_side
    weighted = beam * residual_image
    tiles_back = (
        weighted.reshape(tile_span, TS, q_count, per_group, TS)
        .transpose(2, 0, 3, 1, 4)
        .reshape(q_count, per_slab, tile_cells)
    )
    home_slots = jnp.zeros((groups, q_count, capacity, tile_cells), jnp.float32)
    home_slots = home_slots.at[own_owner, pick_q, own_rank].set(tiles_back)
    arrived = lax.all_to_all(home_slots, "fft", split_axis=0, concat_axis=0, tiled=True)
    summed = (
        jnp.zeros((tile_dev, tile_cells), jnp.float32)
        .at[send_rows.reshape(-1)]
        .add(arrived.reshape(-1, tile_cells))
    )
    gradient = lax.psum_scatter(summed, "pt", scatter_dimension=1, tiled=True)
    return gradient


def solution(mesh):
    in_specs = (
        P("fft", None),
        P("pt", None),
        P(None, "pt", "fft"),
        P(None, "pt", "fft", None),
        P("pt", "fft", None),
        P(None, "pt", "fft", None),
        P("pt", "fft"),
        P("pt", "fft"),
    )
    out_specs = P("fft", "pt")
    return jax.shard_map(body, mesh=mesh, in_specs=in_specs, out_specs=out_specs, check_vma=False)
```

profile of v0, /device:TPU:16, one launch (start us, length us, event | category | flops | bytes accessed | tf_op | source)
XLA Modules:
  0.0 388.9 jit_solution(994576834928815332)
XLA Ops:
  11.5 4.3 %scatter_custom_fusion.4 = s32[32]{0:T(128)S(1)} fusion(s32[1024]{0:T(1024)S(1)} %reshape.651, s32[1024]{0:T(1024)S(1)} %reshape.653, s32[]{:T(128)} %constant.126.clone.1), kind=kCustom, calls=%fused_computation.238 | custom fusion | bytes 132
  17.9 10.5 %all-to-all-start = ((f32[32,1,1,4096]{3,2,1,0:T(1,128)}), f32[32,1,1,4096]{3,2,1,0:T(1,128)S(1)}, u32[]{:S(2)}, u32[]{:S(2)}) async-start(f32[32,1,1,4096]{3,2,1,0:T(1,128)} %copy.269), calls=%async_computation | async-start | bytes 1048576 | tf_op jit(solution)/shard_map/all_to_all | solution.py:110
  29.3 16.3 %all-to-all-done = f32[32,1,1,4096]{3,2,1,0:T(1,128)S(1)} async-done(((f32[32,1,1,4096]{3,2,1,0:T(1,128)}), f32[32,1,1,4096]{3,2,1,0:T(1,128)S(1)}, u32[]{:S(2)}, u32[]{:S(2)}) %all-to-all-start) | async-done | bytes 524320 | tf_op jit(solution)/shard_map/all_to_all | solution.py:110
  47.1 1.6 fusion.22
  48.7 1.9 multiply_subtract_fusion.3
  51.1 1.7 fusion.16
  52.7 1.6 fusion.18
  54.4 1.6 slice_subtract_fusion.5
  57.1 9.9 %reduce.21 = f32[2048,64]{1,0:T(8,128)S(1)} reduce(f32[2048,1,64]{2,1,0:T(1,128)S(1)} %bitcast.234, f32[]{:T(128)} %broadcast.714), dimensions={1}, to_apply=%bitcast.24.reduce_sub_computation | reduce | bytes 1048580 | tf_op jit(solution)/shard_map/reshape;reshape | solution.py:123
  67.0 1.5 reshape.696
  68.5 5.5 %all-to-all-start.1 = ((f32[32,1,4096]{2,1,0:T(1,128)}), f32[32,1,4096]{2,1,0:T(1,128)}, u32[]{:S(2)}, u32[]{:S(2)}) async-start(f32[32,1,4096]{2,1,0:T(1,128)} %reshape.696), calls=%async_computation.1 | async-start | bytes 1048576 | tf_op jit(solution)/shard_map/all_to_all | solution.py:125
  73.9 1.8 copy.278
  75.8 9.4 %reduce.19 = f32[2048,64]{1,0:T(8,128)S(1)} reduce(f32[2048,1,64]{2,1,0:T(1,128)S(1)} %bitcast.235, f32[]{:T(128)} %broadcast.714), dimensions={1}, to_apply=%bitcast.29.reduce_sub_computation | reduce | bytes 1048580 | tf_op jit(solution)/shard_map/reshape;reshape | solution.py:124
  85.2 1.5 reshape.694
  86.6 4.6 %all-to-all-done.1 = f32[32,1,4096]{2,1,0:T(1,128)} async-done(((f32[32,1,4096]{2,1,0:T(1,128)}), f32[32,1,4096]{2,1,0:T(1,128)}, u32[]{:S(2)}, u32[]{:S(2)}) %all-to-all-start.1) | async-done | bytes 524320 | tf_op jit(solution)/shard_map/all_to_all | solution.py:125
  91.3 5.6 %all-to-all-start.2 = ((f32[32,1,4096]{2,1,0:T(1,128)}), f32[32,1,4096]{2,1,0:T(1,128)}, u32[]{:S(2)}, u32[]{:S(2)}) async-start(f32[32,1,4096]{2,1,0:T(1,128)} %reshape.694), calls=%async_computation.2 | async-start | bytes 1048576 | tf_op jit(solution)/shard_map/all_to_all | solution.py:126
  97.8 2.9 reduce.22
  106.4 7.7 %all-to-all-done.2 = f32[32,1,4096]{2,1,0:T(1,128)} async-done(((f32[32,1,4096]{2,1,0:T(1,128)}), f32[32,1,4096]{2,1,0:T(1,128)}, u32[]{:S(2)}, u32[]{:S(2)}) %all-to-all-start.2) | async-done | bytes 524320 | tf_op jit(solution)/shard_map/all_to_all | solution.py:126
  114.1 3.7 reduce.20
  117.8 2.4 reshape.695
  120.2 1.6 copy.360
  121.8 2.4 all_to_all.66
  125.7 2.0 copy.282
  127.7 2.5 fusion.37
  130.2 2.6 fusion.36
  134.5 1.7 fusion.12
  136.2 1.6 fusion.14
  137.8 1.6 slice_subtract_fusion.3
  140.0 3.2 reshape_reshape_reshape.7
  143.2 3.7 copy.295
  149.6 3.2 reshape_reshape_reshape.6
  152.7 4.1 %copy.286 = f32[1,4,128,16,16]{2,1,4,3,0:T(4,128)S(1)} copy(f32[1,4,128,16,16]{4,1,3,2,0:T(4,128)} %bitcast.231) | data formatting | bytes 1048576 | tf_op jit(solution)/shard_map/transpose | solution.py:140
  162.8 2.6 copy.293
  165.5 3.3 concatenate.49
  172.7 2.8 copy.302
  175.5 3.3 concatenate.50
  178.8 2.0 copy.304
  180.8 2.5 fusion.35
  183.3 2.4 fusion.34
  187.4 1.6 fusion.10
  189.0 1.6 fusion.8
  190.7 1.6 slice_subtract_fusion.1
  192.9 9.6 %reduce.25 = f32[2048,64]{1,0:T(8,128)S(1)} reduce(f32[2048,1,64]{2,1,0:T(1,128)S(1)} %bitcast.236, f32[]{:T(128)} %broadcast.714), dimensions={1}, to_apply=%bitcast.51.reduce_sub_computation | reduce | bytes 1048580 | tf_op jit(solution)/shard_map/reshape;reshape | solution.py:195
  202.4 1.5 reshape.700
  203.9 5.5 %all-to-all-start.3 = ((f32[32,1,4096]{2,1,0:T(1,128)}), f32[32,1,4096]{2,1,0:T(1,128)}, u32[]{:S(2)}, u32[]{:S(2)}) async-start(f32[32,1,4096]{2,1,0:T(1,128)} %reshape.700), calls=%async_computation.3 | async-start | bytes 1048576 | tf_op jit(solution)/shard_map/all_to_all | solution.py:197
  209.4 1.8 copy.310
  211.2 9.3 %reduce.23 = f32[2048,64]{1,0:T(8,128)S(1)} reduce(f32[2048,1,64]{2,1,0:T(1,128)S(1)} %bitcast.237, f32[]{:T(128)} %broadcast.714), dimensions={1}, to_apply=%bitcast.56.reduce_sub_computation | reduce | bytes 1048580 | tf_op jit(solution)/shard_map/reshape;reshape | solution.py:196
  222.0 4.7 %all-to-all-done.3 = f32[32,1,4096]{2,1,0:T(1,128)} async-done(((f32[32,1,4096]{2,1,0:T(1,128)}), f32[32,1,4096]{2,1,0:T(1,128)}, u32[]{:S(2)}, u32[]{:S(2)}) %all-to-all-start.3) | async-done | bytes 524320 | tf_op jit(solution)/shard_map/all_to_all | solution.py:197
  226.7 5.9 %all-to-all-start.4 = ((f32[32,1,4096]{2,1,0:T(1,128)}), f32[32,1,4096]{2,1,0:T(1,128)}, u32[]{:S(2)}, u32[]{:S(2)}) async-start(f32[32,1,4096]{2,1,0:T(1,128)} %reshape.698), calls=%async_computation.4 | async-start | bytes 1048576 | tf_op jit(solution)/shard_map/all_to_all | solution.py:198
  232.6 2.9 reduce.26
  241.2 8.3 %all-to-all-done.4 = f32[32,1,4096]{2,1,0:T(1,128)} async-done(((f32[32,1,4096]{2,1,0:T(1,128)}), f32[32,1,4096]{2,1,0:T(1,128)}, u32[]{:S(2)}, u32[]{:S(2)}) %all-to-all-start.4) | async-done | bytes 524320 | tf_op jit(solution)/shard_map/all_to_all | solution.py:198
  249.5 3.7 reduce.24
  253.3 2.4 reshape.699
  255.6 1.6 copy.358
  257.3 2.4 all_to_all.74
  261.1 2.0 copy.314
  263.2 2.5 fusion.33
  265.7 2.6 fusion.32
  270.3 1.7 fusion.4
  272.0 1.7 fusion
  277.1 5.4 %all-to-all-start.5 = ((f32[32,1,1,4096]{3,2,1,0:T(1,128)}), f32[32,1,1,4096]{3,2,1,0:T(1,128)S(1)}, u32[]{:S(2)}, u32[]{:S(2)}) async-start(f32[32,1,1,4096]{3,2,1,0:T(1,128)} %reshape.632), calls=%async_computation.5 | async-start | bytes 1048576 | tf_op jit(solution)/shard_map/all_to_all | solution.py:212
  282.6 17.2 %all-to-all-done.5 = f32[32,1,1,4096]{3,2,1,0:T(1,128)S(1)} async-done(((f32[32,1,1,4096]{3,2,1,0:T(1,128)}), f32[32,1,1,4096]{3,2,1,0:T(1,128)S(1)}, u32[]{:S(2)}, u32[]{:S(2)}) %all-to-all-start.5) | async-done | bytes 524320 | tf_op jit(solution)/shard_map/all_to_all | solution.py:212
  299.8 3.0 scatter_custom_fusion.3
  302.8 79.0 %reduce-scatter.2.cloned.1.call-done = f32[128,256]{1,0:T(8,128)} async-done(((f32[128,4096]{1,0:T(8,128)}), f32[128,256]{1,0:T(8,128)}) %reduce-scatter.2.cloned.1.call-update) | async-done | bytes 131088 | tf_op jit(solution)/shard_map/reduce_scatter | solution.py:218
  (130 shorter events, 49.1 us)
Async XLA Ops:
  6.5 9.3 %copy-start = (f32[128,4096]{1,0:T(8,128)S(1)}, f32[128,4096]{1,0:T(8,128)}, u32[]{:S(2)}) copy-start(f32[128,4096]{1,0:T(8,128)} %param.8) | copy-start | bytes 6291460
  16.6 11.8 %copy-start.9 = (f32[2048,1,64]{0,2,1:T(8,128)S(1)}, f32[2048,1,64]{0,2,1:T(8,128)}, u32[]{:S(2)}) copy-start(f32[2048,1,64]{0,2,1:T(8,128)} %param.10) | copy-start | bytes 1572868
  17.9 27.6 %all-to-all-start = ((f32[32,1,1,4096]{3,2,1,0:T(1,128)}), f32[32,1,1,4096]{3,2,1,0:T(1,128)S(1)}, u32[]{:S(2)}, u32[]{:S(2)}) async-start(f32[32,1,1,4096]{3,2,1,0:T(1,128)} %copy.269), calls=%async_computation | async-start | bytes 1048576 | tf_op jit(solution)/shard_map/all_to_all | solution.py:110
  68.5 22.8 %all-to-all-start.1 = ((f32[32,1,4096]{2,1,0:T(1,128)}), f32[32,1,4096]{2,1,0:T(1,128)}, u32[]{:S(2)}, u32[]{:S(2)}) async-start(f32[32,1,4096]{2,1,0:T(1,128)} %reshape.696), calls=%async_computation.1 | async-start | bytes 1048576 | tf_op jit(solution)/shard_map/all_to_all | solution.py:125
  75.8 21.8 %copy-start.14 = (s32[1,64]{1,0:T(1,128)S(1)}, s32[1,64]{1,0:T(1,128)}, u32[]{:S(2)}) copy-start(s32[1,64]{1,0:T(1,128)} %param.14) | copy-start | bytes 772
  75.8 22.0 %copy-start.12 = (f32[2,1,64,128]{3,2,1,0:T(8,128)S(1)}, f32[2,1,64,128]{3,2,1,0:T(8,128)}, u32[]{:S(2)}) copy-start(f32[2,1,64,128]{3,2,1,0:T(8,128)} %param.13) | copy-start | bytes 196612
  91.3 22.8 %all-to-all-start.2 = ((f32[32,1,4096]{2,1,0:T(1,128)}), f32[32,1,4096]{2,1,0:T(1,128)}, u32[]{:S(2)}, u32[]{:S(2)}) async-start(f32[32,1,4096]{2,1,0:T(1,128)} %reshape.694), calls=%async_computation.2 | async-start | bytes 1048576 | tf_op jit(solution)/shard_map/all_to_all | solution.py:126
  106.4 21.4 %copy-start.4 = (f32[32,64,64]{2,0,1:T(8,128)}, f32[32,64,64]{2,0,1:T(8,128)S(1)}, u32[]{:S(2)}) copy-start(f32[32,64,64]{2,0,1:T(8,128)S(1)} %copy.281) | copy-start | bytes 1572868
  127.7 2.5 copy-start.5
  146.9 2.1 copy-start.8
  156.8 1.3 copy-start.10
  157.8 2.1 copy-start.11
  157.8 2.1 copy-start.13
  169.8 11.0 %copy-start.2 = (f32[32,64,64]{2,0,1:T(8,128)}, f32[32,64,64]{2,0,1:T(8,128)S(1)}, u32[]{:S(2)}) copy-start(f32[32,64,64]{2,0,1:T(8,128)S(1)} %copy.303) | copy-start | bytes 1572868
  180.8 2.5 copy-start.6
  203.9 22.8 %all-to-all-start.3 = ((f32[32,1,4096]{2,1,0:T(1,128)}), f32[32,1,4096]{2,1,0:T(1,128)}, u32[]{:S(2)}, u32[]{:S(2)}) async-start(f32[32,1,4096]{2,1,0:T(1,128)} %reshape.700), calls=%async_computation.3 | async-start | bytes 1048576 | tf_op jit(solution)/shard_map/all_to_all | solution.py:197
  226.7 22.8 %all-to-all-start.4 = ((f32[32,1,4096]{2,1,0:T(1,128)}), f32[32,1,4096]{2,1,0:T(1,128)}, u32[]{:S(2)}, u32[]{:S(2)}) async-start(f32[32,1,4096]{2,1,0:T(1,128)} %reshape.698), calls=%async_computation.4 | async-start | bytes 1048576 | tf_op jit(solution)/shard_map/all_to_all | solution.py:198
  241.2 22.0 %copy-start.3 = (f32[32,64,64]{2,0,1:T(8,128)}, f32[32,64,64]{2,0,1:T(8,128)S(1)}, u32[]{:S(2)}) copy-start(f32[32,64,64]{2,0,1:T(8,128)S(1)} %copy.313) | copy-start | bytes 1572868
  263.2 2.5 copy-start.7
  277.1 22.7 %all-to-all-start.5 = ((f32[32,1,1,4096]{3,2,1,0:T(1,128)}), f32[32,1,1,4096]{3,2,1,0:T(1,128)S(1)}, u32[]{:S(2)}, u32[]{:S(2)}) async-start(f32[32,1,1,4096]{3,2,1,0:T(1,128)} %reshape.632), calls=%async_computation.5 | async-start | bytes 1048576 | tf_op jit(solution)/shard_map/all_to_all | solution.py:212
  282.5 99.3 %reduce-scatter.2.cloned.1.call-start = ((), (), s32[]{:S(2)}) async-start(), calls=%async_computation.7 | async-start | bytes 2228224 | tf_op jit(solution)/shard_map/reduce_scatter | solution.py:218
  282.6 99.3 %copy-start.1 = (f32[128,4096]{1,0:T(8,128)S(1)}, f32[128,4096]{1,0:T(8,128)}, u32[]{:S(2)}) copy-start(f32[128,4096]{1,0:T(8,128)} %param.8) | copy-start | bytes 6291460
Sparse Core Ops, SparseCore 0:
  303.0 78.8 reduce-scatter.1
where the time goes:
time: 394 us; the launch traced here: 389 us
  waiting for transfers between devices  138 us (35%)
  local copies, waits for them, and re-layouts  90.4 us (23%)
  other arithmetic  71.4 us (18%)
  starting transfers between devices  38.3 us (10%)
  matrix products  35.8 us (9%)
  between operations  15.2 us (4%)
    reduce_scatter x1, waiting for transfers between devices, body(): gradient = lax.psum_scatter(summed, 'pt', scatter_dimension=1, tiled=True)  79 us
    concatenate x12, local copies, waits for them, and re-layouts, transform(): jnp.concatenate([data_re, data_im], axis=1)  21.7 us
    unnamed x46, local copies, waits for them, and re-layouts  19 us
    all_to_all x1, waiting for transfers between devices, body(): lax.all_to_all(home_slots, 'fft', split_axis=0, concat_axis=0, tiled=True)  17.2 us
    all_to_all x1, waiting for transfers between devices, body(): lax.all_to_all(outgoing, 'fft', split_axis=0, concat_axis=0, tiled=True)  16.3 us
    dot_general x8, matrix products, apply_table(): jnp.einsum(pattern, table_im, stacked, precision=lax.Precision.HIGHEST)  16.2 us
    dot_general x8, matrix products, apply_table(): jnp.einsum(pattern, table_re, stacked, precision=lax.Precision.HIGHEST)  15.7 us
    all_to_all x1, starting transfers between devices, body(): lax.all_to_all(outgoing, 'fft', split_axis=0, concat_axis=0, tiled=True)  10.5 us
  transfers between devices with their start and end apart: 7, of which 7 were waited for; matrix products, arithmetic and copies ran while one was open for 11% of the time, Pallas kernels for 0%

commit v1 on v0

v1 whole, which is shorter than its diff:
```python
import math

import jax
import jax.numpy as jnp
import numpy as np
from jax import lax
from jax.experimental import pallas as pl
from jax.experimental.pallas import tpu as pltpu
from jax.sharding import PartitionSpec as P

G = 2048
TS = 64
UB = 16
VB = 128
NB = 64
SLABS = 32
HALF = 16
ROWS = 40
KEYS = 34
LANES = 128
VMEM_BYTES = 24 * 1024 * 1024
INTERPRET = False

F32 = jnp.float32
BF16 = jnp.bfloat16


def split_np(table):
    high = np.asarray(table, np.float32).astype(jnp.bfloat16)
    low = (np.asarray(table, np.float64) - high.astype(np.float64)).astype(jnp.bfloat16)
    return high, low


def split(value):
    high = value.astype(BF16)
    return high, (value - high.astype(F32)).astype(BF16)


def dot(left, right):
    return jnp.dot(left, right, preferred_element_type=F32)


def row_tables():
    rho, x1 = np.arange(64)[:, None], np.arange(64)[None, :]
    angle = 2 * np.pi * (rho * x1 % 64) / 64
    forward = np.concatenate([np.cos(angle), -np.sin(angle)], 0)
    high, low = split_np(forward)
    forward_cat = np.concatenate([high, high, low], 1)
    back = np.concatenate([np.cos(angle).T, -np.sin(angle).T], 1) / G
    high, low = split_np(back)
    back_cat = np.concatenate([high, high, low], 1)
    x0 = 2 * np.arange(16)[:, None, None] + (np.arange(LANES) >= 64)[None, None, :]
    twist = 2 * np.pi * (x0 * np.arange(64)[None, :, None]) / G
    return forward_cat, back_cat, np.cos(twist).astype(np.float32), np.sin(twist).astype(np.float32)


def column_tables():
    cols, keys = np.arange(64)[:, None], np.arange(64)[None, :]
    angle = 2 * np.pi * (cols * keys % 64) / 64
    first = np.concatenate([np.cos(angle), np.sin(angle)], 0)
    second = np.concatenate([-np.sin(angle), np.cos(angle)], 0)
    tables = []
    for table in (first, second, first.T, second.T):
        tables.extend(split_np(table))
    k1 = np.arange(ROWS)[:, None]
    lane = np.arange(LANES)[None, :]
    twist = 2 * np.pi * (k1 * (lane % 64)) / G
    cos = np.cos(twist).astype(np.float32)
    sin = (np.sin(twist) * np.where(lane < 64, 1.0, -1.0)).astype(np.float32)
    return tables, cos, sin


def turn(re, im, angle):
    c, s = math.cos(angle), math.sin(angle)
    if abs(s) < 1e-12:
        return (re, im) if c > 0 else (-re, -im)
    if abs(c) < 1e-12:
        return (-im, re) if s > 0 else (im, -re)
    return re * c - im * s, re * s + im * c


def fourier(values, sign):
    count = len(values)
    if count == 1:
        return values
    even, odd = fourier(values[::2], sign), fourier(values[1::2], sign)
    out = [None] * count
    for k in range(count // 2):
        re, im = turn(*odd[k], sign * 2 * math.pi * k / count)
        out[k] = (even[k][0] + re, even[k][1] + im)
        out[k + count // 2] = (even[k][0] - re, even[k][1] - im)
    return out


def fourier_packed(values, sign, flip):
    count = len(values)
    if count == 1:
        return values
    even, odd = fourier_packed(values[::2], sign, flip), fourier_packed(values[1::2], sign, flip)
    out = [None] * count
    for k in range(count // 2):
        angle = sign * 2 * math.pi * k / count
        c, s = math.cos(angle), math.sin(angle)
        value = odd[k]
        if k:
            crossed = pltpu.roll(value, 64, axis=1) * (flip * s)
            value = crossed if abs(c) < 1e-12 else value * c + crossed
        out[k] = even[k] + value
        out[k + count // 2] = even[k] - value
    return out


def call(kernel, out_shape, scratch, spaces, flops, data):
    return pl.pallas_call(
        kernel,
        out_shape=out_shape,
        in_specs=[pl.BlockSpec(memory_space=space) for space in spaces],
        out_specs=jax.tree.map(lambda _: pl.BlockSpec(memory_space=pltpu.VMEM), out_shape),
        scratch_shapes=scratch,
        compiler_params=pltpu.CompilerParams(vmem_limit_bytes=VMEM_BYTES),
        cost_estimate=pl.CostEstimate(flops=flops, bytes_accessed=data, transcendentals=0),
        interpret=INTERPRET,
    )


def low_lanes():
    return lax.broadcasted_iota(jnp.int32, (8, LANES), 1) < 64


def rows_kernel(place, arrived, beam, forward, cos, sin, out, image, step):
    for i in range(SLABS):
        image[pl.ds(32 * i, 32), :] = arrived[lax.rem(place[0] + i, SLABS)] * beam[pl.ds(32 * i, 32), :]
    for kk in range(0, 16, 2):
        data = jnp.concatenate([image[pl.ds(kk + n, 64, stride=16), :] for n in range(2)], axis=1)
        high, low = split(data)
        both = dot(forward[...], jnp.concatenate([high, low, high], axis=0))
        step[kk] = both[:, :LANES]
        step[kk + 1] = both[:, LANES:]
    low_half = low_lanes()
    for group in range(8):
        rho = pl.ds(8 * group, 8)
        values = []
        for kk in range(16):
            re, im = step[kk, rho, :], step[kk, pl.ds(64 + 8 * group, 8), :]
            c, s = cos[kk, rho, :], sin[kk, rho, :]
            values.append((re * c + im * s, im * c - re * s))
        spread = fourier(values, -1.0)
        for u in range(17 if group == 0 else 16):
            re, im = spread[u % 16]
            angle = 2 * math.pi * u / 32
            c = jnp.where(low_half, 1.0, math.cos(angle))
            s = jnp.where(low_half, 0.0, math.sin(angle))
            first, second = re * c + im * s, im * c - re * s
            packed = jnp.where(low_half, first, pltpu.roll(second, 64, axis=1)) + jnp.where(
                low_half, pltpu.roll(first, 64, axis=1), second
            )
            if group < 4:
                if u < 16:
                    out[u, rho, :] = packed
            else:
                out[31 - u, pl.ds(8 * (group - 4), 8), :] = packed
            if group == 4:
                out[u, pl.ds(32, 8), :] = packed
            if group == 0 and u > 0:
                out[32 - u, pl.ds(32, 8), :] = packed


def run_rows(place, arrived, beam, tables):
    smem, vmem = pltpu.SMEM, pltpu.VMEM
    forward, _, cos, sin = tables
    return call(
        rows_kernel,
        jax.ShapeDtypeStruct((SLABS, ROWS, LANES), F32),
        [pltpu.VMEM((1024, LANES), F32), pltpu.VMEM((16, LANES, LANES), F32)],
        [smem, vmem, vmem, vmem, vmem, vmem],
        300_000_000,
        3_000_000,
    )(place, arrived, beam, forward, cos, sin)


def weights_kernel(place, own, other, *refs):
    tables, (data, weight_y, weight_x, params, pick, put) = refs[:8], refs[8:]
    u, half = place[1], place[2]
    lower = half == 0
    lane = lax.broadcasted_iota(jnp.int32, (1, LANES), 1)
    mirrored = lane >= 64

    def stacked(index):
        mine, theirs = own[index], other[index]
        return jnp.concatenate([jnp.where(lower, mine, theirs), jnp.where(lower, theirs, mine)], axis=0)

    def block_parts(names, is_mirrored):
        local = names.astype(jnp.int32) - jnp.where(is_mirrored, 31 - u, u) * 512
        band, column = local >> 7, local & 127
        column = jnp.where(is_mirrored, 127 - column, column)
        side = jnp.where(is_mirrored, 1 - (band & 1), band & 1)
        held = jnp.where(is_mirrored, 1 - (band >> 1), band >> 1) == half
        return column, side, held

    named = stacked(5)
    down = lax.broadcasted_iota(jnp.int32, (LANES, 64), 0)
    column, _, _ = block_parts(named[:, :64], down >= 64)
    across = lax.broadcasted_iota(jnp.int32, (LANES, 64), 1)
    chosen = (across == (column >> 1)).astype(F32).astype(BF16)
    column, side, held = block_parts(named.T[0:1, :], mirrored)
    down = lax.broadcasted_iota(jnp.int32, (64, LANES), 0)
    chosen_t = (down == (column >> 1)).astype(F32).astype(BF16)
    for n in range(2):
        for part in range(2):
            pick[part, :, pl.ds(LANES * n, LANES)] = dot(tables[2 * n + part][...], chosen_t).astype(BF16)
            put[part, pl.ds(LANES * n, LANES), :] = dot(chosen, tables[4 + 2 * n + part][...]).astype(BF16)
    params[0:1, :] = mirrored.astype(F32)
    params[1:2, :] = side.astype(F32)
    params[2:3, :] = (column & 1).astype(F32)
    params[3:8, :] = jnp.zeros((5, LANES), F32)
    data[0] = stacked(0).T
    data[1] = stacked(1).T * jnp.where(mirrored, -1.0, 1.0)
    data[2] = stacked(2).T * held.astype(F32)
    for target, index in ((weight_y, 3), (weight_x, 4)):
        position = stacked(index).T
        position = jnp.where(mirrored, 15.0 - position, position)
        for n in range(UB):
            away = float(n) - position
            target[n] = jnp.exp(away * away * (-1.0 / 8.0))


def run_weights(place, own, other, tables):
    smem, vmem = pltpu.SMEM, pltpu.VMEM
    shape = jax.ShapeDtypeStruct
    return call(
        weights_kernel,
        [
            shape((3, VB, LANES), F32),
            shape((UB, VB, LANES), F32),
            shape((UB, VB, LANES), F32),
            shape((8, LANES), F32),
            shape((2, LANES, 2 * LANES), BF16),
            shape((2, 2 * LANES, LANES), BF16),
        ],
        [],
        [smem] + [vmem] * 10,
        20_000_000,
        3_000_000,
    )(place, own, other, *tables)


def grid_kernel(
    arrived, data, weight_y, weight_x, params, pick, put, cos, sin, out,
    turned, spec, picked, cells, padded, wide, resid,
):
    sign_flip = jnp.where(low_lanes(), -1.0, 1.0)
    chunk = KEYS * ROWS // 5
    for group in range(ROWS // 8):
        rows = pl.ds(8 * group, 8)
        keys = fourier_packed([arrived[g, rows, :] for g in range(SLABS)], -1.0, sign_flip)
        for k1 in range(33):
            value = keys[k1 % 32]
            if k1:
                value = value * cos[k1 : k1 + 1, :] + pltpu.roll(value, 64, axis=1) * sin[k1 : k1 + 1, :]
            turned[pl.ds(ROWS * k1 + 8 * group, 8), :] = value
        turned[pl.ds(ROWS * 33 + 8 * group, 8), :] = jnp.zeros((8, LANES), F32)
    for n in range(5):
        rows = pl.ds(chunk * n, chunk)
        high, low = split(turned[rows, :])
        both = dot(high, pick[0]) + dot(low, pick[0]) + dot(high, pick[1])
        spec[0, rows, :] = both[:, :LANES]
        spec[1, rows, :] = both[:, LANES:]
    mirrored, upper, odd = params[0:1, :] > 0.5, params[1:2, :] > 0.5, params[2:3, :] > 0.5

    def choose(at, step):
        return jnp.where(
            odd if step else upper,
            jnp.where(mirrored, at(17), at(16)),
            jnp.where(mirrored, at(1), at(0)),
        )

    for part in range(2):
        for k1 in range(33):
            picked[part, k1] = choose(lambda off: spec[part, pl.ds(ROWS * k1 + off, 16), :], 0)
        for b in range(UB):
            cells[part, b] = choose(lambda off: picked[part, b + off], 1)
    resid[...] = jnp.zeros(resid.shape, F32)

    def predict(a, carry):
        for top in range(0, VB, 64):
            rows = pl.ds(top, 64)
            total = [jnp.zeros((64, LANES), F32) for _ in range(2)]
            for b in range(UB):
                weight = weight_y[b, rows, :]
                for part in range(2):
                    total[part] = total[part] + weight * cells[part, b, pl.ds(a, 1), :]
            for part in range(2):
                resid[part, rows, :] += weight_x[a, rows, :] * total[part]
        return carry

    lax.fori_loop(0, UB, predict, 0)
    for part in range(2):
        resid[part] = data[2] * (data[part] - resid[part] * (1.0 / G))

    def spread(a, carry):
        for part in range(2):
            scaled = resid[part] * weight_x[a]
            for b in range(UB):
                cells[part, b, pl.ds(a, 1), :] = jnp.sum(scaled * weight_y[b], axis=0, keepdims=True)
        return carry

    lax.fori_loop(0, UB, spread, 0)
    padded[...] = jnp.zeros(padded.shape, F32)
    nothing = jnp.zeros((ROWS, LANES), F32)
    for part in range(2):
        for b in range(UB):
            padded[b, pl.ds(24, 16), :] = cells[part, b]
        for b in range(UB):
            wide[b] = choose(lambda off: padded[b, pl.ds(24 - off, ROWS), :], 0)
        for k1 in range(33):
            at = lambda off: wide[k1 - off] if 0 <= k1 - off < UB else nothing
            spec[part, pl.ds(ROWS * k1, ROWS), :] = choose(at, 1)
        spec[part, pl.ds(ROWS * 33, ROWS), :] = nothing
    for n in range(5):
        rows = pl.ds(chunk * n, chunk)
        high, low = split(jnp.concatenate([spec[0, rows, :], spec[1, rows, :]], axis=1))
        turned[rows, :] = dot(high, put[0]) + dot(low, put[0]) + dot(high, put[1])
    for group in range(ROWS // 8):
        keys = []
        for k1 in range(33):
            value = turned[pl.ds(ROWS * k1 + 8 * group, 8), :]
            if k1:
                value = value * cos[k1 : k1 + 1, :] - pltpu.roll(value, 64, axis=1) * sin[k1 : k1 + 1, :]
            keys.append(value)
        keys[0] = keys[0] + keys.pop()
        for g, value in enumerate(fourier_packed(keys, 1.0, sign_flip)):
            out[g, pl.ds(8 * group, 8), :] = value


def run_grid(arrived, weights, cos, sin):
    vmem = pltpu.VMEM
    return call(
        grid_kernel,
        jax.ShapeDtypeStruct((SLABS, ROWS, LANES), F32),
        [
            pltpu.VMEM((KEYS * ROWS, LANES), F32),
            pltpu.VMEM((2, KEYS * ROWS, LANES), F32),
            pltpu.VMEM((2, 33, UB, LANES), F32),
            pltpu.VMEM((2, UB, UB, LANES), F32),
            pltpu.VMEM((UB, 64, LANES), F32),
            pltpu.VMEM((UB, ROWS, LANES), F32),
            pltpu.VMEM((2, VB, LANES), F32),
        ],
        [vmem] * 9,
        1_000_000_000,
        5_000_000,
    )(arrived, *weights, cos, sin)


def image_kernel(place, arrived, beam, back, cos, sin, out, step, image, *, groups):
    low_half = low_lanes()
    for group in range(8):
        rho = pl.ds(8 * group, 8)
        values = []
        for u in range(16):
            if group < 4:
                packed = arrived[u, rho, :]
                if group == 0 and u > 0:
                    packed = packed + arrived[32 - u, pl.ds(32, 8), :]
            else:
                packed = arrived[31 - u, pl.ds(8 * (group - 4), 8), :]
                if group == 4:
                    packed = packed + arrived[u, pl.ds(32, 8), :]
            crossed = pltpu.roll(packed, 64, axis=1)
            c, s = math.cos(2 * math.pi * u / 32), math.sin(2 * math.pi * u / 32)
            re = jnp.where(low_half, packed, crossed * c - packed * s)
            im = jnp.where(low_half, crossed, packed * c + crossed * s)
            if group == 0 and u == 0:
                packed = arrived[16, pl.ds(32, 8), :]
                crossed = pltpu.roll(packed, 64, axis=1)
                re = re + jnp.where(low_half, packed, -crossed)
                im = im + jnp.where(low_half, crossed, -packed)
            values.append((re, im))
        for kk, (re, im) in enumerate(fourier(values, 1.0)):
            c, s = cos[kk, rho, :], sin[kk, rho, :]
            step[kk, rho, :] = re * c - im * s
            step[kk, pl.ds(64 + 8 * group, 8), :] = re * s + im * c
    for kk in range(0, 16, 2):
        high, low = split(jnp.concatenate([step[kk], step[kk + 1]], axis=1))
        both = dot(back[...], jnp.concatenate([high, low, high], axis=0))
        image[pl.ds(kk, 64, stride=16), :] = both[:, :LANES]
        image[pl.ds(kk + 1, 64, stride=16), :] = both[:, LANES:]
    share = 32 // groups
    for i in range(SLABS):
        target = lax.rem(place[0] + i, SLABS) * share
        for n in range(share):
            rows = pl.ds(32 * i + n, groups, stride=share)
            out[pl.ds(target + n, groups, stride=32 * share), :] = image[rows, :] * beam[rows, :]


def run_image(place, arrived, beam, tables, groups):
    smem, vmem = pltpu.SMEM, pltpu.VMEM
    _, back, cos, sin = tables

    def kernel(*refs):
        image_kernel(*refs, groups=groups)

    return call(
        kernel,
        jax.ShapeDtypeStruct((1024, LANES), F32),
        [pltpu.VMEM((16, LANES, LANES), F32), pltpu.VMEM((1024, LANES), F32)],
        [smem, vmem, vmem, vmem, vmem, vmem],
        300_000_000,
        3_000_000,
    )(place, arrived, beam, back, cos, sin)


def home_kernel(starts, arrived, out, total, *, groups):
    share = 32 // groups
    total[...] = jnp.zeros(total.shape, F32)
    margin = jnp.zeros((8, LANES), F32)
    for p in range(groups):
        start = starts[p]
        rows = pl.ds(pl.multiple_of(start // 8 * 8, 8), 40)
        for n in range(share):
            lanes = pl.ds(LANES * n, LANES)
            part = jnp.concatenate([arrived[pl.ds(32 * share * p + n, 32, stride=share), :], margin], axis=0)
            total[rows, lanes] += pltpu.roll(part, lax.rem(start, 8), axis=0)
    out[...] = total[pl.ds(0, LANES), :]


def run_home(starts, arrived, groups):
    def kernel(*refs):
        home_kernel(*refs, groups=groups)

    return call(
        kernel,
        jax.ShapeDtypeStruct((LANES, 4096 // groups), F32),
        [pltpu.VMEM((LANES + 8, 4096 // groups), F32)],
        [pltpu.SMEM, pltpu.VMEM],
        300_000,
        1_000_000,
    )(starts, arrived)


def body(sky_model, intersection, beam, vis_data, vis_weight, vis_pos, uv_block, counts):
    groups = lax.axis_size("pt")
    mine = lax.axis_index("fft")
    corner = intersection[0, 0]
    top = corner // 128 + corner % 128 // 64 * 32
    left = corner % 64
    row = top + (mine - top) % SLABS
    start = row // SLABS * 64 + left
    half = mine // HALF
    u = jnp.where(half == 0, mine, SLABS - 1 - mine)
    place = jnp.stack([top, u, half, start]).astype(jnp.int32)
    start_block = lax.optimization_barrier(jnp.full((128, LANES), start, jnp.int32))
    starts = lax.optimization_barrier(lax.all_gather(start_block, "pt"))[:, 0, 0]

    outgoing = lax.dynamic_slice(sky_model, (start, 0), (SLABS, TS * TS)).reshape(SLABS, 32, LANES)
    arrived = lax.all_to_all(outgoing, "fft", split_axis=0, concat_axis=0, tiled=True)

    used = (jnp.arange(NB, dtype=jnp.int32)[:, None] < counts[0, 0]).astype(F32)
    named = jnp.broadcast_to(uv_block[0].astype(F32)[:, None], (NB, VB))
    own = jnp.stack([vis_data[0, 0], vis_data[1, 0], used * vis_weight[0], vis_pos[0, 0], vis_pos[1, 0], named])
    other = lax.ppermute(own, "fft", [(n, SLABS - 1 - n) for n in range(SLABS)])
    col_tables, cos, sin = column_tables()
    weights = run_weights(place, own, other, col_tables)

    row_parts = row_tables()
    packed_beam = beam.reshape(1024, LANES)
    rows_out = run_rows(place, arrived, packed_beam, row_parts)
    rows_in = lax.all_to_all(rows_out, "fft", split_axis=0, concat_axis=0, tiled=True)
    grid_out = run_grid(rows_in, weights, cos, sin)
    grid_in = lax.all_to_all(grid_out, "fft", split_axis=0, concat_axis=0, tiled=True)
    tiles = run_image(place, grid_in, packed_beam, row_parts, groups)
    share = 32 // groups
    tiles = tiles.reshape(groups * SLABS, share, LANES)
    home = lax.all_to_all(tiles, ("pt", "fft"), split_axis=0, concat_axis=0, tiled=True)
    return run_home(starts, home.reshape(1024, LANES), groups)


def solution(mesh):
    in_specs = (
        P("fft", None),
        P("pt", None),
        P(None, "pt", "fft"),
        P(None, "pt", "fft", None),
        P("pt", "fft", None),
        P(None, "pt", "fft", None),
        P("pt", "fft"),
        P("pt", "fft"),
    )
    return jax.shard_map(body, mesh=mesh, in_specs=in_specs, out_specs=P("fft", "pt"), check_vma=False)
```

time: 394 us -> 207 us (0.53)
  the two profiles are of different devices: /device:TPU:16 before, /device:TPU:38 now
where the time goes in v1:
time: 207 us; the launch traced here: 205 us
  waiting for transfers between devices  86.9 us (42%)
  starting transfers between devices  53.5 us (26%)
  local copies, waits for them, and re-layouts  31.4 us (15%)
  between operations  17 us (8%)
  Pallas kernels  14.1 us (7%)
  other arithmetic  2.07 us (1%)
    all_gather x1, waiting for transfers between devices, body(): lax.all_gather(start_block, 'pt')  45.2 us
    unnamed x81, local copies, waits for them, and re-layouts  26.7 us
    all_to_all x1, starting transfers between devices, body(): lax.all_to_all(tiles, ('pt', 'fft'), split_axis=0, concat_axis=0, tiled=T...  21.4 us
    ppermute x1, waiting for transfers between devices, body(): other = lax.ppermute(own, 'fft', [(n, SLABS - 1 - n) for n in range(SLABS)])  18.7 us
    all_to_all x1, waiting for transfers between devices, body(): lax.all_to_all(grid_out, 'fft', split_axis=0, concat_axis=0, tiled=True)  14.5 us
    all_to_all x1, starting transfers between devices, body(): lax.all_to_all(rows_out, 'fft', split_axis=0, concat_axis=0, tiled=True)  10.2 us
    all_to_all x1, starting transfers between devices, body(): lax.all_to_all(outgoing, 'fft', split_axis=0, concat_axis=0, tiled=True)  9.91 us
    all_to_all x1, starting transfers between devices, body(): lax.all_to_all(grid_out, 'fft', split_axis=0, concat_axis=0, tiled=True)  9.77 us
  transfers between devices with their start and end apart: 6, of which 4 were waited for; matrix products, arithmetic and copies ran while one was open for 4% of the time, Pallas kernels for 1%

profile of v1, /device:TPU:38, one launch (start us, length us, event | category | flops | bytes accessed | tf_op | source)
XLA Modules:
  0.0 204.9 jit_solution(17099205788728817600)
XLA Ops:
  6.5 0.0 copy-start
  6.5 1.3 slice.18
  10.5 0.0 copy-done
  10.6 0.1 dynamic-slice_bitcast_fusion
  10.6 0.9 copy.26
  11.5 9.9 %all-to-all-start = ((f32[32,32,128]{2,1,0:T(8,128)}), f32[32,32,128]{2,1,0:T(8,128)S(1)}, u32[]{:S(2)}, u32[]{:S(2)}) async-start(f32[32,32,128]{2,1,0:T(8,128)} %bitcast.15), calls=%async_computation | async-start | bytes 1048576 | tf_op jit(solution)/shard_map/all_to_all | solution.py:456
  22.1 1.3 copy.25
  23.5 1.4 reshape.28.beam.refs_2_
  24.9 0.5 compare_convert_fusion
  25.4 0.1 pad_add_fusion.place.refs_0_
  25.5 8.4 %all-to-all-done.arrived = f32[32,32,128]{2,1,0:T(8,128)S(1)} async-done(((f32[32,32,128]{2,1,0:T(8,128)}), f32[32,32,128]{2,1,0:T(8,128)S(1)}, u32[]{:S(2)}, u32[]{:S(2)}) %all-to-all-start) | async-done | bytes 524320 | tf_op jit(solution)/shard_map/all_to_all | solution.py:456
  33.9 1.0 copy-done.4
  35.0 1.0 copy-done.6
  36.0 1.6 shard_map.208
  37.6 0.8 copy-done.1
  38.4 10.2 %all-to-all-start.1 = ((f32[32,40,128]{2,1,0:T(8,128)}), f32[32,40,128]{2,1,0:T(8,128)S(1)}, u32[]{:S(2)}, u32[]{:S(2)}) async-start(f32[32,40,128]{2,1,0:T(8,128)} %copy-done.1), calls=%async_computation.1 | async-start | bytes 1310720 | tf_op jit(solution)/shard_map/all_to_all | solution.py:468
  48.6 0.7 convert_bitcast_fusion
  49.3 0.8 multiply_dynamic-update-slice_fusion
  50.1 0.8 bitcast_dynamic-update-slice_fusion.1
  50.9 0.8 bitcast_dynamic-update-slice_fusion
  51.7 0.1 broadcast_dynamic-update-slice_fusion.own
  51.7 2.2 %collective-permute-start = (f32[6,64,128]{2,1,0:T(8,128)S(1)}, f32[6,64,128]{2,1,0:T(8,128)S(1)}, u32[]{:S(2)}, u32[]{:S(2)}) collective-permute-start(f32[6,64,128]{2,1,0:T(8,128)S(1)} %broadcast_dynamic-update-slice_fusion.own), channel_id=1, source_target_pairs={{0,31},{1,30},{2,29},{3,28},{4,27},{5,26},{6,25},{7,24},{8,23},{9,... | collective-permute-start | bytes 589832 | tf_op jit(solution)/shard_map/ppermute | solution.py:461
  54.0 18.7 %collective-permute-done.other = f32[6,64,128]{2,1,0:T(8,128)S(1)} collective-permute-done((f32[6,64,128]{2,1,0:T(8,128)S(1)}, f32[6,64,128]{2,1,0:T(8,128)S(1)}, u32[]{:S(2)}, u32[]{:S(2)}) %collective-permute-start) | collective-permute-done | bytes 196640 | tf_op jit(solution)/shard_map/ppermute | solution.py:461
  72.7 0.0 copy-done.21
  72.7 0.0 copy-start.22
  72.7 0.7 copy-done.22
  73.4 0.8 copy-done.23
  74.2 0.7 copy-done.27
  74.9 0.7 copy-done.28
  75.6 0.7 copy-done.29
  76.3 0.7 copy-done.31
  77.0 1.1 shard_map.209
  78.1 1.0 copy-done.8
  79.1 1.0 copy-done.10
  80.1 0.7 copy-done.12
  80.7 0.7 copy-done.14
  81.4 0.7 copy-done.16
  82.1 0.6 copy-done.33
  82.6 0.0 all-to-all-done.1.arrived
  82.7 1.2 copy-done.9
  83.9 1.2 copy-done.11
  85.1 0.9 copy-done.13
  86.0 0.9 copy-done.15
  86.9 0.9 copy-done.17
  87.8 0.7 copy-done.24
  88.6 0.7 copy-done.25
  89.3 0.7 copy-done.34
  90.0 8.2 %shard_map.210 = f32[32,40,128]{2,1,0:T(8,128)S(1)} custom-call(f32[32,40,128]{2,1,0:T(8,128)S(1)} %all-to-all-done.1.arrived, f32[3,128,128]{2,1,0:T(8,128)S(1)} %copy-done.13, f32[16,128,128]{2,1,0:T(8,128)S(1)} %copy-done.9, f32[16,128,128]{2,1,0:T(8,128)S(1)} %copy-done.11, f32[8,128]{1,0:T(8,128)S(1)} %copy-done.34, ...), custom_call_target="tpu_custom_call" | custom-call | flops 1000000000 | bytes 5000000 | tf_op jit(solution)/shard_map/pallas_call | solution.py:337
  98.2 0.8 copy-done.2
  99.1 9.8 %all-to-all-start.2 = ((f32[32,40,128]{2,1,0:T(8,128)}), f32[32,40,128]{2,1,0:T(8,128)S(1)}, u32[]{:S(2)}, u32[]{:S(2)}) async-start(f32[32,40,128]{2,1,0:T(8,128)} %copy-done.2), calls=%async_computation.2 | async-start | bytes 1310720 | tf_op jit(solution)/shard_map/all_to_all | solution.py:470
  108.8 0.0 all-gather.3.cloned.1.call-start
  108.9 0.6 broadcast_in_dim.2
  109.5 0.0 all-gather.3.cloned.1.call-update
  109.6 14.5 %all-to-all-done.2.refs_1_ = f32[32,40,128]{2,1,0:T(8,128)S(1)} async-done(((f32[32,40,128]{2,1,0:T(8,128)}), f32[32,40,128]{2,1,0:T(8,128)S(1)}, u32[]{:S(2)}, u32[]{:S(2)}) %all-to-all-start.2) | async-done | bytes 655392 | tf_op jit(solution)/shard_map/all_to_all | solution.py:470
  124.1 1.0 copy-done.5
  125.1 1.0 copy-done.7
  126.2 1.9 shard_map.211
  128.1 0.0 copy-start.3
  128.1 0.8 copy-done.3
  128.9 21.4 %all-to-all-start.3 = ((f32[512,2,128]{2,1,0:T(2,128)}), f32[512,2,128]{2,1,0:T(2,128)S(1)}, u32[]{:S(2)}, u32[]{:S(2)}) async-start(f32[512,2,128]{2,1,0:T(2,128)} %bitcast.26), calls=%async_computation.3 | async-start | bytes 1048576 | tf_op jit(solution)/shard_map/all_to_all | solution.py:474
  150.3 45.2 %all-gather.3.cloned.1.call-done = s32[2048,128]{1,0:T(8,128)} async-done(((s32[128,128]{1,0:T(8,128)}), s32[2048,128]{1,0:T(8,128)}) %all-gather.3.cloned.1.call-update) | async-done | bytes 1048592 | tf_op jit(solution)/shard_map/all_gather | solution.py:453
  195.5 1.2 slice_reduce_fusion.refs_0_
  196.7 0.0 all-to-all-done.3
  196.7 1.4 shard_map.212
  (44 shorter events, 0.1 us)
Async XLA Ops:
  6.5 4.0 %copy-start = (f32[128,4096]{1,0:T(8,128)S(1)}, f32[128,4096]{1,0:T(8,128)}, u32[]{:S(2)}) copy-start(f32[128,4096]{1,0:T(8,128)} %param.22) | copy-start | bytes 6291460
  6.5 15.6 %copy-start.35 = (f32[2048,1,64]{0,2,1:T(8,128)S(1)}, f32[2048,1,64]{0,2,1:T(8,128)}, u32[]{:S(2)}) copy-start(f32[2048,1,64]{0,2,1:T(8,128)} %param.24) | copy-start | bytes 1572868
  11.5 14.0 %copy-start.36 = (f32[2,1,64,128]{3,2,1,0:T(8,128)S(1)}, f32[2,1,64,128]{3,2,1,0:T(8,128)}, u32[]{:S(2)}) copy-start(f32[2,1,64,128]{3,2,1,0:T(8,128)} %param.25) | copy-start | bytes 196612
  11.5 22.4 %copy-start.18 = (bf16[128,192]{1,0:T(8,128)(2,1)S(1)}, bf16[128,192]{1,0:T(8,128)(2,1)}, u32[]{:S(2)}) copy-start(bf16[128,192]{1,0:T(8,128)(2,1)} %constant.117.clone.forward) | copy-start | bytes 147460
  11.5 22.4 %all-to-all-start = ((f32[32,32,128]{2,1,0:T(8,128)}), f32[32,32,128]{2,1,0:T(8,128)S(1)}, u32[]{:S(2)}, u32[]{:S(2)}) async-start(f32[32,32,128]{2,1,0:T(8,128)} %bitcast.15), calls=%async_computation | async-start | bytes 1048576 | tf_op jit(solution)/shard_map/all_to_all | solution.py:456
  25.5 12.9 %copy-start.30 = (s32[4]{0:T(128)}, s32[4]{0:T(128)S(1)}, u32[]{:S(2)}) copy-start(s32[4]{0:T(128)S(1)} %pad_add_fusion.place.refs_0_) | copy-start | bytes 52
  33.9 1.0 copy-start.4
  35.0 1.0 copy-start.6
  36.0 36.6 %copy-start.20 = (bf16[128,64]{1,0:T(8,128)(2,1)S(1)}, bf16[128,64]{1,0:T(8,128)(2,1)}, u32[]{:S(2)}) copy-start(bf16[128,64]{1,0:T(8,128)(2,1)} %constant.112.clone.refs_3_) | copy-start | bytes 49156
  36.0 36.6 %copy-start.21 = (bf16[128,64]{1,0:T(8,128)(2,1)S(1)}, bf16[128,64]{1,0:T(8,128)(2,1)}, u32[]{:S(2)}) copy-start(bf16[128,64]{1,0:T(8,128)(2,1)} %constant.111.clone.refs_2_) | copy-start | bytes 49156
  36.0 36.6 %copy-start.26 = (bf16[64,128]{1,0:T(8,128)(2,1)S(1)}, bf16[64,128]{1,0:T(8,128)(2,1)}, u32[]{:S(2)}) copy-start(bf16[64,128]{1,0:T(8,128)(2,1)} %constant.116.clone.refs_7_) | copy-start | bytes 49156
  37.6 0.8 copy-start.1
  38.4 44.2 %all-to-all-start.1 = ((f32[32,40,128]{2,1,0:T(8,128)}), f32[32,40,128]{2,1,0:T(8,128)S(1)}, u32[]{:S(2)}, u32[]{:S(2)}) async-start(f32[32,40,128]{2,1,0:T(8,128)} %copy-done.1), calls=%async_computation.1 | async-start | bytes 1310720 | tf_op jit(solution)/shard_map/all_to_all | solution.py:468
  51.7 20.9 %collective-permute-start = (f32[6,64,128]{2,1,0:T(8,128)S(1)}, f32[6,64,128]{2,1,0:T(8,128)S(1)}, u32[]{:S(2)}, u32[]{:S(2)}) collective-permute-start(f32[6,64,128]{2,1,0:T(8,128)S(1)} %broadcast_dynamic-update-slice_fusion.own), channel_id=1, source_target_pairs={{0,31},{1,30},{2,29},{3,28},{4,27},{5,26},{6,25},{7,24},{8,23},{9,... | collective-permute-start | bytes 589832 | tf_op jit(solution)/shard_map/ppermute | solution.py:461
  72.7 0.8 copy-start.22
  73.4 0.8 copy-start.23
  74.2 0.7 copy-start.27
  74.9 0.7 copy-start.28
  75.6 0.7 copy-start.29
  76.3 0.7 copy-start.31
  78.1 1.0 copy-start.8
  79.1 1.0 copy-start.10
  80.1 0.7 copy-start.12
  80.7 0.7 copy-start.14
  81.4 0.7 copy-start.16
  82.1 0.6 copy-start.33
  82.7 1.2 copy-start.9
  83.9 1.2 copy-start.11
  85.1 0.9 copy-start.13
  86.0 0.9 copy-start.15
  86.9 0.9 copy-start.17
  87.8 0.7 copy-start.24
  88.6 0.7 copy-start.25
  89.3 0.7 copy-start.34
  90.0 34.1 %copy-start.19 = (bf16[64,384]{1,0:T(8,128)(2,1)S(1)}, bf16[64,384]{1,0:T(8,128)(2,1)}, u32[]{:S(2)}) copy-start(bf16[64,384]{1,0:T(8,128)(2,1)} %constant.122.clone.refs_3_) | copy-start | bytes 147460
  90.0 34.1 %copy-start.32 = (s32[4]{0:T(128)S(1)}, s32[4]{0:T(128)}, u32[]{:S(2)}) copy-start(s32[4]{0:T(128)} %copy-done.30) | copy-start | bytes 52
  98.2 0.8 copy-start.2
  99.1 25.0 %all-to-all-start.2 = ((f32[32,40,128]{2,1,0:T(8,128)}), f32[32,40,128]{2,1,0:T(8,128)S(1)}, u32[]{:S(2)}, u32[]{:S(2)}) async-start(f32[32,40,128]{2,1,0:T(8,128)} %copy-done.2), calls=%async_computation.2 | async-start | bytes 1310720 | tf_op jit(solution)/shard_map/all_to_all | solution.py:470
  108.8 86.6 %all-gather.3.cloned.1.call-start = ((), (), s32[]{:S(2)}) async-start(), calls=%async_computation.4 | async-start | bytes 1114112 | tf_op jit(solution)/shard_map/all_gather | solution.py:453
  124.1 1.0 copy-start.5
  125.1 1.0 copy-start.7
  128.1 0.8 copy-start.3
  128.9 67.8 %all-to-all-start.3 = ((f32[512,2,128]{2,1,0:T(2,128)}), f32[512,2,128]{2,1,0:T(2,128)S(1)}, u32[]{:S(2)}, u32[]{:S(2)}) async-start(f32[512,2,128]{2,1,0:T(2,128)} %bitcast.26), calls=%async_computation.3 | async-start | bytes 1048576 | tf_op jit(solution)/shard_map/all_to_all | solution.py:474
Sparse Core Ops, SparseCore 0:
  111.8 83.6 all-gather.2

commit v2 on v1

v2 whole, which is shorter than its diff:
```python
import math

import jax
import jax.numpy as jnp
import numpy as np
from jax import lax
from jax.experimental import pallas as pl
from jax.experimental.pallas import tpu as pltpu
from jax.sharding import PartitionSpec as P

G = 2048
TS = 64
UB = 16
VB = 128
NB = 64
SLABS = 32
HALF = 16
ROWS = 33
PITCH = 40
KEYS = 34
LANES = 128
VMEM_BYTES = 24 * 1024 * 1024
INTERPRET = False

F32 = jnp.float32
BF16 = jnp.bfloat16


def split_np(table):
    high = np.asarray(table, np.float32).astype(jnp.bfloat16)
    low = (np.asarray(table, np.float64) - high.astype(np.float64)).astype(jnp.bfloat16)
    return high, low


def split(value):
    high = value.astype(BF16)
    return high, (value - high.astype(F32)).astype(BF16)


def dot(left, right):
    return jnp.dot(left, right, preferred_element_type=F32)


def row_tables():
    rho, x1 = np.arange(64)[:, None], np.arange(64)[None, :]
    angle = 2 * np.pi * (rho * x1 % 64) / 64
    forward = np.concatenate([np.cos(angle), -np.sin(angle)], 0)
    high, low = split_np(forward)
    forward_cat = np.concatenate([high, high, low], 1)
    back = np.concatenate([np.cos(angle).T, -np.sin(angle).T], 1) / G
    high, low = split_np(back)
    back_cat = np.concatenate([high, high, low], 1)
    x0 = 2 * np.arange(16)[:, None, None] + (np.arange(LANES) >= 64)[None, None, :]
    twist = 2 * np.pi * (x0 * np.arange(64)[None, :, None]) / G
    return forward_cat, back_cat, np.cos(twist).astype(np.float32), np.sin(twist).astype(np.float32)


def column_tables():
    cols, keys = np.arange(64)[:, None], np.arange(64)[None, :]
    angle = 2 * np.pi * (cols * keys % 64) / 64
    first = np.concatenate([np.cos(angle), np.sin(angle)], 0)
    second = np.concatenate([-np.sin(angle), np.cos(angle)], 0)
    pick = [np.stack(split_np(table)) for table in (first, second)]
    put = [np.stack(split_np(table.T)) for table in (first, second)]
    tables = np.stack(pick), np.stack(put)
    k1 = np.arange(PITCH)[:, None]
    lane = np.arange(LANES)[None, :]
    twist = 2 * np.pi * (k1 * (lane % 64)) / G
    cos = np.cos(twist).astype(np.float32)
    sin = (np.sin(twist) * np.where(lane < 64, 1.0, -1.0)).astype(np.float32)
    return tables, cos, sin


def turn(re, im, angle):
    c, s = math.cos(angle), math.sin(angle)
    if abs(s) < 1e-12:
        return (re, im) if c > 0 else (-re, -im)
    if abs(c) < 1e-12:
        return (-im, re) if s > 0 else (im, -re)
    return re * c - im * s, re * s + im * c


def fourier(values, sign):
    count = len(values)
    if count == 1:
        return values
    even, odd = fourier(values[::2], sign), fourier(values[1::2], sign)
    out = [None] * count
    for k in range(count // 2):
        re, im = turn(*odd[k], sign * 2 * math.pi * k / count)
        out[k] = (even[k][0] + re, even[k][1] + im)
        out[k + count // 2] = (even[k][0] - re, even[k][1] - im)
    return out


def fourier_packed(values, sign, flip):
    count = len(values)
    if count == 1:
        return values
    even, odd = fourier_packed(values[::2], sign, flip), fourier_packed(values[1::2], sign, flip)
    out = [None] * count
    for k in range(count // 2):
        angle = sign * 2 * math.pi * k / count
        c, s = math.cos(angle), math.sin(angle)
        value = odd[k]
        if k:
            crossed = pltpu.roll(value, 64, axis=1) * (flip * s)
            value = crossed if abs(c) < 1e-12 else value * c + crossed
        out[k] = even[k] + value
        out[k + count // 2] = even[k] - value
    return out


def call(kernel, out_shape, scratch, spaces, out_spaces, flops, data):
    return pl.pallas_call(
        kernel,
        out_shape=out_shape,
        in_specs=[pl.BlockSpec(memory_space=space) for space in spaces],
        out_specs=[pl.BlockSpec(memory_space=space) for space in out_spaces],
        scratch_shapes=scratch,
        compiler_params=pltpu.CompilerParams(vmem_limit_bytes=VMEM_BYTES),
        cost_estimate=pl.CostEstimate(flops=flops, bytes_accessed=data, transcendentals=0),
        interpret=INTERPRET,
    )


def start_copies(pairs, sems):
    copies = [pltpu.make_async_copy(src, dst, sems.at[n]) for n, (src, dst) in enumerate(pairs)]
    for copy in copies:
        copy.start()
    return copies


def window_corner(intersection):
    corner = intersection[0, 0]
    return (corner >> 7) + ((corner >> 6) & 1) * 32, corner & 63


def low_lanes():
    return lax.broadcasted_iota(jnp.int32, (8, LANES), 1) < 64


def send_kernel(
    intersection, counts, names, sky, vis_data, vis_weight, vis_pos, tiles, own,
    sky_rows, parts, weight, turned, sems,
):
    top, left = window_corner(intersection)
    mine = lax.axis_index("fft")
    row = top + ((mine - top) & 31)
    start = (row >> 5) * 64 + left
    first = jnp.minimum(start >> 3, 11) * 8
    copies = start_copies(
        [
            (sky.at[pl.ds(pl.multiple_of(first, 8), 40), :], sky_rows),
            (vis_weight.at[0], weight),
            (vis_data.at[:, 0], parts.at[pl.ds(0, 2)]),
            (vis_pos.at[:, 0], parts.at[pl.ds(3, 2)]),
        ],
        sems,
    )
    shift = lax.rem(40 - (start - first), 40)
    copies[0].wait()
    for n in range(32):
        rows = pltpu.roll(sky_rows[:, LANES * n : LANES * (n + 1)], shift, axis=0)
        turned[pl.ds(n, SLABS, stride=32), :] = rows[:32]
    tiles_out = pltpu.make_async_copy(turned, tiles, sems.at[4])
    tiles_out.start()
    parts[5] = jnp.broadcast_to(names[...].astype(F32), (VB, NB)).T
    copies[1].wait()
    used = lax.broadcasted_iota(jnp.int32, (NB, VB), 0) < counts[0, 0]
    parts[2] = jnp.where(used, weight[...], 0.0)
    copies[2].wait()
    copies[3].wait()
    own_out = pltpu.make_async_copy(parts, own, sems.at[5])
    own_out.start()
    tiles_out.wait()
    own_out.wait()


def run_send(intersection, counts, names, sky, vis_data, vis_weight, vis_pos):
    smem, vmem, far = pltpu.SMEM, pltpu.VMEM, pl.ANY
    shape = jax.ShapeDtypeStruct
    return call(
        send_kernel,
        [shape((1024, LANES), F32), shape((6, NB, VB), F32)],
        [
            pltpu.VMEM((40, TS * TS), F32),
            pltpu.VMEM((6, NB, VB), F32),
            pltpu.VMEM((NB, VB), F32),
            pltpu.VMEM((1024, LANES), F32),
            pltpu.SemaphoreType.DMA((6,)),
        ],
        [smem, smem, vmem, far, far, far, far],
        [far, far],
        1_000_000,
        2_000_000,
    )(intersection, counts, names, sky, vis_data, vis_weight, vis_pos)


def rows_kernel(
    intersection, arrived, beam, forward_far, cos_far, sin_far, other, out,
    image, step, forward, cos, sin, message, sems,
):
    del other
    copies = start_copies([(forward_far, forward), (cos_far, cos), (sin_far, sin)], sems)
    top, _ = window_corner(intersection)
    for i in range(SLABS):
        image[pl.ds(32 * i, 32), :] = arrived[(top + i) & 31] * beam[pl.ds(32 * i, 32), :]
    copies[0].wait()
    for kk in range(0, 16, 2):
        data = jnp.concatenate([image[pl.ds(kk + n, 64, stride=16), :] for n in range(2)], axis=1)
        high, low = split(data)
        both = dot(forward[...], jnp.concatenate([high, low, high], axis=0))
        step[kk] = both[:, :LANES]
        step[kk + 1] = both[:, LANES:]
    copies[1].wait()
    copies[2].wait()
    low_half = low_lanes()
    sent = []
    for group in (4, 5, 6, 7, 0, 1, 2, 3):
        rho = pl.ds(8 * group, 8)
        values = []
        for kk in range(16):
            re, im = step[kk, rho, :], step[kk, pl.ds(64 + 8 * group, 8), :]
            c, s = cos[kk, rho, :], sin[kk, rho, :]
            values.append((re * c + im * s, im * c - re * s))
        spread = fourier(values, -1.0)
        for u in range(17 if group == 0 else 16):
            re, im = spread[u % 16]
            angle = 2 * math.pi * u / 32
            c = jnp.where(low_half, 1.0, math.cos(angle))
            s = jnp.where(low_half, 0.0, math.sin(angle))
            first, second = re * c + im * s, im * c - re * s
            packed = jnp.where(low_half, first, pltpu.roll(second, 64, axis=1)) + jnp.where(
                low_half, pltpu.roll(first, 64, axis=1), second
            )
            if group >= 4:
                message[pl.ds(ROWS * (31 - u) + 8 * (group - 4), 8), :] = packed
            elif u < 16:
                message[pl.ds(ROWS * u + 8 * group, 8), :] = packed
            if group == 4:
                message[pl.ds(ROWS * u + 32, 1), :] = packed[:1]
            if group == 0 and u > 0:
                message[pl.ds(ROWS * (32 - u) + 32, 1), :] = packed[:1]
        if group in (0, 3):
            rows = pl.ds(16 * ROWS if group == 0 else 0, 16 * ROWS)
            sent.append(pltpu.make_async_copy(message.at[rows], out.at[rows], sems.at[3 + len(sent)]))
            sent[-1].start()
    for copy in sent:
        copy.wait()


def run_rows(intersection, arrived, beam, other, tables):
    smem, vmem, far = pltpu.SMEM, pltpu.VMEM, pl.ANY
    forward, _, cos, sin = tables
    return call(
        rows_kernel,
        [jax.ShapeDtypeStruct((SLABS * ROWS, LANES), F32)],
        [
            pltpu.VMEM((1024, LANES), F32),
            pltpu.VMEM((16, LANES, LANES), F32),
            pltpu.VMEM(forward.shape, BF16),
            pltpu.VMEM(cos.shape, F32),
            pltpu.VMEM(sin.shape, F32),
            pltpu.VMEM((SLABS * ROWS, LANES), F32),
            pltpu.SemaphoreType.DMA((5,)),
        ],
        [smem, vmem, vmem, far, far, far, far],
        [far],
        300_000_000,
        3_000_000,
    )(intersection, arrived, beam, forward, cos, sin, other)[0]


def weights_kernel(own_far, other_far, picks_far, puts_far, *refs):
    outs, held_outs = refs[:6], refs[6:12]
    own, other, picks, puts, sems = refs[12:]
    data, weight_y, weight_x, params, pick, put = held_outs
    copies = start_copies([(own_far, own), (other_far, other), (picks_far, picks), (puts_far, puts)], sems)
    mine = lax.axis_index("fft")
    half = mine >> 4
    u = jnp.where(half == 0, mine, SLABS - 1 - mine)
    for copy in copies:
        copy.wait()
    lower = half == 0
    lane = lax.broadcasted_iota(jnp.int32, (1, LANES), 1)
    mirrored = lane >= 64

    def stacked(index):
        mine, theirs = own[index], other[index]
        return jnp.concatenate([jnp.where(lower, mine, theirs), jnp.where(lower, theirs, mine)], axis=0)

    def block_parts(names, is_mirrored):
        local = names.astype(jnp.int32) - jnp.where(is_mirrored, 31 - u, u) * 512
        band, column = local >> 7, local & 127
        column = jnp.where(is_mirrored, 127 - column, column)
        side = jnp.where(is_mirrored, 1 - (band & 1), band & 1)
        held = jnp.where(is_mirrored, 1 - (band >> 1), band >> 1) == half
        return column, side, held

    named = stacked(5)
    down = lax.broadcasted_iota(jnp.int32, (LANES, 64), 0)
    column, _, _ = block_parts(named[:, :64], down >= 64)
    across = lax.broadcasted_iota(jnp.int32, (LANES, 64), 1)
    chosen = (across == (column >> 1)).astype(F32).astype(BF16)
    column, side, held = block_parts(named.T[0:1, :], mirrored)
    down = lax.broadcasted_iota(jnp.int32, (64, LANES), 0)
    chosen_t = (down == (column >> 1)).astype(F32).astype(BF16)
    for n in range(2):
        for part in range(2):
            pick[part, :, pl.ds(LANES * n, LANES)] = dot(picks[n, part], chosen_t).astype(BF16)
            put[part, pl.ds(LANES * n, LANES), :] = dot(chosen, puts[n, part]).astype(BF16)
    params[0:1, :] = mirrored.astype(F32)
    params[1:2, :] = side.astype(F32)
    params[2:3, :] = (column & 1).astype(F32)
    params[3:8, :] = jnp.zeros((5, LANES), F32)
    data[0] = stacked(0).T
    data[1] = stacked(1).T * jnp.where(mirrored, -1.0, 1.0)
    data[2] = stacked(2).T * held.astype(F32)
    for target, index in ((weight_y, 3), (weight_x, 4)):
        position = stacked(index).T
        position = jnp.where(mirrored, 15.0 - position, position)
        for n in range(UB):
            away = float(n) - position
            target[n] = jnp.exp(away * away * (-1.0 / 8.0))
    for copy in start_copies(zip(held_outs, outs), sems):
        copy.wait()


WEIGHT_SHAPES = [
    ((3, VB, LANES), F32),
    ((UB, VB, LANES), F32),
    ((UB, VB, LANES), F32),
    ((8, LANES), F32),
    ((2, LANES, 2 * LANES), BF16),
    ((2, 2 * LANES, LANES), BF16),
]


def run_weights(own, other, tables):
    far = pl.ANY
    picks, puts = tables
    return call(
        weights_kernel,
        [jax.ShapeDtypeStruct(*shape) for shape in WEIGHT_SHAPES],
        [pltpu.VMEM(*shape) for shape in WEIGHT_SHAPES]
        + [
            pltpu.VMEM((6, NB, VB), F32),
            pltpu.VMEM((6, NB, VB), F32),
            pltpu.VMEM(picks.shape, BF16),
            pltpu.VMEM(puts.shape, BF16),
            pltpu.SemaphoreType.DMA((6,)),
        ],
        [far] * 4,
        [far] * 6,
        20_000_000,
        3_000_000,
    )(own, other, picks, puts)


def grid_kernel(arrived, *refs):
    sources, out, held, sems = refs[:8], refs[8], refs[9:17], refs[-1]
    turned, spec, picked, cells, padded, wide, resid = refs[17:24]
    params, cos, sin, pick, data, weight_y, weight_x, put = held
    copies = start_copies(zip(sources, held), sems)
    sign_flip = jnp.where(low_lanes(), -1.0, 1.0)
    chunk = KEYS * PITCH // 5
    for copy in copies[:3]:
        copy.wait()
    for group in range(5):
        count = min(8, ROWS - 8 * group)
        flip = sign_flip[:count]
        keys = fourier_packed([arrived[pl.ds(ROWS * g + 8 * group, count), :] for g in range(SLABS)], -1.0, flip)
        for k1 in range(33):
            value = keys[k1 % 32]
            if k1:
                value = value * cos[k1 : k1 + 1, :] + pltpu.roll(value, 64, axis=1) * sin[k1 : k1 + 1, :]
            turned[pl.ds(PITCH * k1 + 8 * group, count), :] = value
    copies[3].wait()
    for n in range(5):
        rows = pl.ds(chunk * n, chunk)
        high, low = split(turned[rows, :])
        both = dot(high, pick[0]) + dot(low, pick[0]) + dot(high, pick[1])
        spec[0, rows, :] = both[:, :LANES]
        spec[1, rows, :] = both[:, LANES:]
    mirrored, upper, odd = params[0:1, :] > 0.5, params[1:2, :] > 0.5, params[2:3, :] > 0.5

    def choose(at, step):
        return jnp.where(
            odd if step else upper,
            jnp.where(mirrored, at(17), at(16)),
            jnp.where(mirrored, at(1), at(0)),
        )

    for part in range(2):
        for k1 in range(33):
            picked[part, k1] = choose(lambda off: spec[part, pl.ds(PITCH * k1 + off, 16), :], 0)
        for b in range(UB):
            cells[part, b] = choose(lambda off: picked[part, b + off], 1)
    resid[...] = jnp.zeros(resid.shape, F32)
    for copy in copies[4:]:
        copy.wait()

    def predict(a, carry):
        for top in range(0, VB, 64):
            rows = pl.ds(top, 64)
            total = [jnp.zeros((64, LANES), F32) for _ in range(2)]
            for b in range(UB):
                weight = weight_y[b, rows, :]
                for part in range(2):
                    total[part] = total[part] + weight * cells[part, b, pl.ds(a, 1), :]
            for part in range(2):
                resid[part, rows, :] += weight_x[a, rows, :] * total[part]
        return carry

    lax.fori_loop(0, UB, predict, 0)
    for part in range(2):
        resid[part] = data[2] * (data[part] - resid[part] * (1.0 / G))

    def spread(a, carry):
        for part in range(2):
            scaled = resid[part] * weight_x[a]
            for b in range(UB):
                cells[part, b, pl.ds(a, 1), :] = jnp.sum(scaled * weight_y[b], axis=0, keepdims=True)
        return carry

    lax.fori_loop(0, UB, spread, 0)
    padded[...] = jnp.zeros(padded.shape, F32)
    nothing = jnp.zeros((PITCH, LANES), F32)
    for part in range(2):
        for b in range(UB):
            padded[b, pl.ds(24, 16), :] = cells[part, b]
        for b in range(UB):
            wide[b] = choose(lambda off: padded[b, pl.ds(24 - off, PITCH), :], 0)
        for k1 in range(33):
            at = lambda off: wide[k1 - off] if 0 <= k1 - off < UB else nothing
            spec[part, pl.ds(PITCH * k1, PITCH), :] = choose(at, 1)
        spec[part, pl.ds(PITCH * 33, PITCH), :] = nothing
    for n in range(5):
        rows = pl.ds(chunk * n, chunk)
        high, low = split(jnp.concatenate([spec[0, rows, :], spec[1, rows, :]], axis=1))
        turned[rows, :] = dot(high, put[0]) + dot(low, put[0]) + dot(high, put[1])
    for group in range(5):
        count = min(8, ROWS - 8 * group)
        keys = []
        for k1 in range(33):
            value = turned[pl.ds(PITCH * k1 + 8 * group, count), :]
            if k1:
                value = value * cos[k1 : k1 + 1, :] - pltpu.roll(value, 64, axis=1) * sin[k1 : k1 + 1, :]
            keys.append(value)
        keys[0] = keys[0] + keys.pop()
        for g, value in enumerate(fourier_packed(keys, 1.0, sign_flip[:count])):
            out[pl.ds(ROWS * g + 8 * group, count), :] = value


def run_grid(arrived, weights, cos, sin):
    vmem, far = pltpu.VMEM, pl.ANY
    data, weight_y, weight_x, params, pick, put = weights
    sources = [params, cos, sin, pick, data, weight_y, weight_x, put]
    return call(
        grid_kernel,
        [jax.ShapeDtypeStruct((SLABS * ROWS, LANES), F32)],
        [pltpu.VMEM(source.shape, source.dtype) for source in sources]
        + [
            pltpu.VMEM((KEYS * PITCH, LANES), F32),
            pltpu.VMEM((2, KEYS * PITCH, LANES), F32),
            pltpu.VMEM((2, 33, UB, LANES), F32),
            pltpu.VMEM((2, UB, UB, LANES), F32),
            pltpu.VMEM((UB, 64, LANES), F32),
            pltpu.VMEM((UB, PITCH, LANES), F32),
            pltpu.VMEM((2, VB, LANES), F32),
            pltpu.SemaphoreType.DMA((8,)),
        ],
        [vmem] + [far] * 8,
        [vmem],
        1_000_000_000,
        5_000_000,
    )(arrived, *sources)[0]


def image_kernel(
    intersection, arrived, beam_far, back_far, cos_far, sin_far, out,
    step, image, beam, back, cos, sin, sems, *, groups,
):
    copies = start_copies([(cos_far, cos), (sin_far, sin), (back_far, back), (beam_far, beam)], sems)
    low_half = low_lanes()
    first_row = lax.broadcasted_iota(jnp.int32, (8, LANES), 0) == 0
    copies[0].wait()
    copies[1].wait()

    def extra(slab):
        return jnp.where(first_row, arrived[pl.ds(ROWS * slab + 32, 1), :], 0.0)

    for group in range(8):
        rho = pl.ds(8 * group, 8)
        values = []
        for u in range(16):
            if group < 4:
                packed = arrived[pl.ds(ROWS * u + 8 * group, 8), :]
                if group == 0 and u > 0:
                    packed = packed + extra(32 - u)
            else:
                packed = arrived[pl.ds(ROWS * (31 - u) + 8 * (group - 4), 8), :]
                if group == 4:
                    packed = packed + extra(u)
            crossed = pltpu.roll(packed, 64, axis=1)
            c, s = math.cos(2 * math.pi * u / 32), math.sin(2 * math.pi * u / 32)
            re = jnp.where(low_half, packed, crossed * c - packed * s)
            im = jnp.where(low_half, crossed, packed * c + crossed * s)
            if group == 0 and u == 0:
                packed = extra(16)
                crossed = pltpu.roll(packed, 64, axis=1)
                re = re + jnp.where(low_half, packed, -crossed)
                im = im + jnp.where(low_half, crossed, -packed)
            values.append((re, im))
        for kk, (re, im) in enumerate(fourier(values, 1.0)):
            c, s = cos[kk, rho, :], sin[kk, rho, :]
            step[kk, rho, :] = re * c - im * s
            step[kk, pl.ds(64 + 8 * group, 8), :] = re * s + im * c
    copies[2].wait()
    for kk in range(0, 16, 2):
        high, low = split(jnp.concatenate([step[kk], step[kk + 1]], axis=1))
        both = dot(back[...], jnp.concatenate([high, low, high], axis=0))
        image[pl.ds(kk, 64, stride=16), :] = both[:, :LANES]
        image[pl.ds(kk + 1, 64, stride=16), :] = both[:, LANES:]
    copies[3].wait()
    share = 32 // groups
    pitch = share + 1
    top, left = window_corner(intersection)
    mine = lax.axis_index("fft")
    lane = lax.broadcasted_iota(jnp.int32, (groups, LANES), 1)
    for i in range(SLABS):
        target = ((top + i) & 31) * pitch
        for n in range(share):
            rows = pl.ds(32 * i + n, groups, stride=share)
            out[pl.ds(target + n, groups, stride=SLABS * pitch), :] = image[rows, :] * beam[rows, :]
        home = ((top + i) >> 5) * 64 + left + mine
        out[pl.ds(target + share, groups, stride=SLABS * pitch), :] = (lane == home).astype(F32)


def run_image(intersection, arrived, beam, tables, groups):
    smem, vmem, far = pltpu.SMEM, pltpu.VMEM, pl.ANY
    _, back, cos, sin = tables

    def kernel(*refs):
        image_kernel(*refs, groups=groups)

    return call(
        kernel,
        [jax.ShapeDtypeStruct((groups * SLABS * (32 // groups + 1), LANES), F32)],
        [
            pltpu.VMEM((16, LANES, LANES), F32),
            pltpu.VMEM((1024, LANES), F32),
            pltpu.VMEM((1024, LANES), F32),
            pltpu.VMEM(back.shape, BF16),
            pltpu.VMEM(cos.shape, F32),
            pltpu.VMEM(sin.shape, F32),
            pltpu.SemaphoreType.DMA((4,)),
        ],
        [smem, vmem, far, far, far, far],
        [vmem],
        300_000_000,
        3_000_000,
    )(intersection, arrived, beam, back, cos, sin)[0]


def home_kernel(arrived, out, *, groups):
    share = 32 // groups
    count = groups * SLABS
    part = [arrived[pl.ds(n, count, stride=share + 1), :] for n in range(share + 1)]
    place = part[share].T.astype(BF16)
    for n in range(share):
        high, low = split(part[n])
        out[:, pl.ds(LANES * n, LANES)] = dot(place, high) + dot(place, low)


def run_home(arrived, groups):
    def kernel(*refs):
        home_kernel(*refs, groups=groups)

    return call(
        kernel,
        [jax.ShapeDtypeStruct((LANES, TS * TS // groups), F32)],
        [],
        [pltpu.VMEM],
        [pltpu.VMEM],
        60_000_000,
        1_000_000,
    )(arrived)[0]


def body(sky_model, intersection, beam, vis_data, vis_weight, vis_pos, uv_block, counts):
    groups = lax.axis_size("pt")

    def to_slabs(rows):
        return lax.all_to_all(rows.reshape(SLABS, -1), "fft", split_axis=0, concat_axis=0, tiled=True)

    tiles, own = run_send(intersection, counts, uv_block, sky_model, vis_data, vis_weight, vis_pos)
    arrived = to_slabs(tiles).reshape(SLABS, 32, LANES)
    other = lax.ppermute(own, "fft", [(n, SLABS - 1 - n) for n in range(SLABS)])
    col_tables, col_cos, col_sin = column_tables()
    row_parts = row_tables()
    packed_beam = beam.reshape(1024, LANES)
    rows_out = run_rows(intersection, arrived, packed_beam, other, row_parts)
    weights = run_weights(own, other, col_tables)
    rows_in = to_slabs(rows_out).reshape(SLABS * ROWS, LANES)
    grid_out = run_grid(rows_in, weights, col_cos, col_sin)
    grid_in = to_slabs(grid_out).reshape(SLABS * ROWS, LANES)
    images = run_image(intersection, grid_in, packed_beam, row_parts, groups)
    home = lax.all_to_all(
        images.reshape(groups * SLABS, -1), ("pt", "fft"), split_axis=0, concat_axis=0, tiled=True
    )
    return run_home(home.reshape(images.shape), groups)


def solution(mesh):
    in_specs = (
        P("fft", None),
        P("pt", None),
        P(None, "pt", "fft"),
        P(None, "pt", "fft", None),
        P("pt", "fft", None),
        P(None, "pt", "fft", None),
        P("pt", "fft"),
        P("pt", "fft"),
    )
    return jax.shard_map(body, mesh=mesh, in_specs=in_specs, out_specs=P("fft", "pt"), check_vma=False)
```

time: 207 us -> 154 us (0.74)
  the two profiles are of different devices: /device:TPU:38 before, /device:TPU:1 now
where the time goes in v2:
time: 154 us; the launch traced here: 153 us
  blocking collectives  66.6 us (43%)
  waiting for transfers between devices  29.2 us (19%)
  starting transfers between devices  23.7 us (15%)
  Pallas kernels  20.3 us (13%)
  local copies, waits for them, and re-layouts  12.6 us (8%)
    all_to_all x1, blocking collectives, body(): lax.all_to_all(images.reshape(groups * SLABS, -1), ('pt', 'fft'), split_a...  43.8 us
    all_to_all x1, blocking collectives, to_slabs(): lax.all_to_all(rows.reshape(SLABS, -1), 'fft', split_axis=0, concat_axis=...  22.8 us
    all_to_all x2, starting transfers between devices, to_slabs(): lax.all_to_all(rows.reshape(SLABS, -1), 'fft', split_axis=0, concat_axis=...  16.5 us
    ppermute x1, waiting for transfers between devices, body(): other = lax.ppermute(own, 'fft', [(n, SLABS - 1 - n) for n in range(SLABS)])  15.7 us
    all_to_all x2, waiting for transfers between devices, to_slabs(): lax.all_to_all(rows.reshape(SLABS, -1), 'fft', split_axis=0, concat_axis=...  13.5 us
    unnamed x41, local copies, waits for them, and re-layouts  11.2 us
    pallas_call x1, Pallas kernels, run_grid(): call(grid_kernel, [jax.ShapeDtypeStruct((SLABS * ROWS, LANES), F32)], [pl...  9.82 us
    ppermute x1, starting transfers between devices, body(): other = lax.ppermute(own, 'fft', [(n, SLABS - 1 - n) for n in range(SLABS)])  7.24 us
  transfers between devices with their start and end apart: 3, of which 2 were waited for; matrix products, arithmetic and copies ran while one was open for 2% of the time, Pallas kernels for 1%

profile of v2, /device:TPU:1, one launch (start us, length us, event | category | flops | bytes accessed | tf_op | source)
XLA Modules:
  0.0 153.3 jit_solution(9295603537456195357)
XLA Ops:
  0.7 0.0 copy-start
  0.7 1.6 %copy-done = f32[128,4096]{1,0:T(8,128)S(1)} copy-done((f32[128,4096]{1,0:T(8,128)S(1)}, f32[128,4096]{1,0:T(8,128)}, u32[]{:S(2)}) %copy-start) | copy-done | bytes 2097176
  2.2 0.0 copy-start.4
  2.2 0.8 copy-done.4
  3.1 0.0 copy-start.5
  3.1 0.8 copy-done.5
  3.9 0.0 copy-start.9
  3.9 0.7 copy-done.9
  4.6 0.0 copy-start.11
  4.6 0.8 copy-done.11
  5.4 0.0 copy-start.12
  5.4 0.7 copy-done.12
  6.0 0.0 copy-start.19
  6.0 2.4 %shard_map.154 = (f32[1024,128]{1,0:T(8,128)}, f32[6,64,128]{2,1,0:T(8,128)S(1)}) custom-call(s32[1,1024]{1,0:T(1,128)S(1)} %copy-done.9, s32[1,1]{1,0:T(1,128)S(6)} %copy.24.counts, s32[1,64]{1,0:T(1,128)S(1)} %copy-done.12, f32[128,4096]{1,0:T(8,128)S(1)} %copy-done, f32[2,1,64,128]{3,2,1,0:T(8,128)S(1)} %copy-done.4, f32[1,64,128]{2,1,0:T(8,128)S(1)} %copy-done.11, ...), custom_call_target="tpu_custom_call" | custom-call | flops 1000000 | bytes 2000000 | tf_op jit(solution)/shard_map/pallas_call | solution.py:183
  8.5 0.0 copy-start.1
  8.5 0.0 copy-start.2
  8.5 0.0 copy-start.7
  8.5 0.0 copy-start.10
  8.5 11.4 %all-to-all-start = ((f32[32,1,4096]{2,1,0:T(1,128)}), f32[32,1,4096]{2,1,0:T(1,128)S(1)}, u32[]{:S(2)}, u32[]{:S(2)}) async-start(f32[32,1,4096]{2,1,0:T(1,128)} %bitcast), calls=%async_computation | async-start | bytes 1048576 | tf_op jit(solution)/shard_map/all_to_all | solution.py:596
  19.9 7.2 %collective-permute-start = (f32[6,64,128]{2,1,0:T(8,128)S(1)}, f32[6,64,128]{2,1,0:T(8,128)S(1)}, u32[]{:S(2)}, u32[]{:S(2)}) collective-permute-start(f32[6,64,128]{2,1,0:T(8,128)S(1)} %get-tuple-element.14.own_far), channel_id=1, source_target_pairs={{0,31},{1,30},{2,29},{3,28},{4,27},{5,26},{6,25},{7,24},{8,23},{9,... | collective-permute-start | bytes 589832 | tf_op jit(solution)/shard_map/ppermute | solution.py:600
  27.1 0.0 copy-done.19
  27.1 1.4 copy.20
  28.5 1.4 reshape.36.beam.refs_2_
  29.9 0.0 copy-start.3
  29.9 0.0 copy-start.6
  29.9 15.7 %collective-permute-done.other.other_far = f32[6,64,128]{2,1,0:T(8,128)S(1)} collective-permute-done((f32[6,64,128]{2,1,0:T(8,128)S(1)}, f32[6,64,128]{2,1,0:T(8,128)S(1)}, u32[]{:S(2)}, u32[]{:S(2)}) %collective-permute-start) | collective-permute-done | bytes 196640 | tf_op jit(solution)/shard_map/ppermute | solution.py:600
  45.7 0.0 all-to-all-done
  45.7 0.0 copy-done.1
  45.7 0.0 copy-done.2
  45.7 0.0 copy-done.7
  45.7 0.0 copy-done.10
  45.7 0.0 copy-start.17
  45.7 0.0 copy-start.18
  45.7 2.5 %shard_map.155 = f32[1056,128]{1,0:T(8,128)} custom-call(s32[1,1024]{1,0:T(1,128)S(1)} %copy-done.10, f32[32,32,128]{2,1,0:T(8,128)S(1)} %bitcast.13, f32[1024,128]{1,0:T(8,128)S(1)} %reshape.36.beam.refs_2_, bf16[128,192]{1,0:T(8,128)(2,1)S(1)} %copy-done.7, f32[16,64,128]{2,1,0:T(8,128)S(1)} %copy-done.2, f32[16,64,128]{2,1,0:T(8,128)S(1)} %copy-done.1, ...), custom_call_target="tpu_custom_call" | custom-call | flops 300000000 | bytes 3000000 | tf_op jit(solution)/shard_map/pallas_call | solution.py:256
  48.2 5.1 %all-to-all-start.1 = ((f32[32,1,4224]{2,1,0:T(1,128)}), f32[32,1,4224]{2,1,0:T(1,128)S(1)}, u32[]{:S(2)}, u32[]{:S(2)}) async-start(f32[32,1,4224]{2,1,0:T(1,128)} %bitcast.2), calls=%async_computation.1 | async-start | bytes 1081344 | tf_op jit(solution)/shard_map/all_to_all | solution.py:596
  53.4 0.0 copy-done.3
  53.4 0.0 copy-done.6
  53.4 2.1 %shard_map.156 = (f32[3,128,128]{2,1,0:T(8,128)S(1)}, f32[16,128,128]{2,1,0:T(8,128)S(1)}, f32[16,128,128]{2,1,0:T(8,128)S(1)}, f32[8,128]{1,0:T(8,128)S(1)}, bf...) custom-call(f32[6,64,128]{2,1,0:T(8,128)S(1)} %get-tuple-element.14.own_far, ...), custom_call_target="tpu_custom_call" | custom-call | flops 20000000 | bytes 3000000 | tf_op jit(solution)/shard_map/pallas_call | solution.py:343
  55.5 0.0 copy-start.13
  55.5 1.0 copy-done.13
  56.5 0.0 copy-start.15
  56.5 1.0 copy-done.15
  57.5 13.5 %all-to-all-done.1 = f32[32,1,4224]{2,1,0:T(1,128)S(1)} async-done(((f32[32,1,4224]{2,1,0:T(1,128)}), f32[32,1,4224]{2,1,0:T(1,128)S(1)}, u32[]{:S(2)}, u32[]{:S(2)}) %all-to-all-start.1) | async-done | bytes 540704 | tf_op jit(solution)/shard_map/all_to_all | solution.py:596
  71.0 0.0 copy-done.17
  71.0 0.0 copy-done.18
  71.0 0.0 copy-start.14
  71.0 1.2 copy-done.14
  72.2 0.0 copy-start.16
  72.2 1.2 copy-done.16
  73.4 0.0 copy-start.8
  73.4 9.8 %shard_map.157 = f32[1056,128]{1,0:T(8,128)S(1)} custom-call(f32[1056,128]{1,0:T(8,128)S(1)} %bitcast.14, f32[8,128]{1,0:T(8,128)S(1)} %get-tuple-element.15.refs_0_, f32[40,128]{1,0:T(8,128)S(1)} %copy-done.18, f32[40,128]{1,0:T(8,128)S(1)} %copy-done.17, bf16[2,128,256]{2,1,0:T(8,128)(2,1)S(1)} %get-tuple-element.16.refs_3_, ...), custom_call_target="tpu_custom_call" | custom-call | flops 1000000000 | bytes 5000000 | tf_op jit(solution)/shard_map/pallas_call | solution.py:460
  83.2 22.8 %all_to_all.36 = f32[32,1,4224]{2,1,0:T(1,128)S(1)} all-to-all(f32[32,1,4224]{2,1,0:T(1,128)S(1)} %bitcast.15), channel_id=1, replica_groups=mesh['pt'=16,'fft'=32] {'fft'}, dimensions={0} | all-to-all | bytes 1081344 | tf_op jit(solution)/shard_map/all_to_all | solution.py:596
  106.1 0.0 copy-done.8
  106.1 2.4 %shard_map.158 = f32[1536,128]{1,0:T(8,128)S(1)} custom-call(s32[1,1024]{1,0:T(1,128)S(1)} %copy-done.10, f32[1056,128]{1,0:T(8,128)S(1)} %bitcast.12, f32[1024,128]{1,0:T(8,128)S(1)} %reshape.36.beam.refs_2_, bf16[64,384]{1,0:T(8,128)(2,1)S(1)} %copy-done.8, f32[16,64,128]{2,1,0:T(8,128)S(1)} %copy-done.2, f32[16,64,128]{2,1,0:T(8,128)S(1)} %copy-done.1), custom_call_target="tpu_custom_call" | custom-call | flops 300000000 | bytes 3000000 | tf_op jit(solution)/shard_map/pallas_call | solution.py:548
  108.5 43.8 %all_to_all.37 = f32[512,1,384]{2,1,0:T(1,128)S(1)} all-to-all(f32[512,1,384]{2,1,0:T(1,128)S(1)} %bitcast.11), channel_id=1, replica_groups=mesh['pt'=16,'fft'=32] {'pt','fft'}, dimensions={0} | all-to-all | bytes 1572864 | tf_op jit(solution)/shard_map/all_to_all | solution.py:610
  152.3 1.0 shard_map.159
Async XLA Ops:
  0.7 1.6 %copy-start = (f32[128,4096]{1,0:T(8,128)S(1)}, f32[128,4096]{1,0:T(8,128)}, u32[]{:S(2)}) copy-start(f32[128,4096]{1,0:T(8,128)} %sky.1) | copy-start | bytes 6291460
  2.2 0.8 copy-start.4
  3.1 0.8 copy-start.5
  3.9 0.7 copy-start.9
  4.6 0.8 copy-start.11
  5.4 0.7 copy-start.12
  6.0 21.1 %copy-start.19 = (f32[2048,1,64]{0,2,1:T(8,128)S(1)}, f32[2048,1,64]{0,2,1:T(8,128)}, u32[]{:S(2)}) copy-start(f32[2048,1,64]{0,2,1:T(8,128)} %param.18) | copy-start | bytes 1572868
  8.5 37.2 %copy-start.1 = (f32[16,64,128]{2,1,0:T(8,128)S(1)}, f32[16,64,128]{2,1,0:T(8,128)}, u32[]{:S(2)}) copy-start(f32[16,64,128]{2,1,0:T(8,128)} %constant.18.clone.sin_far.refs_5_) | copy-start | bytes 1572868
  8.5 37.2 %copy-start.2 = (f32[16,64,128]{2,1,0:T(8,128)S(1)}, f32[16,64,128]{2,1,0:T(8,128)}, u32[]{:S(2)}) copy-start(f32[16,64,128]{2,1,0:T(8,128)} %constant.17.clone.cos_far.refs_4_) | copy-start | bytes 1572868
  8.5 37.2 %copy-start.7 = (bf16[128,192]{1,0:T(8,128)(2,1)S(1)}, bf16[128,192]{1,0:T(8,128)(2,1)}, u32[]{:S(2)}) copy-start(bf16[128,192]{1,0:T(8,128)(2,1)} %constant.16.clone.forward_far) | copy-start | bytes 147460
  8.5 37.2 %copy-start.10 = (s32[1,1024]{1,0:T(1,128)S(1)}, s32[1,1024]{1,0:T(1,128)}, u32[]{:S(2)}) copy-start(s32[1,1024]{1,0:T(1,128)} %refs_0_.1) | copy-start | bytes 12292
  8.5 37.2 %all-to-all-start = ((f32[32,1,4096]{2,1,0:T(1,128)}), f32[32,1,4096]{2,1,0:T(1,128)S(1)}, u32[]{:S(2)}, u32[]{:S(2)}) async-start(f32[32,1,4096]{2,1,0:T(1,128)} %bitcast), calls=%async_computation | async-start | bytes 1048576 | tf_op jit(solution)/shard_map/all_to_all | solution.py:596
  19.9 25.8 %collective-permute-start = (f32[6,64,128]{2,1,0:T(8,128)S(1)}, f32[6,64,128]{2,1,0:T(8,128)S(1)}, u32[]{:S(2)}, u32[]{:S(2)}) collective-permute-start(f32[6,64,128]{2,1,0:T(8,128)S(1)} %get-tuple-element.14.own_far), channel_id=1, source_target_pairs={{0,31},{1,30},{2,29},{3,28},{4,27},{5,26},{6,25},{7,24},{8,23},{9,... | collective-permute-start | bytes 589832 | tf_op jit(solution)/shard_map/ppermute | solution.py:600
  29.9 23.5 %copy-start.3 = (bf16[2,2,128,64]{3,2,1,0:T(8,128)(2,1)S(1)}, bf16[2,2,128,64]{3,2,1,0:T(8,128)(2,1)}, u32[]{:S(2)}) copy-start(bf16[2,2,128,64]{3,2,1,0:T(8,128)(2,1)} %constant.19.clone.picks_far) | copy-start | bytes 196612
  29.9 23.5 %copy-start.6 = (bf16[2,2,64,128]{3,2,1,0:T(8,128)(2,1)S(1)}, bf16[2,2,64,128]{3,2,1,0:T(8,128)(2,1)}, u32[]{:S(2)}) copy-start(bf16[2,2,64,128]{3,2,1,0:T(8,128)(2,1)} %constant.20.clone.puts_far) | copy-start | bytes 196612
  45.7 25.3 %copy-start.17 = (f32[40,128]{1,0:T(8,128)S(1)}, f32[40,128]{1,0:T(8,128)}, u32[]{:S(2)}) copy-start(f32[40,128]{1,0:T(8,128)} %constant.22.clone.refs_2_) | copy-start | bytes 61444
  45.7 25.3 %copy-start.18 = (f32[40,128]{1,0:T(8,128)S(1)}, f32[40,128]{1,0:T(8,128)}, u32[]{:S(2)}) copy-start(f32[40,128]{1,0:T(8,128)} %constant.21.clone.refs_1_) | copy-start | bytes 61444
  48.2 22.7 %all-to-all-start.1 = ((f32[32,1,4224]{2,1,0:T(1,128)}), f32[32,1,4224]{2,1,0:T(1,128)S(1)}, u32[]{:S(2)}, u32[]{:S(2)}) async-start(f32[32,1,4224]{2,1,0:T(1,128)} %bitcast.2), calls=%async_computation.1 | async-start | bytes 1081344 | tf_op jit(solution)/shard_map/all_to_all | solution.py:596
  55.5 1.0 copy-start.13
  56.5 1.0 copy-start.15
  71.0 1.2 copy-start.14
  72.2 1.2 copy-start.16
  73.4 32.7 %copy-start.8 = (bf16[64,384]{1,0:T(8,128)(2,1)S(1)}, bf16[64,384]{1,0:T(8,128)(2,1)}, u32[]{:S(2)}) copy-start(bf16[64,384]{1,0:T(8,128)(2,1)} %constant.23.clone.refs_3_) | copy-start | bytes 147460

commit v3 on v2

v3 whole, which is shorter than its diff:
```python
import math

import jax
import jax.numpy as jnp
import numpy as np
from jax import lax
from jax.experimental import pallas as pl
from jax.experimental.pallas import tpu as pltpu
from jax.sharding import PartitionSpec as P

G = 2048
TS = 64
UB = 16
VB = 128
NB = 64
SLABS = 32
HALF = 16
ROWS = 33
BACK_ROWS = 34
PITCH = 40
KEYS = 34
LANES = 128
INTERPRET = False

F32 = jnp.float32
BF16 = jnp.bfloat16


def split_np(table):
    high = np.asarray(table, np.float32).astype(jnp.bfloat16)
    low = (np.asarray(table, np.float64) - high.astype(np.float64)).astype(jnp.bfloat16)
    return high, low


def split(value):
    high = value.astype(BF16)
    return high, (value - high.astype(F32)).astype(BF16)


def dot(left, right):
    return jnp.dot(left, right, preferred_element_type=F32)


PREP_BASE = 1024
PREP_STEP = PREP_BASE + 128
PREP_FORWARD = PREP_STEP + 128
PREP_BACK = PREP_FORWARD + 128
PREP_ROWS = PREP_BACK + 64


def row_tables():
    rho, x1 = np.arange(64)[:, None], np.arange(64)[None, :]
    angle = 2 * np.pi * (rho * x1 % 64) / 64
    forward = np.zeros((128, LANES))
    forward[:, :64] = np.concatenate([np.cos(angle), -np.sin(angle)], 0)
    back = np.concatenate([np.cos(angle).T, -np.sin(angle).T], 1) / G
    par = (np.arange(LANES) >= 64)[None, None, :]
    top = np.arange(SLABS)[:, None, None]
    rho = rho[None]
    base = 2 * np.pi * ((rho * par - 64 * rho * top) % G) / G
    base = np.concatenate([np.cos(base), np.sin(base)], 1)
    step = 2 * np.pi * 2 * rho[0] * np.ones((1, LANES)) / G
    fixed = np.concatenate([np.cos(step), np.sin(step), forward, back], 0)
    return base.astype(np.float32), fixed.astype(np.float32)


def prepare(intersection, beam):
    base, fixed = row_tables()
    corner = intersection[0, 0]
    top = (corner >> 7) & 31
    tiles = beam.reshape(SLABS, 32, LANES)
    turned = lax.dynamic_slice(jnp.concatenate([tiles, tiles]), ((SLABS - top) & 31, 0, 0), tiles.shape)
    phases = lax.dynamic_slice(base, (top, 0, 0), (1, 128, LANES))[0]
    return jnp.concatenate([turned.reshape(1024, LANES), phases, fixed])


def twists(prep, rho):
    c, s = prep[pl.ds(PREP_BASE + rho, 8), :], prep[pl.ds(PREP_BASE + 64 + rho, 8), :]
    step_c, step_s = prep[pl.ds(PREP_STEP + rho, 8), :], prep[pl.ds(PREP_STEP + 64 + rho, 8), :]
    found = []
    for _ in range(16):
        found.append((c, s))
        c, s = c * step_c - s * step_s, s * step_c + c * step_s
    return found


def column_tables():
    cols, keys = np.arange(64)[:, None], np.arange(64)[None, :]
    angle = 2 * np.pi * (cols * keys % 64) / 64
    first = np.concatenate([np.cos(angle), np.sin(angle)], 0)
    second = np.concatenate([-np.sin(angle), np.cos(angle)], 0)
    pick = [np.stack(split_np(table)) for table in (first, second)]
    put = [np.stack(split_np(table.T)) for table in (first, second)]
    tables = np.stack(pick), np.stack(put)
    k1 = np.arange(PITCH)[:, None]
    lane = np.arange(LANES)[None, :]
    twist = 2 * np.pi * (k1 * (lane % 64)) / G
    cos = np.cos(twist).astype(np.float32)
    sin = (np.sin(twist) * np.where(lane < 64, 1.0, -1.0)).astype(np.float32)
    return tables, cos, sin


def turn(re, im, angle):
    c, s = math.cos(angle), math.sin(angle)
    if abs(s) < 1e-12:
        return (re, im) if c > 0 else (-re, -im)
    if abs(c) < 1e-12:
        return (-im, re) if s > 0 else (im, -re)
    return re * c - im * s, re * s + im * c


def fourier(values, sign):
    count = len(values)
    if count == 1:
        return values
    even, odd = fourier(values[::2], sign), fourier(values[1::2], sign)
    out = [None] * count
    for k in range(count // 2):
        re, im = turn(*odd[k], sign * 2 * math.pi * k / count)
        out[k] = (even[k][0] + re, even[k][1] + im)
        out[k + count // 2] = (even[k][0] - re, even[k][1] - im)
    return out


def fourier_packed(values, sign, flip):
    count = len(values)
    if count == 1:
        return values
    even, odd = fourier_packed(values[::2], sign, flip), fourier_packed(values[1::2], sign, flip)
    out = [None] * count
    for k in range(count // 2):
        angle = sign * 2 * math.pi * k / count
        c, s = math.cos(angle), math.sin(angle)
        value = odd[k]
        if k:
            crossed = pltpu.roll(value, 64, axis=1) * (flip * s)
            value = crossed if abs(c) < 1e-12 else value * c + crossed
        out[k] = even[k] + value
        out[k + count // 2] = even[k] - value
    return out


def call(kernel, out_shape, scratch, spaces, out_spaces, flops, data, grant=24):
    return pl.pallas_call(
        kernel,
        out_shape=out_shape,
        in_specs=[pl.BlockSpec(memory_space=space) for space in spaces],
        out_specs=[pl.BlockSpec(memory_space=space) for space in out_spaces],
        scratch_shapes=scratch,
        compiler_params=pltpu.CompilerParams(vmem_limit_bytes=grant * 1024 * 1024),
        cost_estimate=pl.CostEstimate(flops=flops, bytes_accessed=data, transcendentals=0),
        interpret=INTERPRET,
    )


def start_copies(pairs, sems):
    copies = [pltpu.make_async_copy(src, dst, sems.at[n]) for n, (src, dst) in enumerate(pairs)]
    for copy in copies:
        copy.start()
    return copies


def window_corner(intersection):
    corner = intersection[0, 0]
    return (corner >> 7) + ((corner >> 6) & 1) * 32, corner & 63


def low_lanes():
    return lax.broadcasted_iota(jnp.int32, (8, LANES), 1) < 64


def send_kernel(
    intersection_far, counts_far, names_far, sky, vis_data, vis_weight, vis_pos, tiles, own_far,
    intersection, counts, names, sky_rows, weight, own, turned, sems,
):
    corner_in = pltpu.make_async_copy(intersection_far.at[:, pl.ds(0, LANES)], intersection, sems.at[0])
    corner_in.start()
    copies = start_copies(
        [
            (vis_weight.at[0], weight),
            (vis_data.at[0, 0], own.at[pl.ds(0, NB)]),
            (vis_data.at[1, 0], own.at[pl.ds(NB, NB)]),
            (vis_pos.at[0, 0], own.at[pl.ds(3 * NB, NB)]),
            (vis_pos.at[1, 0], own.at[pl.ds(4 * NB, NB)]),
            (counts_far, counts),
            (names_far, names),
        ],
        sems.at[pl.ds(2, 7)],
    )
    corner_in.wait()
    top, left = window_corner(intersection)
    mine = lax.axis_index("fft")
    row = top + ((mine - top) & 31)
    start = (row >> 5) * 64 + left
    first = jnp.minimum(start >> 3, 11) * 8
    sky_in = pltpu.make_async_copy(sky.at[pl.ds(pl.multiple_of(first, 8), 40), :], sky_rows, sems.at[1])
    sky_in.start()
    for copy in copies:
        copy.wait()
    used = lax.broadcasted_iota(jnp.int32, (NB, VB), 0) < counts[0, 0]
    own[pl.ds(2 * NB, NB), :] = jnp.where(used, weight[...], 0.0)
    own[pl.ds(5 * NB, 8), :] = jnp.zeros((8, VB), F32)
    own[pl.ds(5 * NB, 1), pl.ds(0, NB)] = names[...].astype(F32)
    own_out = pltpu.make_async_copy(own, own_far, sems.at[2])
    own_out.start()
    shift = 16 - (start - first)
    sky_in.wait()
    sent = []
    for part in range(4):
        for n in range(32):
            rows = pltpu.roll(sky_rows[8 * part : 8 * part + 16, LANES * n : LANES * (n + 1)], shift, axis=0)
            turned[pl.ds(256 * part + n, 8, stride=32), :] = rows[:8]
        rows = pl.ds(256 * part, 256)
        sent.append(pltpu.make_async_copy(turned.at[rows], tiles.at[rows], sems.at[3 + part]))
        sent[-1].start()
    for copy in sent:
        copy.wait()
    own_out.wait()


def run_send(intersection, counts, names, sky, vis_data, vis_weight, vis_pos):
    far = pltpu.HBM
    shape = jax.ShapeDtypeStruct
    return call(
        send_kernel,
        [shape((1024, LANES), F32), shape((5 * NB + 8, VB), F32)],
        [
            pltpu.SMEM((1, LANES), jnp.int32),
            pltpu.SMEM((1, 1), jnp.int32),
            pltpu.VMEM((1, NB), jnp.int32),
            pltpu.VMEM((40, TS * TS), F32),
            pltpu.VMEM((NB, VB), F32),
            pltpu.VMEM((5 * NB + 8, VB), F32),
            pltpu.VMEM((1024, LANES), F32),
            pltpu.SemaphoreType.DMA((9,)),
        ],
        [far] * 7,
        [far, far],
        1_000_000,
        2_000_000,
        60,
    )(intersection, counts, names, sky, vis_data, vis_weight, vis_pos)


def rows_kernel(
    arrived, prep, other, out, image, step, message, sems,
):
    del other
    for f in range(SLABS):
        image[pl.ds(32 * f, 32), :] = arrived[f] * prep[pl.ds(32 * f, 32), :]
    forward = split(prep[pl.ds(PREP_FORWARD, 128), :][:, :64])
    forward = jnp.concatenate([forward[0], forward[0], forward[1]], axis=1)
    for kk in range(0, 16, 2):
        data = jnp.concatenate([image[pl.ds(kk + n, 64, stride=16), :] for n in range(2)], axis=1)
        high, low = split(data)
        both = dot(forward, jnp.concatenate([high, low, high], axis=0))
        step[kk] = both[:, :LANES]
        step[kk + 1] = both[:, LANES:]
    low_half = low_lanes()
    sent = []
    for group in (4, 5, 6, 7, 0, 1, 2, 3):
        rho = pl.ds(8 * group, 8)
        values = []
        for kk, (c, s) in enumerate(twists(prep, 8 * group)):
            re, im = step[kk, rho, :], step[kk, pl.ds(64 + 8 * group, 8), :]
            values.append((re * c + im * s, im * c - re * s))
        spread = fourier(values, -1.0)
        for u in range(17 if group == 0 else 16):
            re, im = spread[u % 16]
            angle = 2 * math.pi * u / 32
            c = jnp.where(low_half, 1.0, math.cos(angle))
            s = jnp.where(low_half, 0.0, math.sin(angle))
            first, second = re * c + im * s, im * c - re * s
            packed = jnp.where(low_half, first, pltpu.roll(second, 64, axis=1)) + jnp.where(
                low_half, pltpu.roll(first, 64, axis=1), second
            )
            if group >= 4:
                message[pl.ds(ROWS * (31 - u) + 8 * (group - 4), 8), :] = packed
            elif u < 16:
                message[pl.ds(ROWS * u + 8 * group, 8), :] = packed
            if group == 4:
                message[pl.ds(ROWS * u + 32, 1), :] = packed[:1]
            if group == 0 and u > 0:
                message[pl.ds(ROWS * (32 - u) + 32, 1), :] = packed[:1]
        if group in (0, 3):
            rows = pl.ds(16 * ROWS if group == 0 else 0, 16 * ROWS)
            sent.append(pltpu.make_async_copy(message.at[rows], out.at[rows], sems.at[len(sent)]))
            sent[-1].start()
    for copy in sent:
        copy.wait()


def run_rows(arrived, prep, other):
    vmem, far = pltpu.VMEM, pltpu.HBM
    return call(
        rows_kernel,
        [jax.ShapeDtypeStruct((SLABS * ROWS, LANES), F32)],
        [
            pltpu.VMEM((1024, LANES), F32),
            pltpu.VMEM((16, LANES, LANES), F32),
            pltpu.VMEM((SLABS * ROWS, LANES), F32),
            pltpu.SemaphoreType.DMA((2,)),
        ],
        [vmem, vmem, far],
        [far],
        300_000_000,
        3_000_000,
    )(arrived, prep, other)[0]


AT_Y = 3 * VB
AT_X = AT_Y + UB * VB
AT_FLAGS = AT_X + UB * VB
AT_PICK = AT_FLAGS + 8
AT_PUT = AT_PICK + 2 * LANES
HELD_ROWS = AT_PUT + 2 * LANES
HELD_SPACE = 32768


def weights_kernel(own_far, other_far, picks_far, puts_far, held_far, own, other, picks, puts, out, sems):
    copies = start_copies([(own_far, own), (other_far, other), (picks_far, picks), (puts_far, puts)], sems)
    mine = lax.axis_index("fft")
    half = mine >> 4
    u = jnp.where(half == 0, mine, SLABS - 1 - mine)
    for copy in copies:
        copy.wait()
    lower = half == 0
    lane = lax.broadcasted_iota(jnp.int32, (1, LANES), 1)
    mirrored = lane >= 64

    def stacked(index):
        rows = pl.ds(NB * index, NB)
        mine, theirs = own[rows, :], other[rows, :]
        return jnp.concatenate([jnp.where(lower, mine, theirs), jnp.where(lower, theirs, mine)], axis=0)

    def block_parts(names, is_mirrored):
        local = names.astype(jnp.int32) - jnp.where(is_mirrored, 31 - u, u) * 512
        band, column = local >> 7, local & 127
        column = jnp.where(is_mirrored, 127 - column, column)
        side = jnp.where(is_mirrored, 1 - (band & 1), band & 1)
        kept = jnp.where(is_mirrored, 1 - (band >> 1), band >> 1) == half
        return column, side, kept

    mine, theirs = own[pl.ds(5 * NB, 1), :], other[pl.ds(5 * NB, 1), :]
    direct, turned = jnp.where(lower, mine, theirs), jnp.where(lower, theirs, mine)
    named = jnp.where(mirrored, pltpu.roll(turned, 64, axis=1), direct)
    down = lax.broadcasted_iota(jnp.int32, (LANES, 64), 0)
    column, _, _ = block_parts(jnp.broadcast_to(named, (LANES, LANES)).T[:, :64], down >= 64)
    across = lax.broadcasted_iota(jnp.int32, (LANES, 64), 1)
    chosen = (across == (column >> 1)).astype(F32).astype(BF16)
    column, side, kept = block_parts(named, mirrored)
    down = lax.broadcasted_iota(jnp.int32, (64, LANES), 0)
    chosen_t = (down == (column >> 1)).astype(F32).astype(BF16)
    for n in range(2):
        out[pl.ds(AT_PICK + LANES * n, LANES), :] = dot(picks[n, 0], chosen_t) + dot(picks[n, 1], chosen_t)
        out[pl.ds(AT_PUT + LANES * n, LANES), :] = dot(chosen, puts[n, 0]) + dot(chosen, puts[n, 1])
    out[pl.ds(AT_FLAGS, 8), :] = jnp.zeros((8, LANES), F32)
    out[pl.ds(AT_FLAGS, 1), :] = mirrored.astype(F32)
    out[pl.ds(AT_FLAGS + 1, 1), :] = side.astype(F32)
    out[pl.ds(AT_FLAGS + 2, 1), :] = (column & 1).astype(F32)
    out[pl.ds(0, VB), :] = stacked(0).T
    out[pl.ds(VB, VB), :] = stacked(1).T * jnp.where(mirrored, -1.0, 1.0)
    out[pl.ds(2 * VB, VB), :] = stacked(2).T * kept.astype(F32)
    for at, index in ((AT_Y, 3), (AT_X, 4)):
        position = stacked(index).T
        position = jnp.where(mirrored, 15.0 - position, position)
        for n in range(UB):
            away = float(n) - position
            out[pl.ds(at + VB * n, VB), :] = jnp.exp(away * away * (-1.0 / 8.0))
    copy = pltpu.make_async_copy(out, held_far.at[pl.ds(0, HELD_ROWS)], sems.at[0])
    copy.start()
    copy.wait()


def run_weights(own, other, tables):
    far = pltpu.HBM
    picks, puts = tables
    return call(
        weights_kernel,
        [jax.ShapeDtypeStruct((HELD_SPACE, LANES), F32)],
        [
            pltpu.VMEM(own.shape, F32),
            pltpu.VMEM(own.shape, F32),
            pltpu.VMEM(picks.shape, BF16),
            pltpu.VMEM(puts.shape, BF16),
            pltpu.VMEM((HELD_ROWS, LANES), F32),
            pltpu.SemaphoreType.DMA((4,)),
        ],
        [far] * 4,
        [far],
        20_000_000,
        3_000_000,
        60,
    )(own, other, picks, puts)[0]


def grid_kernel(
    arrived, cos, sin, corner, held_far, out, held, turned, spec, picked, cells, padded, wide, resid, sems,
):
    copies = start_copies(
        [(held_far.at[rows], held.at[rows]) for rows in (pl.ds(AT_FLAGS, HELD_ROWS - AT_FLAGS), pl.ds(0, AT_FLAGS))],
        sems,
    )
    sign_flip = jnp.where(low_lanes(), -1.0, 1.0)
    chunk = KEYS * PITCH // 5
    for group in range(5):
        count = min(8, ROWS - 8 * group)
        flip = sign_flip[:count]
        keys = fourier_packed([arrived[pl.ds(ROWS * g + 8 * group, count), :] for g in range(SLABS)], -1.0, flip)
        for k1 in range(33):
            value = keys[k1 % 32]
            if k1:
                value = value * cos[k1 : k1 + 1, :] + pltpu.roll(value, 64, axis=1) * sin[k1 : k1 + 1, :]
            turned[pl.ds(PITCH * k1 + 8 * group, count), :] = value
    copies[0].wait()
    pick_high, pick_low = split(
        jnp.concatenate([held[pl.ds(AT_PICK, LANES), :], held[pl.ds(AT_PICK + LANES, LANES), :]], axis=1)
    )
    for n in range(5):
        rows = pl.ds(chunk * n, chunk)
        high, low = split(turned[rows, :])
        both = dot(high, pick_high) + dot(low, pick_high) + dot(high, pick_low)
        spec[0, rows, :] = both[:, :LANES]
        spec[1, rows, :] = both[:, LANES:]
    mirrored, upper, odd = [held[pl.ds(AT_FLAGS + n, 1), :] > 0.5 for n in range(3)]

    def choose(at, step):
        return jnp.where(
            odd if step else upper,
            jnp.where(mirrored, at(17), at(16)),
            jnp.where(mirrored, at(1), at(0)),
        )

    for part in range(2):
        for k1 in range(33):
            picked[part, k1] = choose(lambda off: spec[part, pl.ds(PITCH * k1 + off, 16), :], 0)
        for b in range(UB):
            cells[part, b] = choose(lambda off: picked[part, b + off], 1)
    resid[...] = jnp.zeros(resid.shape, F32)
    copies[1].wait()

    def predict(a, carry):
        for top in range(0, VB, 64):
            rows = pl.ds(top, 64)
            total = [jnp.zeros((64, LANES), F32) for _ in range(2)]
            for b in range(UB):
                weight = held[pl.ds(AT_Y + VB * b + top, 64), :]
                for part in range(2):
                    total[part] = total[part] + weight * cells[part, b, pl.ds(a, 1), :]
            for part in range(2):
                resid[part, rows, :] += held[pl.ds(pl.multiple_of(AT_X + VB * a + top, 8), 64), :] * total[part]
        return carry

    lax.fori_loop(0, UB, predict, 0)
    for part in range(2):
        resid[part] = held[pl.ds(2 * VB, VB), :] * (held[pl.ds(VB * part, VB), :] - resid[part] * (1.0 / G))

    def spread(a, carry):
        for part in range(2):
            scaled = resid[part] * held[pl.ds(pl.multiple_of(AT_X + VB * a, 8), VB), :]
            for b in range(UB):
                cells[part, b, pl.ds(a, 1), :] = jnp.sum(
                    scaled * held[pl.ds(AT_Y + VB * b, VB), :], axis=0, keepdims=True
                )
        return carry

    lax.fori_loop(0, UB, spread, 0)
    padded[...] = jnp.zeros(padded.shape, F32)
    nothing = jnp.zeros((PITCH, LANES), F32)
    for part in range(2):
        for b in range(UB):
            padded[b, pl.ds(24, 16), :] = cells[part, b]
        for b in range(UB):
            wide[b] = choose(lambda off: padded[b, pl.ds(24 - off, PITCH), :], 0)
        for k1 in range(33):
            at = lambda off: wide[k1 - off] if 0 <= k1 - off < UB else nothing
            spec[part, pl.ds(PITCH * k1, PITCH), :] = choose(at, 1)
        spec[part, pl.ds(PITCH * 33, PITCH), :] = nothing
    put_high, put_low = split(held[pl.ds(AT_PUT, 2 * LANES), :])
    for n in range(5):
        rows = pl.ds(chunk * n, chunk)
        high, low = split(jnp.concatenate([spec[0, rows, :], spec[1, rows, :]], axis=1))
        turned[rows, :] = dot(high, put_high) + dot(low, put_high) + dot(high, put_low)
    for group in range(5):
        count = min(8, ROWS - 8 * group)
        keys = []
        for k1 in range(33):
            value = turned[pl.ds(PITCH * k1 + 8 * group, count), :]
            if k1:
                value = value * cos[k1 : k1 + 1, :] - pltpu.roll(value, 64, axis=1) * sin[k1 : k1 + 1, :]
            keys.append(value)
        keys[0] = keys[0] + keys.pop()
        for g, value in enumerate(fourier_packed(keys, 1.0, sign_flip[:count])):
            out[pl.ds(BACK_ROWS * g + 8 * group, count), :] = value
    for g in range(SLABS):
        out[pl.ds(BACK_ROWS * g + ROWS, 1), :] = corner[...].astype(F32)


def run_grid(arrived, held, corner, cos, sin):
    vmem, far = pltpu.VMEM, pltpu.HBM
    return call(
        grid_kernel,
        [jax.ShapeDtypeStruct((SLABS * BACK_ROWS, LANES), F32)],
        [
            pltpu.VMEM((HELD_ROWS, LANES), F32),
            pltpu.VMEM((KEYS * PITCH, LANES), F32),
            pltpu.VMEM((2, KEYS * PITCH, LANES), F32),
            pltpu.VMEM((2, 33, UB, LANES), F32),
            pltpu.VMEM((2, UB, UB, LANES), F32),
            pltpu.VMEM((UB, 64, LANES), F32),
            pltpu.VMEM((UB, PITCH, LANES), F32),
            pltpu.VMEM((2, VB, LANES), F32),
            pltpu.SemaphoreType.DMA((2,)),
        ],
        [vmem, vmem, vmem, vmem, far],
        [vmem],
        1_000_000_000,
        5_000_000,
        50,
    )(arrived, cos, sin, corner, held)[0]


def image_kernel(
    arrived, prep, out, corners, step, image, *, groups,
):
    low_half = low_lanes()
    first_row = lax.broadcasted_iota(jnp.int32, (8, LANES), 0) == 0
    pointing = lax.axis_index("pt")
    for p in range(groups):
        corners[pl.ds(p, 1), :] = arrived[pl.ds(BACK_ROWS * lax.rem(pointing + groups - p, groups) + ROWS, 1), :]

    def extra(slab):
        return jnp.where(first_row, arrived[pl.ds(BACK_ROWS * slab + 32, 1), :], 0.0)

    for group in range(8):
        rho = pl.ds(8 * group, 8)
        values = []
        for u in range(16):
            if group < 4:
                packed = arrived[pl.ds(BACK_ROWS * u + 8 * group, 8), :]
                if group == 0 and u > 0:
                    packed = packed + extra(32 - u)
            else:
                packed = arrived[pl.ds(BACK_ROWS * (31 - u) + 8 * (group - 4), 8), :]
                if group == 4:
                    packed = packed + extra(u)
            crossed = pltpu.roll(packed, 64, axis=1)
            c, s = math.cos(2 * math.pi * u / 32), math.sin(2 * math.pi * u / 32)
            re = jnp.where(low_half, packed, crossed * c - packed * s)
            im = jnp.where(low_half, crossed, packed * c + crossed * s)
            if group == 0 and u == 0:
                packed = extra(16)
                crossed = pltpu.roll(packed, 64, axis=1)
                re = re + jnp.where(low_half, packed, -crossed)
                im = im + jnp.where(low_half, crossed, -packed)
            values.append((re, im))
        for kk, ((re, im), (c, s)) in enumerate(zip(fourier(values, 1.0), twists(prep, 8 * group))):
            step[kk, rho, :] = re * c - im * s
            step[kk, pl.ds(64 + 8 * group, 8), :] = re * s + im * c
    back = split(prep[pl.ds(PREP_BACK, 64), :])
    back = jnp.concatenate([back[0], back[0], back[1]], axis=1)
    for kk in range(0, 16, 2):
        high, low = split(jnp.concatenate([step[kk], step[kk + 1]], axis=1))
        both = dot(back, jnp.concatenate([high, low, high], axis=0))
        image[pl.ds(kk, 64, stride=16), :] = both[:, :LANES]
        image[pl.ds(kk + 1, 64, stride=16), :] = both[:, LANES:]
    share = 32 // groups
    for f in range(SLABS):
        for n in range(share):
            rows = pl.ds(32 * f + n, groups, stride=share)
            out[pl.ds(share * f + n, groups, stride=SLABS * share), :] = image[rows, :] * prep[rows, :]


def run_image(arrived, prep, groups):
    vmem = pltpu.VMEM

    def kernel(*refs):
        image_kernel(*refs, groups=groups)

    return call(
        kernel,
        [jax.ShapeDtypeStruct((1024, LANES), F32), jax.ShapeDtypeStruct((groups, LANES), F32)],
        [pltpu.VMEM((16, LANES, LANES), F32), pltpu.VMEM((1024, LANES), F32)],
        [vmem, vmem],
        [vmem, vmem],
        300_000_000,
        3_000_000,
    )(arrived, prep)


def home_kernel(corners, arrived, out, *, groups):
    share = 32 // groups
    count = groups * SLABS
    mine = lax.axis_index("fft")
    lane = lax.broadcasted_iota(jnp.int32, (SLABS, LANES), 1)
    slot = lax.broadcasted_iota(jnp.int32, (SLABS, LANES), 0)
    places = []
    for p in range(groups):
        corner = corners[pl.ds(p, 1), :].astype(jnp.int32)
        top, left = (corner >> 7) + ((corner >> 6) & 1) * 32, corner & 63
        row = top + ((mine - top) & 31)
        places.append((lane == (row >> 5) * 64 + left + slot).astype(F32))
    place = jnp.concatenate(places, axis=0).T.astype(BF16)
    for n in range(share):
        high, low = split(arrived[pl.ds(n, count, stride=share), :])
        out[:, pl.ds(LANES * n, LANES)] = dot(place, high) + dot(place, low)


def run_home(corners, arrived, groups):
    def kernel(*refs):
        home_kernel(*refs, groups=groups)

    return call(
        kernel,
        [jax.ShapeDtypeStruct((LANES, TS * TS // groups), F32)],
        [],
        [pltpu.VMEM, pltpu.VMEM],
        [pltpu.VMEM],
        60_000_000,
        1_000_000,
    )(corners, arrived)[0]


def body(sky_model, intersection, beam, vis_data, vis_weight, vis_pos, uv_block, counts):
    groups = lax.axis_size("pt")

    def to_slabs(rows):
        return lax.all_to_all(rows.reshape(SLABS, -1), "fft", split_axis=0, concat_axis=0, tiled=True)

    tiles, own = run_send(intersection, counts, uv_block, sky_model, vis_data, vis_weight, vis_pos)
    arrived = to_slabs(tiles).reshape(SLABS, 32, LANES)
    other = lax.ppermute(own, "fft", [(n, SLABS - 1 - n) for n in range(SLABS)])
    turns = [
        (p * SLABS + n, (p + n) % groups * SLABS + n) for p in range(groups) for n in range(SLABS)
    ]
    corner = lax.ppermute(jnp.broadcast_to(intersection[:, :1], (1, LANES)), ("pt", "fft"), turns)
    col_tables, col_cos, col_sin = column_tables()
    prep = prepare(intersection, beam)
    rows_out = run_rows(arrived, prep, other)
    held = run_weights(own, other, col_tables)
    rows_in = to_slabs(rows_out).reshape(SLABS * ROWS, LANES)
    grid_out = run_grid(rows_in, held, corner, col_cos, col_sin)
    grid_in = to_slabs(grid_out).reshape(SLABS * BACK_ROWS, LANES)
    images, corners = run_image(grid_in, prep, groups)
    home = lax.all_to_all(
        images.reshape(groups * SLABS, -1), ("pt", "fft"), split_axis=0, concat_axis=0, tiled=True
    )
    return run_home(corners, home.reshape(images.shape), groups)


def solution(mesh):
    in_specs = (
        P("fft", None),
        P("pt", None),
        P(None, "pt", "fft"),
        P(None, "pt", "fft", None),
        P("pt", "fft", None),
        P(None, "pt", "fft", None),
        P("pt", "fft"),
        P("pt", "fft"),
    )
    return jax.shard_map(body, mesh=mesh, in_specs=in_specs, out_specs=P("fft", "pt"), check_vma=False)
```

time: 154 us -> 137 us (0.89)
  local copies, waits for them, and re-layouts: 12.6 us -> 3.24 us
  blocking collectives: 66.6 us -> 61.4 us
  waiting for transfers between devices: 29.2 us -> 25.3 us
  starting transfers between devices: 23.7 us -> 25.8 us
    unnamed x41 -> x11, local copies, waits for them, and re-layouts: 11.2 us -> 0.36 us
    all_to_all x2, waiting for transfers between devices: 13.5 us -> 4.99 us  [to_slabs(): lax.all_to_all(rows.reshape(SLABS, -1), 'fft', split_axis=0, concat_axis=...]
    ppermute x0 -> x1, waiting for transfers between devices: none -> 6.47 us  [body(): lax.ppermute(jnp.broadcast_to(intersection[:, :1], (1, LANES)), ('pt', 'f...]
    all_to_all x1, blocking collectives: 43.8 us -> 38.2 us  [body(): lax.all_to_all(images.reshape(groups * SLABS, -1), ('pt', 'fft'), split_a...]
    ppermute x0 -> x1, starting transfers between devices: none -> 2.22 us  [body(): lax.ppermute(jnp.broadcast_to(intersection[:, :1], (1, LANES)), ('pt', 'f...]
    ppermute x1, waiting for transfers between devices: 15.7 us -> 13.9 us  [body(): other = lax.ppermute(own, 'fft', [(n, SLABS - 1 - n) for n in range(SLABS)])]
  transfers between devices with their start and end apart: 3 -> 4, of which waited for: 2 -> 3; matrix products, arithmetic and copies ran while one was open for 2% -> 2% of each run, Pallas kernels for 1% -> 2%
where the time goes in v3:
time: 137 us
  blocking collectives  61.4 us (45%)
  starting transfers between devices  25.8 us (19%)
  waiting for transfers between devices  25.3 us (18%)
  Pallas kernels  19.4 us (14%)
  local copies, waits for them, and re-layouts  3.24 us (2%)
  between operations  1.52 us (1%)
    all_to_all x1, blocking collectives, body(): lax.all_to_all(images.reshape(groups * SLABS, -1), ('pt', 'fft'), split_a...  38.2 us
    all_to_all x1, blocking collectives, to_slabs(): lax.all_to_all(rows.reshape(SLABS, -1), 'fft', split_axis=0, concat_axis=...  23.2 us
    all_to_all x2, starting transfers between devices, to_slabs(): lax.all_to_all(rows.reshape(SLABS, -1), 'fft', split_axis=0, concat_axis=...  16.4 us
    ppermute x1, waiting for transfers between devices, body(): other = lax.ppermute(own, 'fft', [(n, SLABS - 1 - n) for n in range(SLABS)])  13.9 us
    pallas_call x1, Pallas kernels, run_grid(): call(grid_kernel, [jax.ShapeDtypeStruct((SLABS * BACK_ROWS, LANES), F32)]...  8.89 us
    ppermute x1, starting transfers between devices, body(): other = lax.ppermute(own, 'fft', [(n, SLABS - 1 - n) for n in range(SLABS)])  7.24 us
    ppermute x1, waiting for transfers between devices, body(): lax.ppermute(jnp.broadcast_to(intersection[:, :1], (1, LANES)), ('pt', 'f...  6.47 us
    all_to_all x2, waiting for transfers between devices, to_slabs(): lax.all_to_all(rows.reshape(SLABS, -1), 'fft', split_axis=0, concat_axis=...  4.99 us
  transfers between devices with their start and end apart: 4, of which 3 were waited for; matrix products, arithmetic and copies ran while one was open for 2% of the time, Pallas kernels for 2%

profile of v3, /device:TPU:1, one launch (start us, length us, event | category | flops | bytes accessed | tf_op | source)
XLA Modules:
  0.0 136.8 jit_solution(14751327151091106000)
XLA Ops:
  0.0 0.0 copy-start.3
  0.7 2.9 %shard_map.136 = (f32[1024,128]{1,0:T(8,128)}, f32[328,128]{1,0:T(8,128)}) custom-call(s32[1,1024]{1,0:T(1,128)} %intersection_far.1, s32[1,1]{1,0:T(1,128)S(6)} %copy.21.counts_far, s32[1,64]{1,0:T(1,128)} %names_far.1, f32[128,4096]{1,0:T(8,128)} %sky.1, f32[2,1,64,128]{3,2,1,0:T(8,128)} %vis_data.1, f32[1,64,128]{2,1,0:T(8,128)} %vis_weight.1, ...), custom_call_target="tpu_custom_call" | custom-call | flops 1000000 | bytes 2000000 | tf_op jit(solution)/shard_map/pallas_call | solution.py:224
  3.6 11.2 %all-to-all-start = ((f32[32,1,4096]{2,1,0:T(1,128)}), f32[32,1,4096]{2,1,0:T(1,128)S(1)}, u32[]{:S(2)}, u32[]{:S(2)}) async-start(f32[32,1,4096]{2,1,0:T(1,128)} %bitcast.21), calls=%async_computation | async-start | bytes 1048576 | tf_op jit(solution)/shard_map/all_to_all | solution.py:628
  14.8 7.2 %collective-permute-start = (f32[328,128]{1,0:T(8,128)}, f32[328,128]{1,0:T(8,128)S(1)}, u32[]{:S(2)}, u32[]{:S(2)}) collective-permute-start(f32[328,128]{1,0:T(8,128)} %get-tuple-element.10.own_far), channel_id=1, source_target_pairs={{0,31},{1,30},{2,29},{3,28},{4,27},{5,26},{6,25},{7,24},{8,23},{9,... | collective-permute-start | bytes 503816 | tf_op jit(solution)/shard_map/ppermute | solution.py:632
  22.1 1.2 slice.4
  23.9 0.0 copy-done.3
  23.9 0.0 copy-start.4
  23.9 0.3 copy.17
  24.3 0.2 reshape.41
  24.5 0.9 dynamic-slice_bitcast_fusion
  25.3 0.1 fusion
  25.5 0.0 copy-done.4
  25.5 0.1 pad_maximum_fusion.prep.refs_1_
  25.5 13.9 %collective-permute-done.other.other_far = f32[328,128]{1,0:T(8,128)S(1)} collective-permute-done((f32[328,128]{1,0:T(8,128)}, f32[328,128]{1,0:T(8,128)S(1)}, u32[]{:S(2)}, u32[]{:S(2)}) %collective-permute-start) | collective-permute-done | bytes 167968 | tf_op jit(solution)/shard_map/ppermute | solution.py:632
  39.4 0.0 copy-start
  39.4 0.0 all-to-all-done
  39.4 1.9 %shard_map.137 = f32[1056,128]{1,0:T(8,128)} custom-call(f32[32,32,128]{2,1,0:T(8,128)S(1)} %bitcast.18, f32[1472,128]{1,0:T(8,128)S(1)} %pad_maximum_fusion.prep.refs_1_, f32[328,128]{1,0:T(8,128)S(1)} %collective-permute-done.other.other_far), custom_call_target="tpu_custom_call" | custom-call | flops 300000000 | bytes 3000000 | tf_op jit(solution)/shard_map/pallas_call | solution.py:295
  41.3 5.1 %all-to-all-start.1 = ((f32[32,1,4224]{2,1,0:T(1,128)}), f32[32,1,4224]{2,1,0:T(1,128)S(1)}, u32[]{:S(2)}, u32[]{:S(2)}) async-start(f32[32,1,4224]{2,1,0:T(1,128)} %bitcast.5), calls=%async_computation.1 | async-start | bytes 1081344 | tf_op jit(solution)/shard_map/all_to_all | solution.py:628
  46.4 0.6 broadcast_in_dim.2
  47.1 0.0 copy-start.1
  47.1 0.0 copy-start.2
  47.1 2.2 %collective-permute-start.1 = (s32[1,128]{1,0:T(1,128)S(1)}, s32[1,128]{1,0:T(1,128)S(1)}, u32[]{:S(2)}, u32[]{:S(2)}) collective-permute-start(s32[1,128]{1,0:T(1,128)S(1)} %broadcast_in_dim.2), channel_id=1, source_target_pairs={{0,0},{1,33},{2,66},{3,99},{4,132},{5,165},{6,198},{7,231},{8,264}... | collective-permute-start | bytes 1544 | tf_op jit(solution)/shard_map/ppermute | solution.py:636
  49.3 0.0 copy-done
  49.3 3.2 %shard_map.138.held_far = f32[32768,128]{1,0:T(8,128)} custom-call(f32[328,128]{1,0:T(8,128)} %get-tuple-element.10.own_far, f32[328,128]{1,0:T(8,128)} %copy-done, bf16[2,2,128,64]{3,2,1,0:T(8,128)(2,1)} %constant.24.clone.picks_far, bf16[2,2,64,128]{3,2,1,0:T(8,128)(2,1)} %constant.25.clone.puts_far), custom_call_target="tpu_custom_call" | custom-call | flops 20000000 | bytes 3000000 | tf_op jit(solution)/shard_map/pallas_call | solution.py:378
  52.5 6.5 %collective-permute-done.1.corner = s32[1,128]{1,0:T(1,128)S(1)} collective-permute-done((s32[1,128]{1,0:T(1,128)S(1)}, s32[1,128]{1,0:T(1,128)S(1)}, u32[]{:S(2)}, u32[]{:S(2)}) %collective-permute-start.1) | collective-permute-done | bytes 544 | tf_op jit(solution)/shard_map/ppermute | solution.py:636
  59.0 5.0 %all-to-all-done.1 = f32[32,1,4224]{2,1,0:T(1,128)S(1)} async-done(((f32[32,1,4224]{2,1,0:T(1,128)}), f32[32,1,4224]{2,1,0:T(1,128)S(1)}, u32[]{:S(2)}, u32[]{:S(2)}) %all-to-all-start.1) | async-done | bytes 540704 | tf_op jit(solution)/shard_map/all_to_all | solution.py:628
  64.0 0.0 copy-done.1
  64.0 0.0 copy-done.2
  64.0 8.9 %shard_map.139 = f32[1088,128]{1,0:T(8,128)S(1)} custom-call(f32[1056,128]{1,0:T(8,128)S(1)} %bitcast.16, f32[40,128]{1,0:T(8,128)S(1)} %copy-done.2, f32[40,128]{1,0:T(8,128)S(1)} %copy-done.1, s32[1,128]{1,0:T(1,128)S(1)} %collective-permute-done.1.corner, f32[32768,128]{1,0:T(8,128)} %shard_map.138.held_far), custom_call_target="tpu_custom_call" | custom-call | flops 1000000000 | bytes 5000000 | tf_op jit(solution)/shard_map/pallas_call | solution.py:501
  72.9 23.2 %all_to_all.36 = f32[32,1,4352]{2,1,0:T(1,128)S(1)} all-to-all(f32[32,1,4352]{2,1,0:T(1,128)S(1)} %bitcast.14), channel_id=1, replica_groups=mesh['pt'=16,'fft'=32] {'fft'}, dimensions={0} | all-to-all | bytes 1114112 | tf_op jit(solution)/shard_map/all_to_all | solution.py:628
  96.1 1.5 %shard_map.140 = (f32[1024,128]{1,0:T(8,128)S(1)}, f32[16,128]{1,0:T(8,128)S(1)}) custom-call(f32[1088,128]{1,0:T(8,128)S(1)} %bitcast.15, f32[1472,128]{1,0:T(8,128)S(1)} %pad_maximum_fusion.prep.refs_1_), custom_call_target="tpu_custom_call" | custom-call | flops 300000000 | bytes 3000000 | tf_op jit(solution)/shard_map/pallas_call | solution.py:580
  97.6 38.2 %all_to_all.37 = f32[512,1,256]{2,1,0:T(1,128)S(1)} all-to-all(f32[512,1,256]{2,1,0:T(1,128)S(1)} %bitcast.19), channel_id=1, replica_groups=mesh['pt'=16,'fft'=32] {'pt','fft'}, dimensions={0} | all-to-all | bytes 1048576 | tf_op jit(solution)/shard_map/all_to_all | solution.py:645
  135.8 1.0 shard_map.141
Async XLA Ops:
  0.0 23.9 %copy-start.3 = (f32[2048,1,64]{0,2,1:T(8,128)S(1)}, f32[2048,1,64]{0,2,1:T(8,128)}, u32[]{:S(2)}) copy-start(f32[2048,1,64]{0,2,1:T(8,128)} %param.16) | copy-start | bytes 1572868
  3.6 35.8 %all-to-all-start = ((f32[32,1,4096]{2,1,0:T(1,128)}), f32[32,1,4096]{2,1,0:T(1,128)S(1)}, u32[]{:S(2)}, u32[]{:S(2)}) async-start(f32[32,1,4096]{2,1,0:T(1,128)} %bitcast.21), calls=%async_computation | async-start | bytes 1048576 | tf_op jit(solution)/shard_map/all_to_all | solution.py:628
  14.8 24.6 %collective-permute-start = (f32[328,128]{1,0:T(8,128)}, f32[328,128]{1,0:T(8,128)S(1)}, u32[]{:S(2)}, u32[]{:S(2)}) collective-permute-start(f32[328,128]{1,0:T(8,128)} %get-tuple-element.10.own_far), channel_id=1, source_target_pairs={{0,31},{1,30},{2,29},{3,28},{4,27},{5,26},{6,25},{7,24},{8,23},{9,... | collective-permute-start | bytes 503816 | tf_op jit(solution)/shard_map/ppermute | solution.py:632
  23.9 1.5 %copy-start.4 = (f32[320,128]{1,0:T(8,128)S(1)}, f32[320,128]{1,0:T(8,128)}, u32[]{:S(2)}) copy-start(f32[320,128]{1,0:T(8,128)} %constant.23.clone) | copy-start | bytes 491524
  39.4 9.9 %copy-start = (f32[328,128]{1,0:T(8,128)}, f32[328,128]{1,0:T(8,128)S(1)}, u32[]{:S(2)}) copy-start(f32[328,128]{1,0:T(8,128)S(1)} %collective-permute-done.other.other_far) | copy-start | bytes 503812
  41.3 22.7 %all-to-all-start.1 = ((f32[32,1,4224]{2,1,0:T(1,128)}), f32[32,1,4224]{2,1,0:T(1,128)S(1)}, u32[]{:S(2)}, u32[]{:S(2)}) async-start(f32[32,1,4224]{2,1,0:T(1,128)} %bitcast.5), calls=%async_computation.1 | async-start | bytes 1081344 | tf_op jit(solution)/shard_map/all_to_all | solution.py:628
  47.1 16.9 %copy-start.1 = (f32[40,128]{1,0:T(8,128)S(1)}, f32[40,128]{1,0:T(8,128)}, u32[]{:S(2)}) copy-start(f32[40,128]{1,0:T(8,128)} %constant.27.clone.sin) | copy-start | bytes 61444
  47.1 16.9 %copy-start.2 = (f32[40,128]{1,0:T(8,128)S(1)}, f32[40,128]{1,0:T(8,128)}, u32[]{:S(2)}) copy-start(f32[40,128]{1,0:T(8,128)} %constant.26.clone.cos) | copy-start | bytes 61444
  47.1 11.9 %collective-permute-start.1 = (s32[1,128]{1,0:T(1,128)S(1)}, s32[1,128]{1,0:T(1,128)S(1)}, u32[]{:S(2)}, u32[]{:S(2)}) collective-permute-start(s32[1,128]{1,0:T(1,128)S(1)} %broadcast_in_dim.2), channel_id=1, source_target_pairs={{0,0},{1,33},{2,66},{3,99},{4,132},{5,165},{6,198},{7,231},{8,264}... | collective-permute-start | bytes 1544 | tf_op jit(solution)/shard_map/ppermute | solution.py:636

commit v4 on v3

--- a/solution.py
+++ b/solution.py
@@ -64,9 +64,8 @@
     return base.astype(np.float32), fixed.astype(np.float32)
 
 
-def prepare(intersection, beam):
+def prepare(corner, beam):
     base, fixed = row_tables()
-    corner = intersection[0, 0]
     top = (corner >> 7) & 31
     tiles = beam.reshape(SLABS, 32, LANES)
     turned = lax.dynamic_slice(jnp.concatenate([tiles, tiles]), ((SLABS - top) & 31, 0, 0), tiles.shape)
@@ -201,6 +200,7 @@
     own[pl.ds(2 * NB, NB), :] = jnp.where(used, weight[...], 0.0)
     own[pl.ds(5 * NB, 8), :] = jnp.zeros((8, VB), F32)
     own[pl.ds(5 * NB, 1), pl.ds(0, NB)] = names[...].astype(F32)
+    own[pl.ds(5 * NB, 1), pl.ds(NB, NB)] = jnp.full((1, NB), intersection[0, 0], jnp.int32).astype(F32)
     own_out = pltpu.make_async_copy(own, own_far, sems.at[2])
     own_out.start()
     shift = 16 - (start - first)
@@ -493,7 +493,7 @@
         for g, value in enumerate(fourier_packed(keys, 1.0, sign_flip[:count])):
             out[pl.ds(BACK_ROWS * g + 8 * group, count), :] = value
     for g in range(SLABS):
-        out[pl.ds(BACK_ROWS * g + ROWS, 1), :] = corner[...].astype(F32)
+        out[pl.ds(BACK_ROWS * g + ROWS, 1), :] = corner[...]
 
 
 def run_grid(arrived, held, corner, cos, sin):
@@ -633,9 +633,10 @@
     turns = [
         (p * SLABS + n, (p + n) % groups * SLABS + n) for p in range(groups) for n in range(SLABS)
     ]
-    corner = lax.ppermute(jnp.broadcast_to(intersection[:, :1], (1, LANES)), ("pt", "fft"), turns)
+    mine = other[5 * NB, NB]
+    corner = lax.ppermute(jnp.full((1, LANES), mine), ("pt", "fft"), turns)
     col_tables, col_cos, col_sin = column_tables()
-    prep = prepare(intersection, beam)
+    prep = prepare(mine.astype(jnp.int32), jnp.where(mine >= 0.0, beam, 0.0))
     rows_out = run_rows(arrived, prep, other)
     held = run_weights(own, other, col_tables)
     rows_in = to_slabs(rows_out).reshape(SLABS * ROWS, LANES)

time: 137 us -> 134 us (0.978)
  starting transfers between devices: 25.8 us -> 23.4 us
    ppermute x1, waiting for transfers between devices: 13.9 us -> 1.32 us  [body(): other = lax.ppermute(own, 'fft', [(n, SLABS - 1 - n) for n in range(SLABS)])]
    all_to_all x2, waiting for transfers between devices: 4.99 us -> 17.4 us  [to_slabs(): lax.all_to_all(rows.reshape(SLABS, -1), 'fft', split_axis=0, concat_axis=...]
    all_to_all x2, starting transfers between devices: 16.4 us -> 12.6 us  [to_slabs(): lax.all_to_all(rows.reshape(SLABS, -1), 'fft', split_axis=0, concat_axis=...]
    ppermute x1, starting transfers between devices: 7.24 us -> 8.95 us  [body(): other = lax.ppermute(own, 'fft', [(n, SLABS - 1 - n) for n in range(SLABS)])]
  transfers between devices with their start and end apart: 4 -> 4, of which waited for: 3 -> 4; matrix products, arithmetic and copies ran while one was open for 2% -> 2% of each run, Pallas kernels for 2% -> 2%
where the time goes in v4:
time: 134 us
  blocking collectives  60.9 us (45%)
  waiting for transfers between devices  25 us (19%)
  starting transfers between devices  23.4 us (17%)
  Pallas kernels  19.4 us (14%)
  local copies, waits for them, and re-layouts  2.65 us (2%)
  between operations  2.17 us (2%)
    all_to_all x1, blocking collectives, body(): lax.all_to_all(images.reshape(groups * SLABS, -1), ('pt', 'fft'), split_a...  37.7 us
    all_to_all x1, blocking collectives, to_slabs(): lax.all_to_all(rows.reshape(SLABS, -1), 'fft', split_axis=0, concat_axis=...  23.2 us
    all_to_all x2, waiting for transfers between devices, to_slabs(): lax.all_to_all(rows.reshape(SLABS, -1), 'fft', split_axis=0, concat_axis=...  17.4 us
    all_to_all x2, starting transfers between devices, to_slabs(): lax.all_to_all(rows.reshape(SLABS, -1), 'fft', split_axis=0, concat_axis=...  12.6 us
    ppermute x1, starting transfers between devices, body(): other = lax.ppermute(own, 'fft', [(n, SLABS - 1 - n) for n in range(SLABS)])  8.95 us
    pallas_call x1, Pallas kernels, run_grid(): call(grid_kernel, [jax.ShapeDtypeStruct((SLABS * BACK_ROWS, LANES), F32)]...  8.88 us
    ppermute x1, waiting for transfers between devices, body(): corner = lax.ppermute(jnp.full((1, LANES), mine), ('pt', 'fft'), turns)  6.27 us
    pallas_call x1, Pallas kernels, run_weights(): call(weights_kernel, [jax.ShapeDtypeStruct((HELD_SPACE, LANES), F32)], [p...  3.19 us
  transfers between devices with their start and end apart: 4, of which 4 were waited for; matrix products, arithmetic and copies ran while one was open for 2% of the time, Pallas kernels for 2%

profile of v4, /device:TPU:1, one launch (start us, length us, event | category | flops | bytes accessed | tf_op | source)
XLA Modules:
  0.0 133.7 jit_solution(3161201847118967721)
XLA Ops:
  0.0 0.0 copy-start.3
  0.7 2.9 %shard_map.136 = (f32[1024,128]{1,0:T(8,128)}, f32[328,128]{1,0:T(8,128)}) custom-call(s32[1,1024]{1,0:T(1,128)} %intersection_far.1, s32[1,1]{1,0:T(1,128)S(6)} %copy.21.counts_far, s32[1,64]{1,0:T(1,128)} %names_far.1, f32[128,4096]{1,0:T(8,128)} %sky.1, f32[2,1,64,128]{3,2,1,0:T(8,128)} %vis_data.1, f32[1,64,128]{2,1,0:T(8,128)} %vis_weight.1, ...), custom_call_target="tpu_custom_call" | custom-call | flops 1000000 | bytes 2000000 | tf_op jit(solution)/shard_map/pallas_call | solution.py:224
  3.6 8.9 %collective-permute-start = (f32[328,128]{1,0:T(8,128)}, f32[328,128]{1,0:T(8,128)S(1)}, u32[]{:S(2)}, u32[]{:S(2)}) collective-permute-start(f32[328,128]{1,0:T(8,128)} %get-tuple-element.10.own_far), channel_id=1, source_target_pairs={{0,31},{1,30},{2,29},{3,28},{4,27},{5,26},{6,25},{7,24},{8,23},{9,... | collective-permute-start | bytes 503816 | tf_op jit(solution)/shard_map/ppermute | solution.py:632
  12.6 6.6 %all-to-all-start = ((f32[32,1,4096]{2,1,0:T(1,128)}), f32[32,1,4096]{2,1,0:T(1,128)S(1)}, u32[]{:S(2)}, u32[]{:S(2)}) async-start(f32[32,1,4096]{2,1,0:T(1,128)} %bitcast.21), calls=%async_computation | async-start | bytes 1048576 | tf_op jit(solution)/shard_map/all_to_all | solution.py:628
  19.2 1.3 collective-permute-done.other.other_far
  20.5 0.0 copy-start
  20.5 0.6 slice.4
  22.4 0.0 copy-done.3
  22.5 0.0 copy-start.4
  22.5 0.3 copy.17
  22.8 0.2 reshape.39
  23.0 0.9 dynamic-slice_bitcast_fusion
  23.9 0.1 fusion
  24.0 0.0 copy-done.4
  24.0 0.1 pad_maximum_fusion.prep.refs_1_
  24.1 11.9 %all-to-all-done = f32[32,1,4096]{2,1,0:T(1,128)S(1)} async-done(((f32[32,1,4096]{2,1,0:T(1,128)}), f32[32,1,4096]{2,1,0:T(1,128)S(1)}, u32[]{:S(2)}, u32[]{:S(2)}) %all-to-all-start) | async-done | bytes 524320 | tf_op jit(solution)/shard_map/all_to_all | solution.py:628
  36.0 0.0 copy-done
  36.0 1.9 %shard_map.137 = f32[1056,128]{1,0:T(8,128)} custom-call(f32[32,32,128]{2,1,0:T(8,128)S(1)} %bitcast.18, f32[1472,128]{1,0:T(8,128)S(1)} %pad_maximum_fusion.prep.refs_1_, f32[328,128]{1,0:T(8,128)S(1)} %collective-permute-done.other.other_far), custom_call_target="tpu_custom_call" | custom-call | flops 300000000 | bytes 3000000 | tf_op jit(solution)/shard_map/pallas_call | solution.py:295
  37.9 5.9 %all-to-all-start.1 = ((f32[32,1,4224]{2,1,0:T(1,128)}), f32[32,1,4224]{2,1,0:T(1,128)S(1)}, u32[]{:S(2)}, u32[]{:S(2)}) async-start(f32[32,1,4224]{2,1,0:T(1,128)} %bitcast.5), calls=%async_computation.1 | async-start | bytes 1081344 | tf_op jit(solution)/shard_map/all_to_all | solution.py:628
  43.8 0.6 broadcast_in_dim.8
  44.4 0.0 copy-start.1
  44.5 0.0 copy-start.2
  44.5 1.9 %collective-permute-start.1 = (f32[1,128]{1,0:T(1,128)S(1)}, f32[1,128]{1,0:T(1,128)S(1)}, u32[]{:S(2)}, u32[]{:S(2)}) collective-permute-start(f32[1,128]{1,0:T(1,128)S(1)} %broadcast_in_dim.8), channel_id=1, source_target_pairs={{0,0},{1,33},{2,66},{3,99},{4,132},{5,165},{6,198},{7,231},{8,264}... | collective-permute-start | bytes 1544 | tf_op jit(solution)/shard_map/ppermute | solution.py:637
  46.4 3.2 %shard_map.138.held_far = f32[32768,128]{1,0:T(8,128)} custom-call(f32[328,128]{1,0:T(8,128)} %get-tuple-element.10.own_far, f32[328,128]{1,0:T(8,128)} %copy-done, bf16[2,2,128,64]{3,2,1,0:T(8,128)(2,1)} %constant.26.clone.picks_far, bf16[2,2,64,128]{3,2,1,0:T(8,128)(2,1)} %constant.27.clone.puts_far), custom_call_target="tpu_custom_call" | custom-call | flops 20000000 | bytes 3000000 | tf_op jit(solution)/shard_map/pallas_call | solution.py:378
  49.6 6.3 %collective-permute-done.1.corner = f32[1,128]{1,0:T(1,128)S(1)} collective-permute-done((f32[1,128]{1,0:T(1,128)S(1)}, f32[1,128]{1,0:T(1,128)S(1)}, u32[]{:S(2)}, u32[]{:S(2)}) %collective-permute-start.1) | collective-permute-done | bytes 544 | tf_op jit(solution)/shard_map/ppermute | solution.py:637
  55.9 5.5 %all-to-all-done.1 = f32[32,1,4224]{2,1,0:T(1,128)S(1)} async-done(((f32[32,1,4224]{2,1,0:T(1,128)}), f32[32,1,4224]{2,1,0:T(1,128)S(1)}, u32[]{:S(2)}, u32[]{:S(2)}) %all-to-all-start.1) | async-done | bytes 540704 | tf_op jit(solution)/shard_map/all_to_all | solution.py:628
  61.4 0.0 copy-done.1
  61.4 0.0 copy-done.2
  61.4 8.9 %shard_map.139 = f32[1088,128]{1,0:T(8,128)S(1)} custom-call(f32[1056,128]{1,0:T(8,128)S(1)} %bitcast.16, f32[40,128]{1,0:T(8,128)S(1)} %copy-done.2, f32[40,128]{1,0:T(8,128)S(1)} %copy-done.1, f32[1,128]{1,0:T(1,128)S(1)} %collective-permute-done.1.corner, f32[32768,128]{1,0:T(8,128)} %shard_map.138.held_far), custom_call_target="tpu_custom_call" | custom-call | flops 1000000000 | bytes 5000000 | tf_op jit(solution)/shard_map/pallas_call | solution.py:501
  70.3 23.2 %all_to_all.36 = f32[32,1,4352]{2,1,0:T(1,128)S(1)} all-to-all(f32[32,1,4352]{2,1,0:T(1,128)S(1)} %bitcast.14), channel_id=1, replica_groups=mesh['pt'=16,'fft'=32] {'fft'}, dimensions={0} | all-to-all | bytes 1114112 | tf_op jit(solution)/shard_map/all_to_all | solution.py:628
  93.4 1.5 %shard_map.140 = (f32[1024,128]{1,0:T(8,128)S(1)}, f32[16,128]{1,0:T(8,128)S(1)}) custom-call(f32[1088,128]{1,0:T(8,128)S(1)} %bitcast.15, f32[1472,128]{1,0:T(8,128)S(1)} %pad_maximum_fusion.prep.refs_1_), custom_call_target="tpu_custom_call" | custom-call | flops 300000000 | bytes 3000000 | tf_op jit(solution)/shard_map/pallas_call | solution.py:580
  95.0 37.7 %all_to_all.37 = f32[512,1,256]{2,1,0:T(1,128)S(1)} all-to-all(f32[512,1,256]{2,1,0:T(1,128)S(1)} %bitcast.19), channel_id=1, replica_groups=mesh['pt'=16,'fft'=32] {'pt','fft'}, dimensions={0} | all-to-all | bytes 1048576 | tf_op jit(solution)/shard_map/all_to_all | solution.py:646
  132.6 1.0 shard_map.141
  (1 shorter events, 0.0 us)
Async XLA Ops:
  0.0 22.4 %copy-start.3 = (f32[2048,1,64]{0,2,1:T(8,128)S(1)}, f32[2048,1,64]{0,2,1:T(8,128)}, u32[]{:S(2)}) copy-start(f32[2048,1,64]{0,2,1:T(8,128)} %param.16) | copy-start | bytes 1572868
  3.6 16.9 %collective-permute-start = (f32[328,128]{1,0:T(8,128)}, f32[328,128]{1,0:T(8,128)S(1)}, u32[]{:S(2)}, u32[]{:S(2)}) collective-permute-start(f32[328,128]{1,0:T(8,128)} %get-tuple-element.10.own_far), channel_id=1, source_target_pairs={{0,31},{1,30},{2,29},{3,28},{4,27},{5,26},{6,25},{7,24},{8,23},{9,... | collective-permute-start | bytes 503816 | tf_op jit(solution)/shard_map/ppermute | solution.py:632
  12.6 23.4 %all-to-all-start = ((f32[32,1,4096]{2,1,0:T(1,128)}), f32[32,1,4096]{2,1,0:T(1,128)S(1)}, u32[]{:S(2)}, u32[]{:S(2)}) async-start(f32[32,1,4096]{2,1,0:T(1,128)} %bitcast.21), calls=%async_computation | async-start | bytes 1048576 | tf_op jit(solution)/shard_map/all_to_all | solution.py:628
  20.5 15.5 %copy-start = (f32[328,128]{1,0:T(8,128)}, f32[328,128]{1,0:T(8,128)S(1)}, u32[]{:S(2)}) copy-start(f32[328,128]{1,0:T(8,128)S(1)} %collective-permute-done.other.other_far) | copy-start | bytes 503812
  22.5 1.5 %copy-start.4 = (f32[320,128]{1,0:T(8,128)S(1)}, f32[320,128]{1,0:T(8,128)}, u32[]{:S(2)}) copy-start(f32[320,128]{1,0:T(8,128)} %constant.25.clone) | copy-start | bytes 491524
  37.9 23.5 %all-to-all-start.1 = ((f32[32,1,4224]{2,1,0:T(1,128)}), f32[32,1,4224]{2,1,0:T(1,128)S(1)}, u32[]{:S(2)}, u32[]{:S(2)}) async-start(f32[32,1,4224]{2,1,0:T(1,128)} %bitcast.5), calls=%async_computation.1 | async-start | bytes 1081344 | tf_op jit(solution)/shard_map/all_to_all | solution.py:628
  44.4 16.9 %copy-start.1 = (f32[40,128]{1,0:T(8,128)S(1)}, f32[40,128]{1,0:T(8,128)}, u32[]{:S(2)}) copy-start(f32[40,128]{1,0:T(8,128)} %constant.29.clone.sin) | copy-start | bytes 61444
  44.5 16.9 %copy-start.2 = (f32[40,128]{1,0:T(8,128)S(1)}, f32[40,128]{1,0:T(8,128)}, u32[]{:S(2)}) copy-start(f32[40,128]{1,0:T(8,128)} %constant.28.clone.cos) | copy-start | bytes 61444
  44.5 11.4 %collective-permute-start.1 = (f32[1,128]{1,0:T(1,128)S(1)}, f32[1,128]{1,0:T(1,128)S(1)}, u32[]{:S(2)}, u32[]{:S(2)}) collective-permute-start(f32[1,128]{1,0:T(1,128)S(1)} %broadcast_in_dim.8), channel_id=1, source_target_pairs={{0,0},{1,33},{2,66},{3,99},{4,132},{5,165},{6,198},{7,231},{8,264}... | collective-permute-start | bytes 1544 | tf_op jit(solution)/shard_map/ppermute | solution.py:637

commit v5 on v4

--- a/solution.py
+++ b/solution.py
@@ -203,7 +203,7 @@
     own[pl.ds(5 * NB, 1), pl.ds(NB, NB)] = jnp.full((1, NB), intersection[0, 0], jnp.int32).astype(F32)
     own_out = pltpu.make_async_copy(own, own_far, sems.at[2])
     own_out.start()
-    shift = 16 - (start - first)
+    shift = (16 - (start - first)) & 15
     sky_in.wait()
     sent = []
     for part in range(4):
@@ -564,11 +564,7 @@
         both = dot(back, jnp.concatenate([high, low, high], axis=0))
         image[pl.ds(kk, 64, stride=16), :] = both[:, :LANES]
         image[pl.ds(kk + 1, 64, stride=16), :] = both[:, LANES:]
-    share = 32 // groups
-    for f in range(SLABS):
-        for n in range(share):
-            rows = pl.ds(32 * f + n, groups, stride=share)
-            out[pl.ds(share * f + n, groups, stride=SLABS * share), :] = image[rows, :] * prep[rows, :]
+    out[...] = image[...] * prep[pl.ds(0, 1024), :]
 
 
 def run_image(arrived, prep, groups):
@@ -590,19 +586,14 @@
 
 def home_kernel(corners, arrived, out, *, groups):
     share = 32 // groups
-    count = groups * SLABS
     mine = lax.axis_index("fft")
-    lane = lax.broadcasted_iota(jnp.int32, (SLABS, LANES), 1)
-    slot = lax.broadcasted_iota(jnp.int32, (SLABS, LANES), 0)
-    places = []
-    for p in range(groups):
-        corner = corners[pl.ds(p, 1), :].astype(jnp.int32)
-        top, left = (corner >> 7) + ((corner >> 6) & 1) * 32, corner & 63
-        row = top + ((mine - top) & 31)
-        places.append((lane == (row >> 5) * 64 + left + slot).astype(F32))
-    place = jnp.concatenate(places, axis=0).T.astype(BF16)
+    corner = corners[...].astype(jnp.int32)
+    top, left = (corner >> 7) + ((corner >> 6) & 1) * 32, corner & 63
+    start = ((top + ((mine - top) & 31)) >> 5) * 64 + left
+    ahead = lax.broadcasted_iota(jnp.int32, (groups, LANES), 1) - start
+    place = jnp.concatenate([(ahead == g).astype(F32) for g in range(SLABS)], axis=0).T.astype(BF16)
     for n in range(share):
-        high, low = split(arrived[pl.ds(n, count, stride=share), :])
+        high, low = split(arrived[pl.ds(n, groups * SLABS, stride=share), :])
         out[:, pl.ds(LANES * n, LANES)] = dot(place, high) + dot(place, low)
 
 
@@ -644,7 +635,7 @@
     grid_in = to_slabs(grid_out).reshape(SLABS * BACK_ROWS, LANES)
     images, corners = run_image(grid_in, prep, groups)
     home = lax.all_to_all(
-        images.reshape(groups * SLABS, -1), ("pt", "fft"), split_axis=0, concat_axis=0, tiled=True
+        images.reshape(groups * SLABS, 32 // groups, LANES), ("fft", "pt"), split_axis=0, concat_axis=0, tiled=True
     )
     return run_home(corners, home.reshape(images.shape), groups)
 

time: 134 us -> 134 us (level)
  no operation moved by 1% of the time
where the time goes in v5:
time: 134 us; the launch traced here: 133 us
  blocking collectives  61 us (46%)
  waiting for transfers between devices  25 us (19%)
  starting transfers between devices  23.4 us (17%)
  Pallas kernels  19 us (14%)
  local copies, waits for them, and re-layouts  2.65 us (2%)
  between operations  2.17 us (2%)
    all_to_all x1, blocking collectives, body(): lax.all_to_all(images.reshape(groups * SLABS, 32 // groups, LANES), ('fft...  37.8 us
    all_to_all x1, blocking collectives, to_slabs(): lax.all_to_all(rows.reshape(SLABS, -1), 'fft', split_axis=0, concat_axis=...  23.2 us
    all_to_all x2, waiting for transfers between devices, to_slabs(): lax.all_to_all(rows.reshape(SLABS, -1), 'fft', split_axis=0, concat_axis=...  17.4 us
    all_to_all x2, starting transfers between devices, to_slabs(): lax.all_to_all(rows.reshape(SLABS, -1), 'fft', split_axis=0, concat_axis=...  12.6 us
    ppermute x1, starting transfers between devices, body(): other = lax.ppermute(own, 'fft', [(n, SLABS - 1 - n) for n in range(SLABS)])  8.95 us
    pallas_call x1, Pallas kernels, run_grid(): call(grid_kernel, [jax.ShapeDtypeStruct((SLABS * BACK_ROWS, LANES), F32)]...  8.89 us
    ppermute x1, waiting for transfers between devices, body(): corner = lax.ppermute(jnp.full((1, LANES), mine), ('pt', 'fft'), turns)  6.28 us
    pallas_call x1, Pallas kernels, run_weights(): call(weights_kernel, [jax.ShapeDtypeStruct((HELD_SPACE, LANES), F32)], [p...  3.19 us
  transfers between devices with their start and end apart: 4, of which 4 were waited for; matrix products, arithmetic and copies ran while one was open for 2% of the time, Pallas kernels for 2%

profile of v5, /device:TPU:1, one launch (start us, length us, event | category | flops | bytes accessed | tf_op | source)
XLA Modules:
  0.0 133.4 jit_solution(6306128715507099196)
XLA Ops:
  0.0 0.0 copy-start.3
  0.7 2.9 %shard_map.136 = (f32[1024,128]{1,0:T(8,128)}, f32[328,128]{1,0:T(8,128)}) custom-call(s32[1,1024]{1,0:T(1,128)} %intersection_far.1, s32[1,1]{1,0:T(1,128)S(6)} %copy.20.counts_far, s32[1,64]{1,0:T(1,128)} %names_far.1, f32[128,4096]{1,0:T(8,128)} %sky.1, f32[2,1,64,128]{3,2,1,0:T(8,128)} %vis_data.1, f32[1,64,128]{2,1,0:T(8,128)} %vis_weight.1, ...), custom_call_target="tpu_custom_call" | custom-call | flops 1000000 | bytes 2000000 | tf_op jit(solution)/shard_map/pallas_call | solution.py:224
  3.6 8.9 %collective-permute-start = (f32[328,128]{1,0:T(8,128)}, f32[328,128]{1,0:T(8,128)S(1)}, u32[]{:S(2)}, u32[]{:S(2)}) collective-permute-start(f32[328,128]{1,0:T(8,128)} %get-tuple-element.10.own_far), channel_id=1, source_target_pairs={{0,31},{1,30},{2,29},{3,28},{4,27},{5,26},{6,25},{7,24},{8,23},{9,... | collective-permute-start | bytes 503816 | tf_op jit(solution)/shard_map/ppermute | solution.py:623
  12.5 6.6 %all-to-all-start = ((f32[32,1,4096]{2,1,0:T(1,128)}), f32[32,1,4096]{2,1,0:T(1,128)S(1)}, u32[]{:S(2)}, u32[]{:S(2)}) async-start(f32[32,1,4096]{2,1,0:T(1,128)} %bitcast.21), calls=%async_computation | async-start | bytes 1048576 | tf_op jit(solution)/shard_map/all_to_all | solution.py:619
  19.2 1.3 collective-permute-done.other.other_far
  20.5 0.0 copy-start
  20.5 0.6 slice.4
  22.4 0.0 copy-done.3
  22.5 0.0 copy-start.4
  22.5 0.3 copy.17
  22.8 0.2 reshape.37
  23.0 0.9 dynamic-slice_bitcast_fusion
  23.9 0.1 fusion
  24.0 0.0 copy-done.4
  24.0 0.1 pad_maximum_fusion.prep.refs_1_
  24.1 11.9 %all-to-all-done = f32[32,1,4096]{2,1,0:T(1,128)S(1)} async-done(((f32[32,1,4096]{2,1,0:T(1,128)}), f32[32,1,4096]{2,1,0:T(1,128)S(1)}, u32[]{:S(2)}, u32[]{:S(2)}) %all-to-all-start) | async-done | bytes 524320 | tf_op jit(solution)/shard_map/all_to_all | solution.py:619
  36.0 0.0 copy-done
  36.0 1.9 %shard_map.137 = f32[1056,128]{1,0:T(8,128)} custom-call(f32[32,32,128]{2,1,0:T(8,128)S(1)} %bitcast.18, f32[1472,128]{1,0:T(8,128)S(1)} %pad_maximum_fusion.prep.refs_1_, f32[328,128]{1,0:T(8,128)S(1)} %collective-permute-done.other.other_far), custom_call_target="tpu_custom_call" | custom-call | flops 300000000 | bytes 3000000 | tf_op jit(solution)/shard_map/pallas_call | solution.py:295
  37.8 5.9 %all-to-all-start.1 = ((f32[32,1,4224]{2,1,0:T(1,128)}), f32[32,1,4224]{2,1,0:T(1,128)S(1)}, u32[]{:S(2)}, u32[]{:S(2)}) async-start(f32[32,1,4224]{2,1,0:T(1,128)} %bitcast.5), calls=%async_computation.1 | async-start | bytes 1081344 | tf_op jit(solution)/shard_map/all_to_all | solution.py:619
  43.8 0.6 broadcast_in_dim.8
  44.4 0.0 copy-start.1
  44.4 0.0 copy-start.2
  44.5 1.9 %collective-permute-start.1 = (f32[1,128]{1,0:T(1,128)S(1)}, f32[1,128]{1,0:T(1,128)S(1)}, u32[]{:S(2)}, u32[]{:S(2)}) collective-permute-start(f32[1,128]{1,0:T(1,128)S(1)} %broadcast_in_dim.8), channel_id=1, source_target_pairs={{0,0},{1,33},{2,66},{3,99},{4,132},{5,165},{6,198},{7,231},{8,264}... | collective-permute-start | bytes 1544 | tf_op jit(solution)/shard_map/ppermute | solution.py:628
  46.4 3.2 %shard_map.138.held_far = f32[32768,128]{1,0:T(8,128)} custom-call(f32[328,128]{1,0:T(8,128)} %get-tuple-element.10.own_far, f32[328,128]{1,0:T(8,128)} %copy-done, bf16[2,2,128,64]{3,2,1,0:T(8,128)(2,1)} %constant.26.clone.picks_far, bf16[2,2,64,128]{3,2,1,0:T(8,128)(2,1)} %constant.27.clone.puts_far), custom_call_target="tpu_custom_call" | custom-call | flops 20000000 | bytes 3000000 | tf_op jit(solution)/shard_map/pallas_call | solution.py:378
  49.6 6.3 %collective-permute-done.1.corner = f32[1,128]{1,0:T(1,128)S(1)} collective-permute-done((f32[1,128]{1,0:T(1,128)S(1)}, f32[1,128]{1,0:T(1,128)S(1)}, u32[]{:S(2)}, u32[]{:S(2)}) %collective-permute-start.1) | collective-permute-done | bytes 544 | tf_op jit(solution)/shard_map/ppermute | solution.py:628
  55.9 5.5 %all-to-all-done.1 = f32[32,1,4224]{2,1,0:T(1,128)S(1)} async-done(((f32[32,1,4224]{2,1,0:T(1,128)}), f32[32,1,4224]{2,1,0:T(1,128)S(1)}, u32[]{:S(2)}, u32[]{:S(2)}) %all-to-all-start.1) | async-done | bytes 540704 | tf_op jit(solution)/shard_map/all_to_all | solution.py:619
  61.4 0.0 copy-done.1
  61.4 0.0 copy-done.2
  61.4 8.9 %shard_map.139 = f32[1088,128]{1,0:T(8,128)S(1)} custom-call(f32[1056,128]{1,0:T(8,128)S(1)} %bitcast.16, f32[40,128]{1,0:T(8,128)S(1)} %copy-done.2, f32[40,128]{1,0:T(8,128)S(1)} %copy-done.1, f32[1,128]{1,0:T(1,128)S(1)} %collective-permute-done.1.corner, f32[32768,128]{1,0:T(8,128)} %shard_map.138.held_far), custom_call_target="tpu_custom_call" | custom-call | flops 1000000000 | bytes 5000000 | tf_op jit(solution)/shard_map/pallas_call | solution.py:501
  70.3 23.2 %all_to_all.32 = f32[32,1,4352]{2,1,0:T(1,128)S(1)} all-to-all(f32[32,1,4352]{2,1,0:T(1,128)S(1)} %bitcast.14), channel_id=1, replica_groups=mesh['pt'=16,'fft'=32] {'fft'}, dimensions={0} | all-to-all | bytes 1114112 | tf_op jit(solution)/shard_map/all_to_all | solution.py:619
  93.4 1.1 shard_map.140
  94.6 37.8 %all_to_all.33 = f32[512,2,128]{2,1,0:T(2,128)S(1)} all-to-all(f32[512,2,128]{2,1,0:T(2,128)S(1)} %bitcast.19), channel_id=1, replica_groups=mesh['pt'=16,'fft'=32] {'fft','pt'}, dimensions={0} | all-to-all | bytes 1048576 | tf_op jit(solution)/shard_map/all_to_all | solution.py:637
  132.3 1.0 shard_map.141
  (1 shorter events, 0.0 us)
Async XLA Ops:
  0.0 22.4 %copy-start.3 = (f32[2048,1,64]{0,2,1:T(8,128)S(1)}, f32[2048,1,64]{0,2,1:T(8,128)}, u32[]{:S(2)}) copy-start(f32[2048,1,64]{0,2,1:T(8,128)} %param.16) | copy-start | bytes 1572868
  3.6 16.9 %collective-permute-start = (f32[328,128]{1,0:T(8,128)}, f32[328,128]{1,0:T(8,128)S(1)}, u32[]{:S(2)}, u32[]{:S(2)}) collective-permute-start(f32[328,128]{1,0:T(8,128)} %get-tuple-element.10.own_far), channel_id=1, source_target_pairs={{0,31},{1,30},{2,29},{3,28},{4,27},{5,26},{6,25},{7,24},{8,23},{9,... | collective-permute-start | bytes 503816 | tf_op jit(solution)/shard_map/ppermute | solution.py:623
  12.5 23.4 %all-to-all-start = ((f32[32,1,4096]{2,1,0:T(1,128)}), f32[32,1,4096]{2,1,0:T(1,128)S(1)}, u32[]{:S(2)}, u32[]{:S(2)}) async-start(f32[32,1,4096]{2,1,0:T(1,128)} %bitcast.21), calls=%async_computation | async-start | bytes 1048576 | tf_op jit(solution)/shard_map/all_to_all | solution.py:619
  20.5 15.5 %copy-start = (f32[328,128]{1,0:T(8,128)}, f32[328,128]{1,0:T(8,128)S(1)}, u32[]{:S(2)}) copy-start(f32[328,128]{1,0:T(8,128)S(1)} %collective-permute-done.other.other_far) | copy-start | bytes 503812
  22.5 1.5 %copy-start.4 = (f32[320,128]{1,0:T(8,128)S(1)}, f32[320,128]{1,0:T(8,128)}, u32[]{:S(2)}) copy-start(f32[320,128]{1,0:T(8,128)} %constant.25.clone) | copy-start | bytes 491524
  37.8 23.5 %all-to-all-start.1 = ((f32[32,1,4224]{2,1,0:T(1,128)}), f32[32,1,4224]{2,1,0:T(1,128)S(1)}, u32[]{:S(2)}, u32[]{:S(2)}) async-start(f32[32,1,4224]{2,1,0:T(1,128)} %bitcast.5), calls=%async_computation.1 | async-start | bytes 1081344 | tf_op jit(solution)/shard_map/all_to_all | solution.py:619
  44.4 16.9 %copy-start.1 = (f32[40,128]{1,0:T(8,128)S(1)}, f32[40,128]{1,0:T(8,128)}, u32[]{:S(2)}) copy-start(f32[40,128]{1,0:T(8,128)} %constant.29.clone.sin) | copy-start | bytes 61444
  44.4 16.9 %copy-start.2 = (f32[40,128]{1,0:T(8,128)S(1)}, f32[40,128]{1,0:T(8,128)}, u32[]{:S(2)}) copy-start(f32[40,128]{1,0:T(8,128)} %constant.28.clone.cos) | copy-start | bytes 61444
  44.5 11.4 %collective-permute-start.1 = (f32[1,128]{1,0:T(1,128)S(1)}, f32[1,128]{1,0:T(1,128)S(1)}, u32[]{:S(2)}, u32[]{:S(2)}) collective-permute-start(f32[1,128]{1,0:T(1,128)S(1)} %broadcast_in_dim.8), channel_id=1, source_target_pairs={{0,0},{1,33},{2,66},{3,99},{4,132},{5,165},{6,198},{7,231},{8,264}... | collective-permute-start | bytes 1544 | tf_op jit(solution)/shard_map/ppermute | solution.py:628

commit v6 on v5

--- a/solution.py
+++ b/solution.py
@@ -21,6 +21,8 @@
 KEYS = 34
 LANES = 128
 INTERPRET = False
+PT = ("z", "x_lo")
+FFT = ("y", "x_hi", "core")
 
 F32 = jnp.float32
 BF16 = jnp.bfloat16
@@ -188,7 +190,7 @@
     )
     corner_in.wait()
     top, left = window_corner(intersection)
-    mine = lax.axis_index("fft")
+    mine = lax.axis_index(FFT)
     row = top + ((mine - top) & 31)
     start = (row >> 5) * 64 + left
     first = jnp.minimum(start >> 3, 11) * 8
@@ -319,7 +321,7 @@
 
 def weights_kernel(own_far, other_far, picks_far, puts_far, held_far, own, other, picks, puts, out, sems):
     copies = start_copies([(own_far, own), (other_far, other), (picks_far, picks), (puts_far, puts)], sems)
-    mine = lax.axis_index("fft")
+    mine = lax.axis_index(FFT)
     half = mine >> 4
     u = jnp.where(half == 0, mine, SLABS - 1 - mine)
     for copy in copies:
@@ -525,9 +527,10 @@
 ):
     low_half = low_lanes()
     first_row = lax.broadcasted_iota(jnp.int32, (8, LANES), 0) == 0
-    pointing = lax.axis_index("pt")
-    for p in range(groups):
-        corners[pl.ds(p, 1), :] = arrived[pl.ds(BACK_ROWS * lax.rem(pointing + groups - p, groups) + ROWS, 1), :]
+    pointing = lax.axis_index(PT)
+    for n in range(2 * groups):
+        p = 2 * (n >> 2) + (n & 1)
+        corners[pl.ds(n, 1), :] = arrived[pl.ds(BACK_ROWS * lax.rem(pointing + groups - p, groups) + ROWS, 1), :]
 
     def extra(slab):
         return jnp.where(first_row, arrived[pl.ds(BACK_ROWS * slab + 32, 1), :], 0.0)
@@ -564,7 +567,11 @@
         both = dot(back, jnp.concatenate([high, low, high], axis=0))
         image[pl.ds(kk, 64, stride=16), :] = both[:, :LANES]
         image[pl.ds(kk + 1, 64, stride=16), :] = both[:, LANES:]
-    out[...] = image[...] * prep[pl.ds(0, 1024), :]
+    for f in range(SLABS):
+        y, side, core = f >> 2, f >> 1 & 1, f & 1
+        for n in range(4):
+            rows = pl.ds(32 * f + n, 8, stride=4)
+            out[pl.ds(512 * core + 64 * y + 4 * side + n, 8, stride=8), :] = image[rows, :] * prep[rows, :]
 
 
 def run_image(arrived, prep, groups):
@@ -575,7 +582,7 @@
 
     return call(
         kernel,
-        [jax.ShapeDtypeStruct((1024, LANES), F32), jax.ShapeDtypeStruct((groups, LANES), F32)],
+        [jax.ShapeDtypeStruct((1024, LANES), F32), jax.ShapeDtypeStruct((2 * groups, LANES), F32)],
         [pltpu.VMEM((16, LANES, LANES), F32), pltpu.VMEM((1024, LANES), F32)],
         [vmem, vmem],
         [vmem, vmem],
@@ -586,12 +593,14 @@
 
 def home_kernel(corners, arrived, out, *, groups):
     share = 32 // groups
-    mine = lax.axis_index("fft")
+    mine = lax.axis_index(FFT)
     corner = corners[...].astype(jnp.int32)
     top, left = (corner >> 7) + ((corner >> 6) & 1) * 32, corner & 63
     start = ((top + ((mine - top) & 31)) >> 5) * 64 + left
-    ahead = lax.broadcasted_iota(jnp.int32, (groups, LANES), 1) - start
-    place = jnp.concatenate([(ahead == g).astype(F32) for g in range(SLABS)], axis=0).T.astype(BF16)
+    down = lax.broadcasted_iota(jnp.int32, (2 * groups, LANES), 0)
+    ahead = lax.broadcasted_iota(jnp.int32, (2 * groups, LANES), 1) - start - (down >> 1 & 1) * 2
+    slots = [4 * y + core for core in range(2) for y in range(8)]
+    place = jnp.concatenate([(ahead == slot).astype(F32) for slot in slots], axis=0).T.astype(BF16)
     for n in range(share):
         high, low = split(arrived[pl.ds(n, groups * SLABS, stride=share), :])
         out[:, pl.ds(LANES * n, LANES)] = dot(place, high) + dot(place, low)
@@ -613,19 +622,19 @@
 
 
 def body(sky_model, intersection, beam, vis_data, vis_weight, vis_pos, uv_block, counts):
-    groups = lax.axis_size("pt")
+    groups = lax.axis_size(PT)
 
     def to_slabs(rows):
-        return lax.all_to_all(rows.reshape(SLABS, -1), "fft", split_axis=0, concat_axis=0, tiled=True)
+        return lax.all_to_all(rows.reshape(SLABS, -1), FFT, split_axis=0, concat_axis=0, tiled=True)
 
     tiles, own = run_send(intersection, counts, uv_block, sky_model, vis_data, vis_weight, vis_pos)
     arrived = to_slabs(tiles).reshape(SLABS, 32, LANES)
-    other = lax.ppermute(own, "fft", [(n, SLABS - 1 - n) for n in range(SLABS)])
+    other = lax.ppermute(own, FFT, [(n, SLABS - 1 - n) for n in range(SLABS)])
     turns = [
         (p * SLABS + n, (p + n) % groups * SLABS + n) for p in range(groups) for n in range(SLABS)
     ]
     mine = other[5 * NB, NB]
-    corner = lax.ppermute(jnp.full((1, LANES), mine), ("pt", "fft"), turns)
+    corner = lax.ppermute(jnp.full((1, LANES), mine), PT + FFT, turns)
     col_tables, col_cos, col_sin = column_tables()
     prep = prepare(mine.astype(jnp.int32), jnp.where(mine >= 0.0, beam, 0.0))
     rows_out = run_rows(arrived, prep, other)
@@ -635,20 +644,25 @@
     grid_in = to_slabs(grid_out).reshape(SLABS * BACK_ROWS, LANES)
     images, corners = run_image(grid_in, prep, groups)
     home = lax.all_to_all(
-        images.reshape(groups * SLABS, 32 // groups, LANES), ("fft", "pt"), split_axis=0, concat_axis=0, tiled=True
+        images.reshape(groups * SLABS, 32 // groups, LANES),
+        ("core", "y", "z", "x_hi", "x_lo"),
+        split_axis=0,
+        concat_axis=0,
+        tiled=True,
     )
     return run_home(corners, home.reshape(images.shape), groups)
 
 
 def solution(mesh):
+    parts = jax.sharding.Mesh(mesh.devices.reshape(8, 2, 8, 2, 2), PT + FFT)
     in_specs = (
-        P("fft", None),
-        P("pt", None),
-        P(None, "pt", "fft"),
-        P(None, "pt", "fft", None),
-        P("pt", "fft", None),
-        P(None, "pt", "fft", None),
-        P("pt", "fft"),
-        P("pt", "fft"),
+        P(FFT, None),
+        P(PT, None),
+        P(None, PT, FFT),
+        P(None, PT, FFT, None),
+        P(PT, FFT, None),
+        P(None, PT, FFT, None),
+        P(PT, FFT),
+        P(PT, FFT),
     )
-    return jax.shard_map(body, mesh=mesh, in_specs=in_specs, out_specs=P("fft", "pt"), check_vma=False)
+    return jax.shard_map(body, mesh=parts, in_specs=in_specs, out_specs=P(FFT, PT), check_vma=False)

time: 134 us -> 134 us (level)
  no operation moved by 1% of the time
where the time goes in v6:
time: 134 us; the launch traced here: 133 us
  blocking collectives  60.6 us (45%)
  waiting for transfers between devices  25 us (19%)
  starting transfers between devices  23.4 us (17%)
  Pallas kernels  19 us (14%)
  local copies, waits for them, and re-layouts  2.65 us (2%)
  between operations  2.17 us (2%)
    all_to_all x1, blocking collectives, body(): lax.all_to_all(images.reshape(groups * SLABS, 32 // groups, LANES), ('cor...  37.4 us
    all_to_all x1, blocking collectives, to_slabs(): lax.all_to_all(rows.reshape(SLABS, -1), FFT, split_axis=0, concat_axis=0,...  23.2 us
    all_to_all x2, waiting for transfers between devices, to_slabs(): lax.all_to_all(rows.reshape(SLABS, -1), FFT, split_axis=0, concat_axis=0,...  17.4 us
    all_to_all x2, starting transfers between devices, to_slabs(): lax.all_to_all(rows.reshape(SLABS, -1), FFT, split_axis=0, concat_axis=0,...  12.6 us
    ppermute x1, starting transfers between devices, body(): other = lax.ppermute(own, FFT, [(n, SLABS - 1 - n) for n in range(SLABS)])  8.95 us
    pallas_call x1, Pallas kernels, run_grid(): call(grid_kernel, [jax.ShapeDtypeStruct((SLABS * BACK_ROWS, LANES), F32)]...  8.89 us
    ppermute x1, waiting for transfers between devices, body(): corner = lax.ppermute(jnp.full((1, LANES), mine), PT + FFT, turns)  6.27 us
    pallas_call x1, Pallas kernels, run_weights(): call(weights_kernel, [jax.ShapeDtypeStruct((HELD_SPACE, LANES), F32)], [p...  3.19 us
  transfers between devices with their start and end apart: 4, of which 4 were waited for; matrix products, arithmetic and copies ran while one was open for 2% of the time, Pallas kernels for 2%

profile of v6, /device:TPU:1, one launch (start us, length us, event | category | flops | bytes accessed | tf_op | source)
XLA Modules:
  0.0 133.0 jit_solution(13352137154740375836)
XLA Ops:
  0.0 0.0 copy-start.3
  0.7 2.9 %shard_map.136 = (f32[1024,128]{1,0:T(8,128)}, f32[328,128]{1,0:T(8,128)}) custom-call(s32[1,1024]{1,0:T(1,128)} %intersection_far.1, s32[1,1]{1,0:T(1,128)S(6)} %copy.20.counts_far, s32[1,64]{1,0:T(1,128)} %names_far.1, f32[128,4096]{1,0:T(8,128)} %sky.1, f32[2,1,64,128]{3,2,1,0:T(8,128)} %vis_data.1, f32[1,64,128]{2,1,0:T(8,128)} %vis_weight.1, ...), custom_call_target="tpu_custom_call" | custom-call | flops 1000000 | bytes 2000000 | tf_op jit(solution)/shard_map/pallas_call | solution.py:226
  3.6 8.9 %collective-permute-start = (f32[328,128]{1,0:T(8,128)}, f32[328,128]{1,0:T(8,128)S(1)}, u32[]{:S(2)}, u32[]{:S(2)}) collective-permute-start(f32[328,128]{1,0:T(8,128)} %get-tuple-element.10.own_far), channel_id=1, source_target_pairs={{0,31},{1,30},{2,29},{3,28},{4,27},{5,26},{6,25},{7,24},{8,23},{9,... | collective-permute-start | bytes 503816 | tf_op jit(solution)/shard_map/ppermute | solution.py:632
  12.6 6.6 %all-to-all-start = ((f32[32,1,4096]{2,1,0:T(1,128)}), f32[32,1,4096]{2,1,0:T(1,128)S(1)}, u32[]{:S(2)}, u32[]{:S(2)}) async-start(f32[32,1,4096]{2,1,0:T(1,128)} %bitcast.21), calls=%async_computation | async-start | bytes 1048576 | tf_op jit(solution)/shard_map/all_to_all | solution.py:628
  19.2 1.3 collective-permute-done.other.other_far
  20.5 0.0 copy-start
  20.5 0.6 slice.4
  22.4 0.0 copy-done.3
  22.5 0.0 copy-start.4
  22.5 0.3 copy.17
  22.8 0.2 reshape.37
  23.0 0.9 dynamic-slice_bitcast_fusion
  23.9 0.1 fusion
  24.0 0.0 copy-done.4
  24.0 0.1 pad_maximum_fusion.prep.refs_1_
  24.1 11.9 %all-to-all-done = f32[32,1,4096]{2,1,0:T(1,128)S(1)} async-done(((f32[32,1,4096]{2,1,0:T(1,128)}), f32[32,1,4096]{2,1,0:T(1,128)S(1)}, u32[]{:S(2)}, u32[]{:S(2)}) %all-to-all-start) | async-done | bytes 524320 | tf_op jit(solution)/shard_map/all_to_all | solution.py:628
  36.0 0.0 copy-done
  36.0 1.9 %shard_map.137 = f32[1056,128]{1,0:T(8,128)} custom-call(f32[32,32,128]{2,1,0:T(8,128)S(1)} %bitcast.18, f32[1472,128]{1,0:T(8,128)S(1)} %pad_maximum_fusion.prep.refs_1_, f32[328,128]{1,0:T(8,128)S(1)} %collective-permute-done.other.other_far), custom_call_target="tpu_custom_call" | custom-call | flops 300000000 | bytes 3000000 | tf_op jit(solution)/shard_map/pallas_call | solution.py:297
  37.9 5.9 %all-to-all-start.1 = ((f32[32,1,4224]{2,1,0:T(1,128)}), f32[32,1,4224]{2,1,0:T(1,128)S(1)}, u32[]{:S(2)}, u32[]{:S(2)}) async-start(f32[32,1,4224]{2,1,0:T(1,128)} %bitcast.5), calls=%async_computation.1 | async-start | bytes 1081344 | tf_op jit(solution)/shard_map/all_to_all | solution.py:628
  43.8 0.6 broadcast_in_dim.8
  44.4 0.0 copy-start.1
  44.5 0.0 copy-start.2
  44.5 1.9 %collective-permute-start.1 = (f32[1,128]{1,0:T(1,128)S(1)}, f32[1,128]{1,0:T(1,128)S(1)}, u32[]{:S(2)}, u32[]{:S(2)}) collective-permute-start(f32[1,128]{1,0:T(1,128)S(1)} %broadcast_in_dim.8), channel_id=1, source_target_pairs={{0,0},{1,33},{2,66},{3,99},{4,132},{5,165},{6,198},{7,231},{8,264}... | collective-permute-start | bytes 1544 | tf_op jit(solution)/shard_map/ppermute | solution.py:637
  46.4 3.2 %shard_map.138.held_far = f32[32768,128]{1,0:T(8,128)} custom-call(f32[328,128]{1,0:T(8,128)} %get-tuple-element.10.own_far, f32[328,128]{1,0:T(8,128)} %copy-done, bf16[2,2,128,64]{3,2,1,0:T(8,128)(2,1)} %constant.26.clone.picks_far, bf16[2,2,64,128]{3,2,1,0:T(8,128)(2,1)} %constant.27.clone.puts_far), custom_call_target="tpu_custom_call" | custom-call | flops 20000000 | bytes 3000000 | tf_op jit(solution)/shard_map/pallas_call | solution.py:380
  49.6 6.3 %collective-permute-done.1.corner = f32[1,128]{1,0:T(1,128)S(1)} collective-permute-done((f32[1,128]{1,0:T(1,128)S(1)}, f32[1,128]{1,0:T(1,128)S(1)}, u32[]{:S(2)}, u32[]{:S(2)}) %collective-permute-start.1) | collective-permute-done | bytes 544 | tf_op jit(solution)/shard_map/ppermute | solution.py:637
  55.9 5.5 %all-to-all-done.1 = f32[32,1,4224]{2,1,0:T(1,128)S(1)} async-done(((f32[32,1,4224]{2,1,0:T(1,128)}), f32[32,1,4224]{2,1,0:T(1,128)S(1)}, u32[]{:S(2)}, u32[]{:S(2)}) %all-to-all-start.1) | async-done | bytes 540704 | tf_op jit(solution)/shard_map/all_to_all | solution.py:628
  61.4 0.0 copy-done.1
  61.4 0.0 copy-done.2
  61.4 8.9 %shard_map.139 = f32[1088,128]{1,0:T(8,128)S(1)} custom-call(f32[1056,128]{1,0:T(8,128)S(1)} %bitcast.16, f32[40,128]{1,0:T(8,128)S(1)} %copy-done.2, f32[40,128]{1,0:T(8,128)S(1)} %copy-done.1, f32[1,128]{1,0:T(1,128)S(1)} %collective-permute-done.1.corner, f32[32768,128]{1,0:T(8,128)} %shard_map.138.held_far), custom_call_target="tpu_custom_call" | custom-call | flops 1000000000 | bytes 5000000 | tf_op jit(solution)/shard_map/pallas_call | solution.py:503
  70.3 23.2 %all_to_all.32 = f32[32,1,4352]{2,1,0:T(1,128)S(1)} all-to-all(f32[32,1,4352]{2,1,0:T(1,128)S(1)} %bitcast.14), channel_id=1, replica_groups=mesh['z'=8,'x_lo'=2,'y'=8,'x_hi'=2,'core'=2] {'y','x_hi','core'}, dimensions={0} | all-to-all | bytes 1114112 | tf_op jit(solution)/shard_map/all_to_all | solution.py:628
  93.5 1.2 shard_map.140
  94.6 37.4 %all_to_all.33 = f32[512,2,128]{2,1,0:T(2,128)S(1)} all-to-all(f32[512,2,128]{2,1,0:T(2,128)S(1)} %bitcast.19), channel_id=1, replica_groups=mesh['z'=8,'x_lo'=2,'y'=8,'x_hi'=2,'core'=2] {'core','y','z','x_hi','x_lo'}, dimensions={0} | all-to-all | bytes 1048576 | tf_op jit(solution)/shard_map/all_to_all | solution.py:646
  132.0 1.0 shard_map.141
  (1 shorter events, 0.0 us)
Async XLA Ops:
  0.0 22.4 %copy-start.3 = (f32[2048,1,64]{0,2,1:T(8,128)S(1)}, f32[2048,1,64]{0,2,1:T(8,128)}, u32[]{:S(2)}) copy-start(f32[2048,1,64]{0,2,1:T(8,128)} %param.16) | copy-start | bytes 1572868
  3.6 16.9 %collective-permute-start = (f32[328,128]{1,0:T(8,128)}, f32[328,128]{1,0:T(8,128)S(1)}, u32[]{:S(2)}, u32[]{:S(2)}) collective-permute-start(f32[328,128]{1,0:T(8,128)} %get-tuple-element.10.own_far), channel_id=1, source_target_pairs={{0,31},{1,30},{2,29},{3,28},{4,27},{5,26},{6,25},{7,24},{8,23},{9,... | collective-permute-start | bytes 503816 | tf_op jit(solution)/shard_map/ppermute | solution.py:632
  12.6 23.4 %all-to-all-start = ((f32[32,1,4096]{2,1,0:T(1,128)}), f32[32,1,4096]{2,1,0:T(1,128)S(1)}, u32[]{:S(2)}, u32[]{:S(2)}) async-start(f32[32,1,4096]{2,1,0:T(1,128)} %bitcast.21), calls=%async_computation | async-start | bytes 1048576 | tf_op jit(solution)/shard_map/all_to_all | solution.py:628
  20.5 15.5 %copy-start = (f32[328,128]{1,0:T(8,128)}, f32[328,128]{1,0:T(8,128)S(1)}, u32[]{:S(2)}) copy-start(f32[328,128]{1,0:T(8,128)S(1)} %collective-permute-done.other.other_far) | copy-start | bytes 503812
  22.5 1.5 %copy-start.4 = (f32[320,128]{1,0:T(8,128)S(1)}, f32[320,128]{1,0:T(8,128)}, u32[]{:S(2)}) copy-start(f32[320,128]{1,0:T(8,128)} %constant.25.clone) | copy-start | bytes 491524
  37.9 23.5 %all-to-all-start.1 = ((f32[32,1,4224]{2,1,0:T(1,128)}), f32[32,1,4224]{2,1,0:T(1,128)S(1)}, u32[]{:S(2)}, u32[]{:S(2)}) async-start(f32[32,1,4224]{2,1,0:T(1,128)} %bitcast.5), calls=%async_computation.1 | async-start | bytes 1081344 | tf_op jit(solution)/shard_map/all_to_all | solution.py:628
  44.4 16.9 %copy-start.1 = (f32[40,128]{1,0:T(8,128)S(1)}, f32[40,128]{1,0:T(8,128)}, u32[]{:S(2)}) copy-start(f32[40,128]{1,0:T(8,128)} %constant.29.clone.sin) | copy-start | bytes 61444
  44.5 16.9 %copy-start.2 = (f32[40,128]{1,0:T(8,128)S(1)}, f32[40,128]{1,0:T(8,128)}, u32[]{:S(2)}) copy-start(f32[40,128]{1,0:T(8,128)} %constant.28.clone.cos) | copy-start | bytes 61444
  44.5 11.4 %collective-permute-start.1 = (f32[1,128]{1,0:T(1,128)S(1)}, f32[1,128]{1,0:T(1,128)S(1)}, u32[]{:S(2)}, u32[]{:S(2)}) collective-permute-start(f32[1,128]{1,0:T(1,128)S(1)} %broadcast_in_dim.8), channel_id=1, source_target_pairs={{0,0},{1,33},{2,66},{3,99},{4,132},{5,165},{6,198},{7,231},{8,264}... | collective-permute-start | bytes 1544 | tf_op jit(solution)/shard_map/ppermute | solution.py:637

commit v7 on v6

--- a/solution.py
+++ b/solution.py
@@ -453,7 +453,7 @@
                 resid[part, rows, :] += held[pl.ds(pl.multiple_of(AT_X + VB * a + top, 8), 64), :] * total[part]
         return carry
 
-    lax.fori_loop(0, UB, predict, 0)
+    lax.fori_loop(0, UB, predict, 0, unroll=2)
     for part in range(2):
         resid[part] = held[pl.ds(2 * VB, VB), :] * (held[pl.ds(VB * part, VB), :] - resid[part] * (1.0 / G))
 
@@ -466,7 +466,7 @@
                 )
         return carry
 
-    lax.fori_loop(0, UB, spread, 0)
+    lax.fori_loop(0, UB, spread, 0, unroll=2)
     padded[...] = jnp.zeros(padded.shape, F32)
     nothing = jnp.zeros((PITCH, LANES), F32)
     for part in range(2):

time: 134 us -> 133 us (level)
  no operation moved by 1% of the time
where the time goes in v7:
time: 133 us
  blocking collectives  60.6 us (46%)
  waiting for transfers between devices  25 us (19%)
  starting transfers between devices  23.4 us (18%)
  Pallas kernels  18.7 us (14%)
  local copies, waits for them, and re-layouts  2.65 us (2%)
  between operations  2.17 us (2%)
    all_to_all x1, blocking collectives, body(): lax.all_to_all(images.reshape(groups * SLABS, 32 // groups, LANES), ('cor...  37.4 us
    all_to_all x1, blocking collectives, to_slabs(): lax.all_to_all(rows.reshape(SLABS, -1), FFT, split_axis=0, concat_axis=0,...  23.2 us
    all_to_all x2, waiting for transfers between devices, to_slabs(): lax.all_to_all(rows.reshape(SLABS, -1), FFT, split_axis=0, concat_axis=0,...  17.4 us
    all_to_all x2, starting transfers between devices, to_slabs(): lax.all_to_all(rows.reshape(SLABS, -1), FFT, split_axis=0, concat_axis=0,...  12.6 us
    ppermute x1, starting transfers between devices, body(): other = lax.ppermute(own, FFT, [(n, SLABS - 1 - n) for n in range(SLABS)])  8.95 us
    pallas_call x1, Pallas kernels, run_grid(): call(grid_kernel, [jax.ShapeDtypeStruct((SLABS * BACK_ROWS, LANES), F32)]...  8.54 us
    ppermute x1, waiting for transfers between devices, body(): corner = lax.ppermute(jnp.full((1, LANES), mine), PT + FFT, turns)  6.27 us
    pallas_call x1, Pallas kernels, run_weights(): call(weights_kernel, [jax.ShapeDtypeStruct((HELD_SPACE, LANES), F32)], [p...  3.19 us
  transfers between devices with their start and end apart: 4, of which 4 were waited for; matrix products, arithmetic and copies ran while one was open for 2% of the time, Pallas kernels for 2%

profile of v7, /device:TPU:1, one launch (start us, length us, event | category | flops | bytes accessed | tf_op | source)
XLA Modules:
  0.0 132.7 jit_solution(2694744573793641838)
XLA Ops:
  0.0 0.0 copy-start.3
  0.7 2.9 %shard_map.136 = (f32[1024,128]{1,0:T(8,128)}, f32[328,128]{1,0:T(8,128)}) custom-call(s32[1,1024]{1,0:T(1,128)} %intersection_far.1, s32[1,1]{1,0:T(1,128)S(6)} %copy.20.counts_far, s32[1,64]{1,0:T(1,128)} %names_far.1, f32[128,4096]{1,0:T(8,128)} %sky.1, f32[2,1,64,128]{3,2,1,0:T(8,128)} %vis_data.1, f32[1,64,128]{2,1,0:T(8,128)} %vis_weight.1, ...), custom_call_target="tpu_custom_call" | custom-call | flops 1000000 | bytes 2000000 | tf_op jit(solution)/shard_map/pallas_call | solution.py:226
  3.6 8.9 %collective-permute-start = (f32[328,128]{1,0:T(8,128)}, f32[328,128]{1,0:T(8,128)S(1)}, u32[]{:S(2)}, u32[]{:S(2)}) collective-permute-start(f32[328,128]{1,0:T(8,128)} %get-tuple-element.10.own_far), channel_id=1, source_target_pairs={{0,31},{1,30},{2,29},{3,28},{4,27},{5,26},{6,25},{7,24},{8,23},{9,... | collective-permute-start | bytes 503816 | tf_op jit(solution)/shard_map/ppermute | solution.py:632
  12.6 6.6 %all-to-all-start = ((f32[32,1,4096]{2,1,0:T(1,128)}), f32[32,1,4096]{2,1,0:T(1,128)S(1)}, u32[]{:S(2)}, u32[]{:S(2)}) async-start(f32[32,1,4096]{2,1,0:T(1,128)} %bitcast.21), calls=%async_computation | async-start | bytes 1048576 | tf_op jit(solution)/shard_map/all_to_all | solution.py:628
  19.2 1.3 collective-permute-done.other.other_far
  20.5 0.0 copy-start
  20.5 0.6 slice.4
  22.4 0.0 copy-done.3
  22.5 0.0 copy-start.4
  22.5 0.3 copy.17
  22.8 0.2 reshape.37
  23.0 0.9 dynamic-slice_bitcast_fusion
  23.9 0.1 fusion
  24.0 0.0 copy-done.4
  24.0 0.1 pad_maximum_fusion.prep.refs_1_
  24.1 11.9 %all-to-all-done = f32[32,1,4096]{2,1,0:T(1,128)S(1)} async-done(((f32[32,1,4096]{2,1,0:T(1,128)}), f32[32,1,4096]{2,1,0:T(1,128)S(1)}, u32[]{:S(2)}, u32[]{:S(2)}) %all-to-all-start) | async-done | bytes 524320 | tf_op jit(solution)/shard_map/all_to_all | solution.py:628
  36.0 0.0 copy-done
  36.0 1.9 %shard_map.137 = f32[1056,128]{1,0:T(8,128)} custom-call(f32[32,32,128]{2,1,0:T(8,128)S(1)} %bitcast.18, f32[1472,128]{1,0:T(8,128)S(1)} %pad_maximum_fusion.prep.refs_1_, f32[328,128]{1,0:T(8,128)S(1)} %collective-permute-done.other.other_far), custom_call_target="tpu_custom_call" | custom-call | flops 300000000 | bytes 3000000 | tf_op jit(solution)/shard_map/pallas_call | solution.py:297
  37.9 5.9 %all-to-all-start.1 = ((f32[32,1,4224]{2,1,0:T(1,128)}), f32[32,1,4224]{2,1,0:T(1,128)S(1)}, u32[]{:S(2)}, u32[]{:S(2)}) async-start(f32[32,1,4224]{2,1,0:T(1,128)} %bitcast.5), calls=%async_computation.1 | async-start | bytes 1081344 | tf_op jit(solution)/shard_map/all_to_all | solution.py:628
  43.8 0.6 broadcast_in_dim.8
  44.4 0.0 copy-start.1
  44.5 0.0 copy-start.2
  44.5 1.9 %collective-permute-start.1 = (f32[1,128]{1,0:T(1,128)S(1)}, f32[1,128]{1,0:T(1,128)S(1)}, u32[]{:S(2)}, u32[]{:S(2)}) collective-permute-start(f32[1,128]{1,0:T(1,128)S(1)} %broadcast_in_dim.8), channel_id=1, source_target_pairs={{0,0},{1,33},{2,66},{3,99},{4,132},{5,165},{6,198},{7,231},{8,264}... | collective-permute-start | bytes 1544 | tf_op jit(solution)/shard_map/ppermute | solution.py:637
  46.4 3.2 %shard_map.138.held_far = f32[32768,128]{1,0:T(8,128)} custom-call(f32[328,128]{1,0:T(8,128)} %get-tuple-element.10.own_far, f32[328,128]{1,0:T(8,128)} %copy-done, bf16[2,2,128,64]{3,2,1,0:T(8,128)(2,1)} %constant.26.clone.picks_far, bf16[2,2,64,128]{3,2,1,0:T(8,128)(2,1)} %constant.27.clone.puts_far), custom_call_target="tpu_custom_call" | custom-call | flops 20000000 | bytes 3000000 | tf_op jit(solution)/shard_map/pallas_call | solution.py:380
  49.6 6.3 %collective-permute-done.1.corner = f32[1,128]{1,0:T(1,128)S(1)} collective-permute-done((f32[1,128]{1,0:T(1,128)S(1)}, f32[1,128]{1,0:T(1,128)S(1)}, u32[]{:S(2)}, u32[]{:S(2)}) %collective-permute-start.1) | collective-permute-done | bytes 544 | tf_op jit(solution)/shard_map/ppermute | solution.py:637
  55.9 5.5 %all-to-all-done.1 = f32[32,1,4224]{2,1,0:T(1,128)S(1)} async-done(((f32[32,1,4224]{2,1,0:T(1,128)}), f32[32,1,4224]{2,1,0:T(1,128)S(1)}, u32[]{:S(2)}, u32[]{:S(2)}) %all-to-all-start.1) | async-done | bytes 540704 | tf_op jit(solution)/shard_map/all_to_all | solution.py:628
  61.4 0.0 copy-done.1
  61.4 0.0 copy-done.2
  61.4 8.5 %shard_map.139 = f32[1088,128]{1,0:T(8,128)S(1)} custom-call(f32[1056,128]{1,0:T(8,128)S(1)} %bitcast.16, f32[40,128]{1,0:T(8,128)S(1)} %copy-done.2, f32[40,128]{1,0:T(8,128)S(1)} %copy-done.1, f32[1,128]{1,0:T(1,128)S(1)} %collective-permute-done.1.corner, f32[32768,128]{1,0:T(8,128)} %shard_map.138.held_far), custom_call_target="tpu_custom_call" | custom-call | flops 1000000000 | bytes 5000000 | tf_op jit(solution)/shard_map/pallas_call | solution.py:503
  69.9 23.2 %all_to_all.32 = f32[32,1,4352]{2,1,0:T(1,128)S(1)} all-to-all(f32[32,1,4352]{2,1,0:T(1,128)S(1)} %bitcast.14), channel_id=1, replica_groups=mesh['z'=8,'x_lo'=2,'y'=8,'x_hi'=2,'core'=2] {'y','x_hi','core'}, dimensions={0} | all-to-all | bytes 1114112 | tf_op jit(solution)/shard_map/all_to_all | solution.py:628
  93.1 1.2 shard_map.140
  94.3 37.4 %all_to_all.33 = f32[512,2,128]{2,1,0:T(2,128)S(1)} all-to-all(f32[512,2,128]{2,1,0:T(2,128)S(1)} %bitcast.19), channel_id=1, replica_groups=mesh['z'=8,'x_lo'=2,'y'=8,'x_hi'=2,'core'=2] {'core','y','z','x_hi','x_lo'}, dimensions={0} | all-to-all | bytes 1048576 | tf_op jit(solution)/shard_map/all_to_all | solution.py:646
  131.7 1.0 shard_map.141
  (1 shorter events, 0.0 us)
Async XLA Ops:
  0.0 22.4 %copy-start.3 = (f32[2048,1,64]{0,2,1:T(8,128)S(1)}, f32[2048,1,64]{0,2,1:T(8,128)}, u32[]{:S(2)}) copy-start(f32[2048,1,64]{0,2,1:T(8,128)} %param.16) | copy-start | bytes 1572868
  3.6 16.9 %collective-permute-start = (f32[328,128]{1,0:T(8,128)}, f32[328,128]{1,0:T(8,128)S(1)}, u32[]{:S(2)}, u32[]{:S(2)}) collective-permute-start(f32[328,128]{1,0:T(8,128)} %get-tuple-element.10.own_far), channel_id=1, source_target_pairs={{0,31},{1,30},{2,29},{3,28},{4,27},{5,26},{6,25},{7,24},{8,23},{9,... | collective-permute-start | bytes 503816 | tf_op jit(solution)/shard_map/ppermute | solution.py:632
  12.6 23.4 %all-to-all-start = ((f32[32,1,4096]{2,1,0:T(1,128)}), f32[32,1,4096]{2,1,0:T(1,128)S(1)}, u32[]{:S(2)}, u32[]{:S(2)}) async-start(f32[32,1,4096]{2,1,0:T(1,128)} %bitcast.21), calls=%async_computation | async-start | bytes 1048576 | tf_op jit(solution)/shard_map/all_to_all | solution.py:628
  20.5 15.5 %copy-start = (f32[328,128]{1,0:T(8,128)}, f32[328,128]{1,0:T(8,128)S(1)}, u32[]{:S(2)}) copy-start(f32[328,128]{1,0:T(8,128)S(1)} %collective-permute-done.other.other_far) | copy-start | bytes 503812
  22.5 1.5 %copy-start.4 = (f32[320,128]{1,0:T(8,128)S(1)}, f32[320,128]{1,0:T(8,128)}, u32[]{:S(2)}) copy-start(f32[320,128]{1,0:T(8,128)} %constant.25.clone) | copy-start | bytes 491524
  37.9 23.5 %all-to-all-start.1 = ((f32[32,1,4224]{2,1,0:T(1,128)}), f32[32,1,4224]{2,1,0:T(1,128)S(1)}, u32[]{:S(2)}, u32[]{:S(2)}) async-start(f32[32,1,4224]{2,1,0:T(1,128)} %bitcast.5), calls=%async_computation.1 | async-start | bytes 1081344 | tf_op jit(solution)/shard_map/all_to_all | solution.py:628
  44.4 16.9 %copy-start.1 = (f32[40,128]{1,0:T(8,128)S(1)}, f32[40,128]{1,0:T(8,128)}, u32[]{:S(2)}) copy-start(f32[40,128]{1,0:T(8,128)} %constant.29.clone.sin) | copy-start | bytes 61444
  44.5 16.9 %copy-start.2 = (f32[40,128]{1,0:T(8,128)S(1)}, f32[40,128]{1,0:T(8,128)}, u32[]{:S(2)}) copy-start(f32[40,128]{1,0:T(8,128)} %constant.28.clone.cos) | copy-start | bytes 61444
  44.5 11.4 %collective-permute-start.1 = (f32[1,128]{1,0:T(1,128)S(1)}, f32[1,128]{1,0:T(1,128)S(1)}, u32[]{:S(2)}, u32[]{:S(2)}) collective-permute-start(f32[1,128]{1,0:T(1,128)S(1)} %broadcast_in_dim.8), channel_id=1, source_target_pairs={{0,0},{1,33},{2,66},{3,99},{4,132},{5,165},{6,198},{7,231},{8,264}... | collective-permute-start | bytes 1544 | tf_op jit(solution)/shard_map/ppermute | solution.py:637
